TPU v7x, 32 devices: a whole 2x2x4 slice. The times are simulated.
32 devices in a mesh: rows: 8 (over y, x, core), blk: 4 (over z).
Axes of the slice: x: 2, y: 2, z: 4, core: 2. Of those that a mesh axis runs over, the one named last changes fastest.
Arguments:
- hidden_in: bfloat16 [40, 800, 768], P('rows', 'blk'), may hold values from -6 to 6
- segment_ids: int32 [40, 800], P('rows', 'blk'), may hold values from 0 to 3, as said below
- bucket_map: int32 [1599], replicated, may hold values from 0 to 319, as said below
- qkv_weight: bfloat16 [768, 2304], P(('rows', 'blk')), may hold values from -0.21875 to 0.21875
- out_weight: bfloat16 [768, 768], P(('rows', 'blk')), may hold values from -0.875 to 0.875
- up_weight: bfloat16 [768, 3072], P(('rows', 'blk')), may hold values from -0.21875 to 0.21875
- down_weight: bfloat16 [3072, 768], P(('rows', 'blk')), may hold values from -0.109375 to 0.109375
- bias_cols: bfloat16 [768, 6], P(('rows', 'blk')), may hold values from -4 to 4
- norm_gains: bfloat16 [768, 2], P(('rows', 'blk')), may hold values from 0.25 to 1.75
- up_bias: bfloat16 [3072], P(('rows', 'blk')), may hold values from -4 to 4
- rel_table: float32 [320, 12], replicated, may hold values from -6 to 6
- gate_weight: float32 [64, 8], replicated, may hold values from -0.375 to 0.375
- gate_scale: float32 [12], replicated, may hold values from 0.5 to 2
- cotangent: bfloat16 [40, 800, 768], P('rows', 'blk'), may hold values from -6 to 6
Outputs:
- hidden_out: bfloat16 [40, 800, 768], P('rows', 'blk')
- grad_input: bfloat16 [40, 800, 768], P('rows', 'blk')
- grad_qkv: float32 [768, 2304], P(('rows', 'blk'))
- grad_out: float32 [768, 768], P(('rows', 'blk'))
- grad_up: float32 [768, 3072], P(('rows', 'blk'))
- grad_down: float32 [3072, 768], P(('rows', 'blk'))
- grad_biases: float32 [768, 6], P(('rows', 'blk'))
- grad_gains: float32 [768, 2], P(('rows', 'blk'))
- grad_upbias: float32 [3072], P(('rows', 'blk'))
- grad_table: float32 [320, 12], replicated
- grad_gate_weight: float32 [64, 8], replicated
- grad_gate_scale: float32 [12], replicated
Inputs may be any that keep to these rules, and one draw needn't show every extreme that they name: `segment_ids`: along a row the utterance numbers never fall except to the padding 0, which closes every row; one utterance of each row runs from the first block of 200 frames to the last. `bucket_map`: entry d + 799 is the bucket of a key d frames after its query: 0 for d = 0, under 320 / 2 for d < 0, 160 or more for d > 0, never falling as the magnitude of d grows.
All inputs are finite; a program needn't handle non-finite values.
Results may differ from a plain program's by a relative error of at most 0.03.
Values may be sent and summed in bfloat16 or wider, within the bound.
No kernel may reach another device: no remote copies, remote signals or barrier semaphores. Data moves between devices by JAX's collectives and lax.ppermute only.
A program may use at most 256 MiB of HBM per device.

v0:
```python
import jax
import jax.numpy as jnp
from jax import lax
from jax.sharding import PartitionSpec as P

NEG_BIG = -1e30
EPS_NORM = 1e-05


def layer_norm(hidden, gain, shift):
    centred = hidden - jnp.mean(hidden, axis=-1, keepdims=True)
    spread = jnp.mean(centred * centred, axis=-1, keepdims=True)
    return centred * lax.rsqrt(spread + EPS_NORM) * gain + shift


def exact_gelu(inner):
    return jax.nn.gelu(inner, approximate=False)


def gate_values(tokens, gate_weight, gate_scale):
    head_count = gate_scale.shape[0]
    split_heads = tokens.reshape(tokens.shape[0], head_count, -1)
    first_dir = jnp.sum(gate_weight[:, :4], axis=1)
    second_dir = jnp.sum(gate_weight[:, 4:], axis=1)
    first_gate = jax.nn.sigmoid(
        jnp.einsum("nhd,d->nh", split_heads, first_dir, precision=lax.Precision.HIGHEST)
    )
    second_gate = jax.nn.sigmoid(
        jnp.einsum("nhd,d->nh", split_heads, second_dir, precision=lax.Precision.HIGHEST)
    )
    return first_gate * (second_gate * gate_scale - 1.0) + 2.0


def toeplitz_rows(table_values, row_total, col_total):
    head_count, length = table_values.shape
    tiled = jnp.broadcast_to(table_values[:, None, :], (head_count, row_total, length)).reshape(
        head_count, row_total * length
    )
    padded = jnp.pad(tiled, ((0, 0), (0, row_total)))
    shaped = padded.reshape(head_count, row_total, length + 1)
    return shaped[:, ::-1, :col_total]


def diagonal_sums(matrix):
    head_count, row_total, col_total = matrix.shape
    flipped = matrix[:, ::-1, :]
    padded = jnp.pad(flipped, ((0, 0), (0, 0), (0, row_total)))
    flat = padded.reshape(head_count, row_total * (row_total + col_total))[
        :, : row_total * (row_total + col_total - 1)
    ]
    return jnp.sum(flat.reshape(head_count, row_total, row_total + col_total - 1), axis=1)


def shards(
    hidden_in,
    segment_ids,
    bucket_map,
    qkv_weight,
    out_weight,
    up_weight,
    down_weight,
    bias_cols,
    norm_gains,
    up_bias,
    rel_table,
    gate_weight,
    gate_scale,
    cotangent,
):
    row_count, block_len, model_width = hidden_in.shape
    head_count = gate_scale.shape[0]
    head_dim = model_width // head_count
    bucket_count = rel_table.shape[0]
    token_count = row_count * block_len
    cycle_length = lax.axis_size("blk")
    frame_count = block_len * cycle_length
    cycle_place = lax.axis_index("blk")
    query_first = cycle_place * block_len
    scaling = head_dim ** (-0.5)
    gathered = (
        lax.all_gather(qkv_weight, ("rows", "blk"), axis=0, tiled=True),
        lax.all_gather(out_weight, ("rows", "blk"), axis=0, tiled=True),
        lax.all_gather(up_weight, ("rows", "blk"), axis=0, tiled=True),
        lax.all_gather(down_weight, ("rows", "blk"), axis=0, tiled=True),
        lax.all_gather(bias_cols, ("rows", "blk"), axis=0, tiled=True),
        lax.all_gather(norm_gains, ("rows", "blk"), axis=0, tiled=True),
        lax.all_gather(up_bias, ("rows", "blk"), axis=0, tiled=True),
    )
    qkv_full, out_full, up_full, down_full, bias_full, gains_full, upbias_full = gathered
    biases = bias_full.astype(jnp.float32)
    gain_cols = gains_full.astype(jnp.float32)
    inner_bias = upbias_full.astype(jnp.float32)
    tokens = hidden_in.reshape(token_count, model_width)
    tokens_f32 = tokens.astype(jnp.float32)
    projected = jnp.dot(tokens, qkv_full, preferred_element_type=jnp.float32)
    queries = ((projected[:, :model_width] + biases[:, 0]) * scaling).astype(jnp.bfloat16)
    keys_local = projected[:, model_width : 2 * model_width].astype(jnp.bfloat16)
    values_local = (projected[:, 2 * model_width :] + biases[:, 1]).astype(jnp.bfloat16)
    gating, gate_back = jax.vjp(gate_values, tokens_f32, gate_weight, gate_scale)
    gate_rows = gating.reshape(row_count, block_len, head_count).transpose(0, 2, 1)
    query_heads = queries.reshape(row_count, block_len, head_count, head_dim)
    segment_half = segment_ids.astype(jnp.bfloat16)
    bucket_ids = jnp.arange(bucket_count, dtype=jnp.int32)
    key_rows = keys_local.reshape(row_count, block_len, model_width)
    value_rows = values_local.reshape(row_count, block_len, model_width)

    def bias_block(offset, key_total):
        length = block_len + key_total - 1
        first_index = offset - query_first - block_len + frame_count
        chosen = lax.dynamic_slice_in_dim(bucket_map, first_index, length)
        one_hot = (chosen[:, None] == bucket_ids[None, :]).astype(jnp.float32)
        table_values = jnp.dot(one_hot, rel_table, precision=lax.Precision.HIGHEST)
        return (one_hot, toeplitz_rows(table_values.T, block_len, key_total))

    def scores_block(key_part, seg_part, offset):
        key_total = key_part.shape[1]
        key_heads = key_part.reshape(row_count, key_total, head_count, head_dim)
        raw = jnp.einsum(
            "rqhd,rkhd->rhqk", query_heads, key_heads, preferred_element_type=jnp.float32
        )
        one_hot, toeplitz = bias_block(offset, key_total)
        scores = raw + gate_rows[..., None] * toeplitz[None]
        allowed = (segment_half[:, :, None] == seg_part[:, None, :])[:, None]
        return (jnp.where(allowed, scores, NEG_BIG), allowed, one_hot, toeplitz, key_heads)

    running_max = jnp.full((row_count, head_count, block_len), NEG_BIG, jnp.float32)
    key_part = lax.all_gather(key_rows, "blk", axis=1, tiled=True)
    value_part = lax.all_gather(value_rows, "blk", axis=1, tiled=True)
    seg_part = lax.all_gather(segment_half, "blk", axis=1, tiled=True)
    scores, allowed, one_hot, toeplitz, key_heads = scores_block(key_part, seg_part, jnp.int32(0))
    new_max = jnp.maximum(running_max, jnp.max(scores, axis=-1))
    weights = jnp.where(allowed, jnp.exp(scores - new_max[..., None]), 0.0)
    value_heads = value_part.reshape(row_count, key_part.shape[1], head_count, head_dim)
    update = jnp.einsum(
        "rhqk,rkhd->rhqd",
        weights.astype(jnp.bfloat16),
        value_heads,
        preferred_element_type=jnp.float32,
    )
    totals = jnp.sum(weights, axis=-1)
    log_total = new_max + jnp.log(totals)
    attended_f32 = (update / totals[..., None]).transpose(0, 2, 1, 3)
    attended = attended_f32.reshape(token_count, model_width).astype(jnp.bfloat16)
    attn_out = jnp.dot(attended, out_full, preferred_element_type=jnp.float32) + biases[:, 2]
    normed, norm_one_back = jax.vjp(
        layer_norm, tokens_f32 + attn_out, gain_cols[:, 0], biases[:, 4]
    )
    normed_half = normed.astype(jnp.bfloat16)
    inner = jnp.dot(normed_half, up_full, preferred_element_type=jnp.float32) + inner_bias
    activated, gelu_back = jax.vjp(exact_gelu, inner)
    activated_half = activated.astype(jnp.bfloat16)
    residual_two = (
        normed
        + jnp.dot(activated_half, down_full, preferred_element_type=jnp.float32)
        + biases[:, 3]
    )
    result, norm_two_back = jax.vjp(layer_norm, residual_two, gain_cols[:, 1], biases[:, 5])
    hidden_out = result.astype(jnp.bfloat16).reshape(row_count, block_len, model_width)
    upstream = cotangent.reshape(token_count, model_width).astype(jnp.float32)
    grad_two, gain_two, shift_two = norm_two_back(upstream)
    down_in = grad_two.astype(jnp.bfloat16)
    down_grad = jnp.einsum("nf,nd->fd", activated_half, down_in, preferred_element_type=jnp.float32)
    grad_act = jnp.einsum("nd,fd->nf", down_in, down_full, preferred_element_type=jnp.float32)
    (grad_inner,) = gelu_back(grad_act)
    inner_half = grad_inner.astype(jnp.bfloat16)
    up_grad = jnp.einsum("nd,nf->df", normed_half, inner_half, preferred_element_type=jnp.float32)
    upbias_grad = jnp.sum(grad_inner, axis=0)
    grad_normed = grad_two + jnp.einsum(
        "nf,df->nd", inner_half, up_full, preferred_element_type=jnp.float32
    )
    grad_one, gain_one, shift_one = norm_one_back(grad_normed)
    attn_half = grad_one.astype(jnp.bfloat16)
    out_grad = jnp.einsum("nd,ne->de", attended, attn_half, preferred_element_type=jnp.float32)
    grad_attended = jnp.einsum(
        "ne,de->nd", attn_half, out_full, preferred_element_type=jnp.float32
    ).astype(jnp.bfloat16)
    out_heads = grad_attended.reshape(row_count, block_len, head_count, head_dim)
    delta = jnp.sum(out_heads.astype(jnp.float32) * attended_f32, axis=-1).transpose(0, 2, 1)
    key_part = lax.all_gather(key_rows, "blk", axis=1, tiled=True)
    value_part = lax.all_gather(value_rows, "blk", axis=1, tiled=True)
    seg_part = lax.all_gather(segment_half, "blk", axis=1, tiled=True)
    key_total = key_part.shape[1]
    key_total = key_part.shape[1]
    scores, allowed, one_hot, toeplitz, key_heads = scores_block(key_part, seg_part, jnp.int32(0))
    probs = jnp.where(allowed, jnp.exp(scores - log_total[..., None]), 0.0)
    value_heads = value_part.reshape(row_count, key_total, head_count, head_dim)
    grad_probs = jnp.einsum(
        "rqhd,rkhd->rhqk", out_heads, value_heads, preferred_element_type=jnp.float32
    )
    grad_scores = probs * (grad_probs - delta[..., None])
    scores_half = grad_scores.astype(jnp.bfloat16)
    query_add = jnp.einsum(
        "rhqk,rkhd->rqhd", scores_half, key_heads, preferred_element_type=jnp.float32
    )
    key_update = jnp.einsum(
        "rhqk,rqhd->rkhd", scores_half, query_heads, preferred_element_type=jnp.float32
    )
    value_update = jnp.einsum(
        "rhqk,rqhd->rkhd", probs.astype(jnp.bfloat16), out_heads, preferred_element_type=jnp.float32
    )
    gate_add = jnp.sum(grad_scores * toeplitz[None], axis=-1)
    diagonal = diagonal_sums(jnp.sum(grad_scores * gate_rows[..., None], axis=0))
    table_add = jnp.dot(one_hot.T, diagonal.T, precision=lax.Precision.HIGHEST)
    query_add, key_update, value_update, gate_add, table_add = (
        query_add,
        key_update,
        value_update,
        gate_add,
        table_add,
    )
    grad_keys = key_update
    grad_values = value_update
    grad_query, grad_keys, grad_values, grad_gate, grad_table = (
        query_add,
        grad_keys,
        grad_values,
        gate_add,
        table_add,
    )
    key_sums, value_sums = (
        lax.psum_scatter(
            grad_keys.reshape(row_count, frame_count, model_width).astype(jnp.bfloat16),
            "blk",
            scatter_dimension=1,
            tiled=True,
        ).astype(jnp.float32),
        lax.psum_scatter(
            grad_values.reshape(row_count, frame_count, model_width).astype(jnp.bfloat16),
            "blk",
            scatter_dimension=1,
            tiled=True,
        ).astype(jnp.float32),
    )
    query_half = grad_query.reshape(token_count, model_width).astype(jnp.bfloat16)
    query_scaled = (query_half.astype(jnp.float32) * scaling).astype(jnp.bfloat16)
    keys_half = key_sums.reshape(token_count, model_width).astype(jnp.bfloat16)
    values_half = value_sums.reshape(token_count, model_width).astype(jnp.bfloat16)
    stacked = jnp.concatenate([query_scaled, keys_half, values_half], axis=1)
    qkv_grad = jnp.einsum("nd,ne->de", tokens, stacked, preferred_element_type=jnp.float32)
    grad_tokens = grad_one + jnp.einsum(
        "ne,de->nd", stacked, qkv_full, preferred_element_type=jnp.float32
    )
    gate_tokens, gate_weight_grad, gate_scale_grad = gate_back(
        grad_gate.transpose(0, 2, 1).reshape(token_count, head_count)
    )
    grad_input = (
        (grad_tokens + gate_tokens).astype(jnp.bfloat16).reshape(row_count, block_len, model_width)
    )
    bias_grad = jnp.stack(
        [
            jnp.sum(query_scaled.astype(jnp.float32), axis=0),
            jnp.sum(values_half.astype(jnp.float32), axis=0),
            jnp.sum(grad_one, axis=0),
            jnp.sum(grad_two, axis=0),
            shift_one,
            shift_two,
        ],
        axis=1,
    )
    gains_grad = jnp.stack([gain_one, gain_two], axis=1)
    qkv_sum, out_sum, up_sum, down_sum, bias_sum, gains_sum, upbias_sum = (
        lax.psum_scatter(qkv_grad, ("rows", "blk"), scatter_dimension=0, tiled=True),
        lax.psum_scatter(out_grad, ("rows", "blk"), scatter_dimension=0, tiled=True),
        lax.psum_scatter(up_grad, ("rows", "blk"), scatter_dimension=0, tiled=True),
        lax.psum_scatter(down_grad, ("rows", "blk"), scatter_dimension=0, tiled=True),
        lax.psum_scatter(bias_grad, ("rows", "blk"), scatter_dimension=0, tiled=True),
        lax.psum_scatter(gains_grad, ("rows", "blk"), scatter_dimension=0, tiled=True),
        lax.psum_scatter(upbias_grad, ("rows", "blk"), scatter_dimension=0, tiled=True),
    )
    table_sum, gate_weight_sum, gate_scale_sum = lax.psum(
        (grad_table, gate_weight_grad, gate_scale_grad), ("rows", "blk")
    )
    return (
        hidden_out,
        grad_input,
        qkv_sum,
        out_sum,
        up_sum,
        down_sum,
        bias_sum,
        gains_sum,
        upbias_sum,
        table_sum,
        gate_weight_sum,
        gate_scale_sum,
    )


def solution(mesh):
    placed = (
        P("rows", "blk", None),
        P("rows", "blk"),
        P(),
        P(("rows", "blk"), None),
        P(("rows", "blk"), None),
        P(("rows", "blk"), None),
        P(("rows", "blk"), None),
        P(("rows", "blk"), None),
        P(("rows", "blk"), None),
        P(("rows", "blk")),
        P(),
        P(),
        P(),
        P("rows", "blk", None),
    )
    return jax.shard_map(
        shards,
        mesh=mesh,
        in_specs=placed,
        out_specs=(
            P("rows", "blk", None),
            P("rows", "blk", None),
            P(("rows", "blk"), None),
            P(("rows", "blk"), None),
            P(("rows", "blk"), None),
            P(("rows", "blk"), None),
            P(("rows", "blk"), None),
            P(("rows", "blk"), None),
            P(("rows", "blk")),
            P(),
            P(),
            P(),
        ),
        check_vma=False,
    )
```

profile of v0, /device:TPU:0, one launch (start us, length us, event | category | flops | bytes accessed | tf_op | source)
XLA Modules:
  0.0 1449.7 jit_solution(8607601486546100197)
XLA Ops:
  8.0 65.7 %all-gather.10.cloned.1.call-done = bf16[768,2304]{1,0:T(8,128)(2,1)} async-done(((bf16[24,2304]{1,0:T(8,128)(2,1)}), bf16[768,2304]{1,0:T(8,128)(2,1)}) %all-gather.10.cloned.1.call-update) | async-done | bytes 3538960 | tf_op jit(solution)/shard_map/all_gather | solution.py:81
  73.7 6.2 fusion.84
  84.9 68.1 %all-gather.1 = bf16[32,24,6]{1,2,0:T(8,128)(2,1)S(1)} all-gather(bf16[1,24,6]{1,2,0:T(8,128)(2,1)S(1)} %bitcast.175), channel_id=1, replica_groups=mesh['rows'=8,'blk'=4] {'rows','blk'}, dimensions={0}, use_global_device_ids=true | all-gather | bytes 9504 | tf_op jit(solution)/shard_map/all_gather | solution.py:85
  164.9 43.3 %all-reduce.4 = bf16[3072]{0:T(1024)(128)(2,1)S(1)} all-reduce(bf16[3072]{0:T(1024)(128)(2,1)S(1)} %dynamic-update-slice), channel_id=1, replica_groups=mesh['rows'=8,'blk'=4] {'rows','blk'}, use_global_device_ids=true, to_apply=%add.4 | all-reduce | flops 3072 | bytes 12288
  208.2 14.3 all-gather
  222.6 72.5 %all-gather.2 = bf16[32,24,2]{1,2,0:T(2,128)(2,1)S(1)} all-gather(bf16[1,24,2]{1,2,0:T(2,128)(2,1)S(1)} %bitcast.176), channel_id=1, replica_groups=mesh['rows'=8,'blk'=4] {'rows','blk'}, dimensions={0}, use_global_device_ids=true | all-gather | bytes 3168 | tf_op jit(solution)/shard_map/all_gather | solution.py:86
  300.1 5.1 fusion.63
  326.5 16.8 %reshape.202 = f32[12,199800]{1,0:T(8,128)} reshape(f32[12,200,999]{2,1,0:T(8,128)} %broadcast_in_dim.43) | data formatting | bytes 19180800 | tf_op jit(solution)/shard_map/reshape | solution.py:36
  343.3 10.4 pad.15
  353.7 18.8 %reshape.203 = f32[12,200,1000]{2,1,0:T(8,128)} reshape(f32[12,200000]{1,0:T(8,128)} %pad.15) | data formatting | bytes 19200000 | tf_op jit(solution)/shard_map/reshape | solution.py:40
  372.6 7.3 slice.65
  379.8 81.6 %rev.7 = f32[12,200,800]{2,1,0:T(8,128)} reverse(f32[12,200,800]{2,1,0:T(8,128)} %slice.65), dimensions={1} | reverse | bytes 15360000 | tf_op jit(solution)/shard_map/rev | solution.py:41
  464.0 5.8 reshape.242
  469.7 6.0 copy.126
  475.8 9.6 copy.125
  485.4 23.0 %fusion.79 = (f32[5,12,200]{2,1,0:T(8,128)S(1)}, f32[5,12,200,800]{3,2,1,0:T(8,128)}) fusion(f32[12,200,800]{2,1,0:T(8,128)} %rev.7, f32[5,12,200]{2,1,0:T(8,128)S(1)} %copy.128, bf16[5,200,12,64]{1,3,2,0:T(8,128)(2,1)} %copy.126, bf16[5,800,12,64]{1,3,2,0:T(8,128)(2,1)} %bitcast.147, pred[5,200,800]{2,1,0:T(8,128)(4,1)S(1)} %broadcast_compare_fusion), kind=kOutput, calls=%fused_computation.148 | convolution fusion | flops 1267187968 | bytes 54656000 | tf_op jit(solution)/shard_map/rqhd,rkhd->rhqk/dot_general | solution.py:118
  508.4 19.1 %fusion = f32[5,12,200]{2,1,0:T(8,128)S(1)} fusion(f32[5,12,200,800]{3,2,1,0:T(8,128)} %get-tuple-element.121, f32[5,12,200]{2,1,0:T(8,128)S(1)} %broadcast_maximum_fusion, pred[5,200,800]{2,1,0:T(8,128)(4,1)S(1)} %broadcast_compare_fusion), kind=kLoop, calls=%fused_computation.6 | loop fusion | flops 28788000 | bytes 39296000 | tf_op jit(solution)/shard_map/reduce_sum | solution.py:140
  527.6 9.5 copy.129
  537.1 21.3 %fusion.80 = (bf16[5,200,12,64]{1,3,2,0:T(8,128)(2,1)}, f32[5,200,12,64]{1,3,2,0:T(8,128)}) fusion(f32[5,200,12]{1,2,0:T(8,128)S(1)} %bitcast.169, bf16[5,800,12,64]{1,3,2,0:T(8,128)(2,1)} %bitcast.153, f32[5,12,200,800]{3,2,1,0:T(8,128)} %get-tuple-element.121, f32[5,12,200]{2,1,0:T(8,128)S(1)} %broadcast_maximum_fusion, ...), kind=kOutput, calls=%fused_computation.149 | convolution fusion | flops 1259136000 | bytes 50048000 | tf_op jit(solution)/shard_map/rhqk,rkhd->rhqd/dot_general | solution.py:134
  570.6 35.4 %multiply_convert_fusion = (bf16[1000,3072]{1,0:T(8,128)(2,1)}, f32[1000,3072]{1,0:T(8,128)}, f32[1000,3072]{1,0:T(8,128)}) fusion(f32[3072]{0:T(1024)S(1)} %convert_element_type.146, bf16[768,3072]{1,0:T(8,128)(2,1)} %all-gather.18.cloned.1.call-done, f32[1000,768]{1,0:T(8,128)S(1)} %get-tuple-element.125, f32[768]{0:T(1024)S(1)} %get-tuple-element.93, ...), kind=kOutput, calls=%fused_computation.20 | convolution fusion | flops 4925184000 | bytes 38537024 | tf_op jit(solution)/shard_map/dot_general | solution.py:149
  606.0 9.6 fusion.82
  624.0 17.5 %fusion.83 = (f32[3072]{0:T(1024)}, bf16[1000,3072]{1,0:T(8,128)(2,1)}) fusion(f32[1000,3072]{1,0:T(8,128)} %get-tuple-element.112, bf16[3072,768]{1,0:T(8,128)(2,1)} %all-gather.20.cloned.1.call-done, f32[1000,768]{1,0:T(8,128)} %get-tuple-element.115, f32[1000]{0:T(1024)S(1)} %negate_multiply_fusion.2, f32[1000,3072]{1,0:T(8,128)} %get-tuple-element.126, ...), kind=kOutput, calls=%fused_computation.152 | convolution fusion | flops 4769276928 | bytes 38539168 | tf_op jit(solution)/shard_map/nd,fd->nf/dot_general | solution.py:163
  641.4 10.8 multiply_reduce_fusion.3
  666.4 20.7 %fusion.26 = bf16[5,12,64,800]{3,2,1,0:T(8,128)(2,1)} fusion(bf16[5,200,12,64]{1,3,2,0:T(8,128)(2,1)S(1)} %copy.134, f32[5,12,200,800]{3,2,1,0:T(8,128)} %get-tuple-element.121, f32[5,12,200]{2,1,0:T(8,128)S(1)} %copy-done.16, pred[5,200,800]{2,1,0:T(8,128)(4,1)S(1)} %copy-done.8), kind=kOutput, calls=%fused_computation.39 | convolution fusion | flops 1260672000 | bytes 46928000 | tf_op jit(solution)/shard_map/rhqk,rqhd->rkhd/dot_general | solution.py:198
  687.1 13.9 copy.152
  701.0 8.5 copy.167
  712.7 38.5 %multiply_reduce_fusion = (f32[12,200,800]{2,1,0:T(8,128)}, f32[5,12,200]{2,1,0:T(8,128)S(1)}, bf16[5,12,200,800]{3,2,1,0:T(8,128)(2,1)}) fusion(f32[5,12,200]{2,1,0:T(8,128)S(1)} %copy-done.18, f32[12,200,800]{2,1,0:T(8,128)} %rev.7, f32[5,12,200]{2,1,0:T(8,128)S(1)} %bitcast.171, bf16[5,200,12,64]{1,3,2,0:T(8,128)(2,1)S(1)} %copy.134, ...), kind=kOutput, calls=%fused_computation | convolution fusion | flops 1313267968 | bytes 81632000 | tf_op jit(solution)/shard_map/rqhd,rkhd->rhqk/dot_general | solution.py:187
  751.1 15.5 %fusion.23 = bf16[5,12,64,800]{3,2,1,0:T(8,128)(2,1)} fusion(bf16[5,200,12,64]{1,3,2,0:T(8,128)(2,1)} %copy.126, bf16[5,12,200,800]{3,2,1,0:T(8,128)(2,1)} %get-tuple-element.130), kind=kOutput, calls=%fused_computation.38 | convolution fusion | flops 1231872000 | bytes 26880000 | tf_op jit(solution)/shard_map/rhqk,rqhd->rkhd/dot_general | solution.py:195
  766.6 13.9 copy.150
  780.4 8.8 copy.166
  789.3 5.5 fusion.73
  794.8 10.6 fusion.33
  807.3 10.9 fusion.71
  818.3 15.8 %convert_reduce_fusion = (f32[12,64]{1,0:T(8,128)S(1)}, bf16[5,200,12,64]{1,3,2,0:T(8,128)(2,1)}) fusion(bf16[5,800,12,64]{1,3,2,0:T(8,128)(2,1)} %bitcast.148, bf16[5,12,200,800]{3,2,1,0:T(8,128)(2,1)} %get-tuple-element.130), kind=kOutput, calls=%fused_computation.45 | convolution fusion | flops 1233407232 | bytes 26883072 | tf_op jit(solution)/shard_map/rhqk,rkhd->rqhd/dot_general | solution.py:192
  838.7 5.5 convert_element_type.159
  854.6 73.6 %reduce-scatter.21.cloned.1.call-done = bf16[200,3840]{1,0:T(8,128)(2,1)} async-done(((bf16[800,3840]{1,0:T(8,128)(2,1)}), bf16[200,3840]{1,0:T(8,128)(2,1)}) %reduce-scatter.21.cloned.1.call-update) | async-done | bytes 1536016
  938.3 9.7 convolution_bitcast_fusion
  947.9 8.3 copy.154
  960.6 81.5 %rev.8 = f32[12,200,800]{2,1,0:T(8,128)} reverse(f32[12,200,800]{2,1,0:T(8,128)} %get-tuple-element.84), dimensions={1} | reverse | bytes 15360000 | tf_op jit(solution)/shard_map/rev | solution.py:46
  1042.2 8.8 pad.16
  1051.0 20.1 %reshape.211 = f32[12,200000]{1,0:T(8,128)} reshape(f32[12,200,1000]{2,1,0:T(8,128)} %pad.16) | data formatting | bytes 19200000 | tf_op jit(solution)/shard_map/reshape | solution.py:48
  1071.1 10.7 slice.74
  1081.8 18.5 %reshape.212 = f32[12,200,999]{2,1,0:T(8,128)} reshape(f32[12,199800]{1,0:T(8,128)} %slice.74) | data formatting | bytes 19180800 | tf_op jit(solution)/shard_map/reshape | solution.py:51
  1114.9 43.2 %all-reduce.8 = (f32[768,6]{0,1:T(8,128)S(1)}, f32[768,2]{0,1:T(2,128)S(1)}, f32[3072]{0:T(1024)S(1)}, f32[320,12]{0,1:T(8,128)}, f32[64,8]{0,1:T(8,128)}, /*index=5*/f32[12]{0:T(128)}) all-reduce(f32[768,6]{0,1:T(8,128)S(1)} %stack.36, f32[768,2]{0,1:T(2,128)S(1)} %pad_maximum_fusion.5, ...), channel_id=8, replica_groups=mesh['rows'=8,'blk'=4] {'rows','blk'}, use_global_device_ids=true, to_apply=%region_26.27.clone | all-reduce | flops 13580 | bytes 108640
  1160.0 10.3 add_convert_fusion
  1170.3 5.9 reduce-scatter.17.cloned.1.call-done
  1176.2 141.1 %reduce-scatter.19.cloned.1.call-done = f32[96,768]{1,0:T(8,128)} async-done(((f32[3072,768]{1,0:T(8,128)}), f32[96,768]{1,0:T(8,128)}) %reduce-scatter.19.cloned.1.call-update) | async-done | bytes 294928 | tf_op jit(solution)/shard_map/reduce_scatter | solution.py:265
  1317.2 125.1 %reduce-scatter.25.cloned.1.call-done = f32[24,2304]{1,0:T(8,128)} async-done(((f32[768,2304]{1,0:T(8,128)}), f32[24,2304]{1,0:T(8,128)}) %reduce-scatter.25.cloned.1.call-update) | async-done | bytes 221200
  (208 shorter events, 131.6 us)
Async XLA Ops:
  7.2 313.4 %copy-start = (f32[320,12]{0,1:T(8,128)S(1)}, f32[320,12]{0,1:T(8,128)}, u32[]{:S(2)}) copy-start(f32[320,12]{0,1:T(8,128)} %param.24) | copy-start | bytes 46084
  7.2 66.5 %all-gather.10.cloned.1.call-start = ((), (), s32[]{:S(2)}) async-start(), calls=%async_computation.6 | async-start | bytes 3649536 | tf_op jit(solution)/shard_map/all_gather | solution.py:81
  7.9 467.8 %all-gather.12.cloned.1.call-start = ((), (), s32[]{:S(2)}) async-start(), calls=%async_computation.7 | async-start | bytes 7680000 | tf_op jit(solution)/shard_map/all_gather | solution.py:127
  79.9 3.6 copy-start.13
  84.8 442.8 %all-gather.14.cloned.1.call-start = ((), (), s32[]{:S(2)}) async-start(), calls=%async_computation.8 | async-start | bytes 7680000 | tf_op jit(solution)/shard_map/all_gather | solution.py:128
  154.0 6.9 copy-start.25
  154.0 6.9 copy-start.15
  159.0 5.6 copy-start.33
  159.0 5.6 copy-start.43
  159.0 63.5 %copy-start.41 = (bf16[24,2]{0,1:T(2,128)(2,1)S(1)}, bf16[24,2]{0,1:T(2,128)(2,1)}, u32[]{:S(2)}) copy-start(bf16[24,2]{0,1:T(2,128)(2,1)} %param.22) | copy-start | bytes 292
  159.1 406.1 %all-gather.16.cloned.1.call-start = ((), (), s32[]{:S(2)}) async-start(), calls=%async_computation.9 | async-start | bytes 1216512 | tf_op jit(solution)/shard_map/all_gather | solution.py:82
  159.6 411.0 %all-gather.18.cloned.1.call-start = ((), (), s32[]{:S(2)}) async-start(), calls=%async_computation.10 | async-start | bytes 4866048 | tf_op jit(solution)/shard_map/all_gather | solution.py:83
  160.2 445.8 %all-gather.20.cloned.1.call-start = ((), (), s32[]{:S(2)}) async-start(), calls=%async_computation.11 | async-start | bytes 4866048 | tf_op jit(solution)/shard_map/all_gather | solution.py:84
  160.8 683.5 %reduce-scatter.23.cloned.1.call-start = ((), (), s32[]{:S(2)}) async-start(), calls=%async_computation.16 | async-start | bytes 7680000
  164.6 140.6 %copy-start.29 = (f32[64]{0:T(128)}, f32[64]{0:T(128)S(1)}, u32[]{:S(2)}) copy-start(f32[64]{0:T(128)S(1)} %get-tuple-element.99) | copy-start | bytes 772
  164.6 145.5 %copy-start.31 = (f32[64]{0:T(128)}, f32[64]{0:T(128)S(1)}, u32[]{:S(2)}) copy-start(f32[64]{0:T(128)S(1)} %get-tuple-element.100) | copy-start | bytes 772
  295.4 166.7 %copy-start.23 = (f32[768]{0:T(1024)}, f32[768]{0:T(1024)S(1)}, u32[]{:S(2)}) copy-start(f32[768]{0:T(1024)S(1)} %get-tuple-element.97) | copy-start | bytes 9220
  300.1 10.1 copy-start.9
  310.1 10.1 copy-start.19
  315.3 4.9 copy-start.37
  315.3 5.2 copy-start.40
  320.2 6.3 copy-start.21
  320.4 164.9 %copy-start.17 = (f32[5,12,200]{2,1,0:T(8,128)}, f32[5,12,200]{2,1,0:T(8,128)S(1)}, u32[]{:S(2)}) copy-start(f32[5,12,200]{2,1,0:T(8,128)S(1)} %copy.128) | copy-start | bytes 144004
  320.5 5.9 copy-start.34
  379.8 82.3 %copy-start.5 = (bf16[5,200,768]{2,1,0:T(8,128)(2,1)S(1)}, bf16[5,200,768]{2,1,0:T(8,128)(2,1)}, u32[]{:S(2)}) copy-start(bf16[5,200,768]{2,1,0:T(8,128)(2,1)} %param.27) | copy-start | bytes 4608004
  462.1 75.0 %copy-start.7 = (pred[5,200,800]{2,1,0:T(8,128)(4,1)}, pred[5,200,800]{2,1,0:T(8,128)(4,1)S(1)}, u32[]{:S(2)}) copy-start(pred[5,200,800]{2,1,0:T(8,128)(4,1)S(1)} %broadcast_compare_fusion) | copy-start | bytes 2400004
  569.0 83.3 %copy-start.2 = (f32[1000,768]{1,0:T(8,128)}, f32[1000,768]{1,0:T(8,128)S(1)}, u32[]{:S(2)}) copy-start(f32[1000,768]{1,0:T(8,128)S(1)} %get-tuple-element.125) | copy-start | bytes 9216004
  570.6 35.4 %copy-start.36 = (f32[768]{0:T(1024)S(1)}, f32[768]{0:T(1024)}, u32[]{:S(2)}) copy-start(f32[768]{0:T(1024)} %get-tuple-element.92) | copy-start | bytes 9220
  606.0 10.1 copy-start.12
  652.3 3.3 copy-start.42
  661.3 5.1 copy-start.8
  661.3 5.1 copy-start.16
  709.5 218.6 %reduce-scatter.21.cloned.1.call-start = ((), (), s32[]{:S(2)}) async-start(), calls=%async_computation.15 | async-start | bytes 7680000
  789.2 5.6 copy-start.3
  789.2 381.0 %reduce-scatter.15.cloned.1.call-start = ((), (), s32[]{:S(2)}) async-start(), calls=%async_computation.12 | async-start | bytes 2433024 | tf_op jit(solution)/shard_map/reduce_scatter | solution.py:263
  794.8 381.4 %reduce-scatter.17.cloned.1.call-start = ((), (), s32[]{:S(2)}) async-start(), calls=%async_computation.13 | async-start | bytes 9732096 | tf_op jit(solution)/shard_map/reduce_scatter | solution.py:264
  805.5 511.8 %reduce-scatter.19.cloned.1.call-start = ((), (), s32[]{:S(2)}) async-start(), calls=%async_computation.14 | async-start | bytes 9732096 | tf_op jit(solution)/shard_map/reduce_scatter | solution.py:265
  818.3 624.0 %reduce-scatter.25.cloned.1.call-start = ((), (), s32[]{:S(2)}) async-start(), calls=%async_computation.17 | async-start | bytes 7299072
  1100.3 5.0 copy-start.20
  1100.3 5.0 copy-start.22
  1100.3 5.0 copy-start.38
  1100.3 5.2 copy-start.30
  1100.3 5.2 copy-start.32
  1105.5 5.9 copy-start.10
  1107.6 6.5 copy-start.35
  1107.6 7.2 copy-start.28
  1107.6 52.4 %copy-start.14 = (bf16[1000,768]{0,1:T(8,128)(2,1)S(1)}, bf16[1000,768]{0,1:T(8,128)(2,1)}, u32[]{:S(2)}) copy-start(bf16[1000,768]{0,1:T(8,128)(2,1)} %copy.142) | copy-start | bytes 4608004
  1160.0 282.3 %copy-start.1 = (f32[320,12]{0,1:T(8,128)S(1)}, f32[320,12]{0,1:T(8,128)}, u32[]{:S(2)}) copy-start(f32[320,12]{0,1:T(8,128)} %param.24) | copy-start | bytes 46084
  (8 other events, 16.2 us)
Sparse Core Ops, SparseCore 0:
  10.8 62.8 all-gather.9
  84.9 113.6 all-gather.11
  200.8 111.5 all-gather.13
  315.1 52.3 all-gather.15
  370.1 62.4 all-gather.17
  435.3 62.3 all-gather.19
  709.6 107.0 reduce-scatter.22
  819.1 109.0 reduce-scatter.20
  934.0 99.4 reduce-scatter.14
  1040.9 135.2 reduce-scatter.16
  1182.6 134.5 reduce-scatter.18
  1324.3 117.9 reduce-scatter.24
where the time goes:
time: 1470 us; the launch traced here: 1450 us
  local copies, waits for them, and re-layouts  442 us (30%)
  waiting for transfers between devices  414 us (28%)
  matrix products  281 us (19%)
  blocking collectives  241 us (16%)
  other arithmetic  55.3 us (4%)
  between operations  15.5 us (1%)
    unnamed x15, waiting for transfers between devices  201 us
    reduce_scatter x1, waiting for transfers between devices, shards(): lax.psum_scatter(down_grad, ('rows', 'blk'), scatter_dimension=0, tiled=T...  141 us
    unnamed x2, blocking collectives  86.5 us
    rev x1, local copies, waits for them, and re-layouts, toeplitz_rows(): return shaped[:, ::-1, :col_total]  81.6 us
    rev x1, local copies, waits for them, and re-layouts, diagonal_sums(): flipped = matrix[:, ::-1, :]  81.5 us
    unnamed x103, local copies, waits for them, and re-layouts  79 us
    all_gather x1, blocking collectives, shards(): lax.all_gather(norm_gains, ('rows', 'blk'), axis=0, tiled=True)  72.5 us
    all_gather x1, blocking collectives, shards(): lax.all_gather(bias_cols, ('rows', 'blk'), axis=0, tiled=True)  68.1 us
  transfers between devices with their start and end apart: 12, of which 5 were waited for; matrix products, arithmetic and copies ran while one was open for 46% of the time, Pallas kernels for 0%

commit v1 on v0

v1 whole, which is shorter than its diff:
```python
import functools

import jax
import jax.numpy as jnp
from jax import lax
from jax.experimental import pallas as pl
from jax.experimental.pallas import tpu as pltpu
from jax.sharding import PartitionSpec as P

EPS_NORM = 1e-05
LANES = 128
SMALL = 128
BF16 = jnp.bfloat16
F32 = jnp.float32
NN = (((1,), (0,)), ((), ()))
NT = (((1,), (1,)), ((), ()))
TN = (((0,), (0,)), ((), ()))
HIGHEST = lax.Precision.HIGHEST


def dotf(a, b, dims):
    return lax.dot_general(a, b, dims, preferred_element_type=F32)


def tiles_of(total, tile):
    return [(s, min(tile, total - s)) for s in range(0, total, tile)]


def exp_rows(u_ref, head, width):
    return pltpu.roll(
        jnp.broadcast_to(u_ref[head : head + 1, :], (LANES, width)), 0, 1, stride=1, stride_axis=0
    )


def forward_kernel(
    tile, flip, u_ref, q_ref, k_ref, v_ref, qa_ref, ka_ref, g_ref, o_ref, ob_ref, lse_ref, t_scr
):
    nq, nk, width = q_ref.shape[0], k_ref.shape[0], u_ref.shape[-1]
    half = LANES // 2
    shift = -(-nk // LANES)
    low = lax.broadcasted_iota(jnp.int32, (1, LANES), 1) < half
    low_rows = lax.broadcasted_iota(jnp.int32, (LANES, 1), 0) < half
    k, v, q = k_ref[...], v_ref[...], q_ref[...]
    zero = jnp.zeros((), BF16)
    khs, qhs, vzs = [], [], []
    for hh in range(2):
        t_scr[hh] = exp_rows(u_ref, hh, width)
        sel = low if hh == 0 else jnp.logical_not(low)
        khs.append(jnp.where(sel, k, ka_ref[...]))
        qhs.append(jnp.where(sel, q, qa_ref[...]))
        vzs.append(jnp.where(sel, v, zero))
    vt = v.T if flip else None
    for first, cols in tiles_of(nq, tile):
        total, scales, parts = None, [], []
        for hh in range(2):
            raw = dotf(khs[hh], qhs[hh][first : first + cols], NT)
            g = g_ref[hh : hh + 1, first : first + cols]
            scores, peak = [], None
            for f2, r2 in tiles_of(nk, LANES):
                col = (shift - f2 // LANES) * LANES + first
                s = raw[f2 : f2 + r2] + g * t_scr[hh, 0:r2, col : col + cols]
                top = jnp.max(s, axis=0, keepdims=True)
                peak = top if peak is None else jnp.maximum(peak, top)
                scores.append(s)
            probs, mass = [], None
            for s in scores:
                p = jnp.exp(s - peak)
                part = jnp.sum(p, axis=0, keepdims=True)
                mass = part if mass is None else mass + part
                probs.append(p.astype(BF16))
            lse_ref[hh : hh + 1, first : first + cols] = peak + jnp.log(mass)
            pb = jnp.concatenate(probs, axis=0)
            if flip:
                parts.append(dotf(vt[hh * half : (hh + 1) * half], pb, NN) / mass)
            else:
                x = dotf(pb, vzs[hh], TN)
                total = x if total is None else total + x
                scales.append(1.0 / mass)
        if flip:
            o = jnp.concatenate(parts, axis=0).T
        else:
            o = total * jnp.where(low_rows, scales[0], scales[1]).T
        o_ref[first : first + cols, :] = o
        ob_ref[first : first + cols, :] = o.astype(BF16)


def attend_forward(u, q, k, v, qa, ka, g, cols, tile, flip):
    nq, nk = q.shape[0], k.shape[0]
    pairs, _, width = u.shape
    col = lambda c: (lambda p: (0, c + p))
    fix = lambda p: (0, 0)
    row_spec = pl.BlockSpec((None, 2, nq), lambda p: (p, 0, 0))
    return pl.pallas_call(
        functools.partial(forward_kernel, tile, flip),
        grid=(pairs,),
        in_specs=[
            pl.BlockSpec((None, 2, width), lambda p: (p, 0, 0)),
            pl.BlockSpec((nq, LANES), col(cols[0])),
            pl.BlockSpec((nk, LANES), col(cols[1])),
            pl.BlockSpec((nk, LANES), col(cols[2])),
            pl.BlockSpec((nq, LANES), fix),
            pl.BlockSpec((nk, LANES), fix),
            row_spec,
        ],
        out_specs=[
            pl.BlockSpec((nq, LANES), lambda p: (0, p)),
            pl.BlockSpec((nq, LANES), lambda p: (0, p)),
            row_spec,
        ],
        out_shape=[
            jax.ShapeDtypeStruct((nq, pairs * LANES), F32),
            jax.ShapeDtypeStruct((nq, pairs * LANES), BF16),
            jax.ShapeDtypeStruct((pairs, 2, nq), F32),
        ],
        scratch_shapes=[pltpu.VMEM((2, LANES, width), F32)],
        compiler_params=pltpu.CompilerParams(vmem_limit_bytes=48 * 2**20),
        name="attention_forward",
    )(u, q, k, v, qa, ka, g)


def backward_kernel(
    u_ref, q_ref, k_ref, v_ref, do_ref, att_ref, qa_ref, ka_ref, g_ref, lse_ref,
    dq_ref, dkv_ref, gate_ref, diag_ref, t_scr, c_scr,
):
    nq, nk, width = q_ref.shape[0], k_ref.shape[0], u_ref.shape[-1]
    shift = -(-nk // LANES)
    low = lax.broadcasted_iota(jnp.int32, (1, LANES), 1) < LANES // 2
    k, v, q, do = k_ref[...], v_ref[...], q_ref[...], do_ref[...]
    prod = do.astype(F32) * att_ref[...]
    zero = jnp.zeros((), BF16)
    dq, dk, dv = None, None, None
    for hh in range(2):
        t_scr[hh] = exp_rows(u_ref, hh, width)
        c_scr[...] = jnp.zeros_like(c_scr)
        sel = low if hh == 0 else jnp.logical_not(low)
        ones = jnp.broadcast_to(jnp.where(sel, 1.0, 0.0), (8, LANES))
        delta = lax.dot_general(ones, prod, NT, precision=HIGHEST, preferred_element_type=F32)[0:1]
        ka = jnp.where(sel, k, ka_ref[...])
        qa = jnp.where(sel, q, qa_ref[...])
        kz, qz, doz = jnp.where(sel, k, zero), jnp.where(sel, q, zero), jnp.where(sel, do, zero)
        lse = lse_ref[hh : hh + 1, :]
        g = g_ref[hh : hh + 1, :]
        gate = jnp.zeros((1, nq), F32)
        raw = dotf(ka, qa, NT)
        dp = dotf(v, doz, NT)
        ps, ds = [], []
        for first, rows in tiles_of(nk, LANES):
            col = (shift - first // LANES) * LANES
            t = t_scr[hh, 0:rows, col : col + nq]
            p = jnp.exp(raw[first : first + rows] + (g * t - lse))
            d = p * (dp[first : first + rows] - delta)
            gate += jnp.sum(d * t, axis=0, keepdims=True)
            c_scr[0:rows, col : col + nq] += d * g
            ps.append(p.astype(BF16))
            ds.append(d.astype(BF16))
        pb, db = jnp.concatenate(ps, axis=0), jnp.concatenate(ds, axis=0)
        dk_add, dv_add, dq_add = dotf(db, qz, NN), dotf(pb, doz, NN), dotf(db, kz, TN)
        dk = dk_add if dk is None else dk + dk_add
        dv = dv_add if dv is None else dv + dv_add
        dq = dq_add if dq is None else dq + dq_add
        gate_ref[hh : hh + 1, :] = gate
        half = LANES // 2
        acc = c_scr[...]
        while half >= 8:
            acc = acc[:half] + pltpu.roll(acc[half:], width - half, 1)
            half //= 2
        row = lax.broadcasted_iota(jnp.int32, (8, 1), 0)
        for bit in (1, 2, 4):
            acc = jnp.where((row & bit) != 0, pltpu.roll(acc, width - bit, 1), acc)
        diag_ref[hh : hh + 1, :] = jnp.sum(acc, axis=0, keepdims=True)
    dq_ref[...] = (dq.astype(BF16) * (LANES // 2) ** -0.5).astype(BF16)
    dkv_ref[0] = dk.astype(BF16)
    dkv_ref[1] = dv.astype(BF16)


def attend_backward(u, q, k, v, do, att, qa, ka, g, lse, cols):
    nq, nk = q.shape[0], k.shape[0]
    pairs, _, width = u.shape
    col = lambda c: (lambda p: (0, c + p))
    fix = lambda p: (0, 0)
    row_spec = pl.BlockSpec((None, 2, nq), lambda p: (p, 0, 0))
    wide_spec = pl.BlockSpec((None, 2, width), lambda p: (p, 0, 0))
    return pl.pallas_call(
        backward_kernel,
        grid=(pairs,),
        in_specs=[
            wide_spec,
            pl.BlockSpec((nq, LANES), col(cols[0])),
            pl.BlockSpec((nk, LANES), col(cols[1])),
            pl.BlockSpec((nk, LANES), col(cols[2])),
            pl.BlockSpec((nq, LANES), col(0)),
            pl.BlockSpec((nq, LANES), col(0)),
            pl.BlockSpec((nq, LANES), fix),
            pl.BlockSpec((nk, LANES), fix),
            row_spec,
            row_spec,
        ],
        out_specs=[
            pl.BlockSpec((nq, LANES), col(0)),
            pl.BlockSpec((2, nk, LANES), lambda p: (0, 0, p)),
            row_spec,
            wide_spec,
        ],
        out_shape=[
            jax.ShapeDtypeStruct((nq, pairs * LANES), BF16),
            jax.ShapeDtypeStruct((2, nk, pairs * LANES), BF16),
            jax.ShapeDtypeStruct((pairs, 2, nq), F32),
            jax.ShapeDtypeStruct((pairs, 2, width), F32),
        ],
        scratch_shapes=[pltpu.VMEM((2, LANES, width), F32), pltpu.VMEM((LANES, width), F32)],
        compiler_params=pltpu.CompilerParams(vmem_limit_bytes=56 * 2**20),
        name="attention_backward",
    )(u, q, k, v, do, att, qa, ka, g, lse)


def project_kernel(own_ref, all_ref, loc_ref, w_ref, b_ref, own_out, q_out, kv_out):
    step = pl.program_id(0)
    w = w_ref[...]
    b = b_ref[0:1, :]
    scale = jnp.where(step == 0, (LANES // 2) ** -0.5, 1.0)
    own_out[...] = ((dotf(own_ref[...], w, NN) + b) * scale).astype(BF16)

    @pl.when(step == 0)
    def _():
        q_out[...] = ((dotf(loc_ref[...], w, NN) + b) * scale).astype(BF16)

    @pl.when(step > 0)
    def _():
        kv_out[...] = (dotf(all_ref[...], w, NN) + b).astype(BF16)


def project(x_own, x_all, x_loc, weight, bias):
    width = x_own.shape[1]
    n_own, n_all, n_loc = x_own.shape[0], x_all.shape[0], x_loc.shape[0]
    fix = lambda c: (0, 0)
    return pl.pallas_call(
        project_kernel,
        grid=(3,),
        in_specs=[
            pl.BlockSpec((n_own, width), fix),
            pl.BlockSpec((n_all, width), fix),
            pl.BlockSpec((n_loc, width), fix),
            pl.BlockSpec((width, width), lambda c: (0, c)),
            pl.BlockSpec((8, width), lambda c: (0, c)),
        ],
        out_specs=[
            pl.BlockSpec((n_own, width), lambda c: (0, c)),
            pl.BlockSpec((n_loc, width), fix),
            pl.BlockSpec((n_all, width), lambda c: (0, jnp.maximum(c - 1, 0))),
        ],
        out_shape=[
            jax.ShapeDtypeStruct((n_own, 3 * width), BF16),
            jax.ShapeDtypeStruct((n_loc, width), BF16),
            jax.ShapeDtypeStruct((n_all, 2 * width), BF16),
        ],
        compiler_params=pltpu.CompilerParams(vmem_limit_bytes=48 * 2**20),
        name="projection",
    )(x_own, x_all, x_loc, weight, bias)


def gelu_parts(x):
    size = jnp.abs(x)
    t = 1.0 / (1.0 + (0.3275911 * 0.7071067811865476) * size)
    poly = t * (
        0.254829592
        + t * (-0.284496736 + t * (1.421413741 + t * (-1.453152027 + t * 1.061405429)))
    )
    bell = jnp.exp(-0.5 * x * x)
    tail = 0.5 * poly * bell
    phi = jnp.where(x >= 0, 1.0 - tail, tail)
    return x * phi, phi + x * bell * 0.3989422804014327


def mean_last(v):
    return jnp.sum(v, axis=-1, keepdims=True) * (1.0 / v.shape[-1])


def layer_kernel(
    chunks, tiles,
    x0_ref, x1_ref, a0_ref, a1_ref, c0_ref, c1_ref, wo_ref, up_ref, down_ref, vec_ref, ub_ref,
    h0_ref, h1_ref, ga0_ref, ga1_ref, g10_ref, g11_ref, grad_ref, sums_ref, ubg_ref,
    z_scr, r_scr, nh_scr, acc_scr, gn_scr, di_scr, act_scr, der_scr, ih_scr,
):
    step = pl.program_id(0)
    width = x0_ref.shape[1]
    own = x0_ref.shape[0]

    def pick(first_ref, second_ref, first, rows):
        if first < own:
            return first_ref[first : first + rows, :]
        return second_ref[first - own : first - own + rows, :]

    def put(first_ref, second_ref, first, rows, value):
        if first < own:
            first_ref[first : first + rows, :] = value
        else:
            second_ref[first - own : first - own + rows, :] = value

    vec = lambda i: vec_ref[i : i + 1, :]

    @pl.when(step == 0)
    def _():
        sums_ref[...] = jnp.zeros_like(sums_ref)
        for first, rows in tiles:
            y = dotf(pick(a0_ref, a1_ref, first, rows), wo_ref[...], NN) + vec(0)
            y = y + pick(x0_ref, x1_ref, first, rows).astype(F32)
            y = y - mean_last(y)
            r = lax.rsqrt(mean_last(y * y) + EPS_NORM)
            z = y * r
            z_scr[first : first + rows, :] = z
            r_scr[first : first + rows, :] = r
            nh_scr[first : first + rows, :] = (z * vec(4) + vec(2)).astype(BF16)

    for j in range(chunks):
        @pl.when(step == j)
        def _():
            cols = slice(j * width, (j + 1) * width)
            for first, rows in tiles:
                here = slice(first, first + rows)
                inner = dotf(nh_scr[here, :], up_ref[...], NN) + ub_ref[j : j + 1, :]
                act, der = gelu_parts(inner)
                act = act.astype(BF16)
                act_scr[here, cols] = act
                der_scr[here, cols] = der.astype(BF16)
                add = dotf(act, down_ref[...], NN)
                acc_scr[here, :] = add if j == 0 else acc_scr[here, :] + add

    @pl.when(step == chunks)
    def _():
        for first, rows in tiles:
            here = slice(first, first + rows)
            v = z_scr[here, :] * vec(4) + vec(2) + acc_scr[here, :] + vec(1)
            v = v - mean_last(v)
            r = lax.rsqrt(mean_last(v * v) + EPS_NORM)
            z = v * r
            put(h0_ref, h1_ref, first, rows, (z * vec(5) + vec(3)).astype(BF16))
            c = pick(c0_ref, c1_ref, first, rows).astype(F32)
            q = c * vec(5)
            gt = r * (q - mean_last(q) - z * mean_last(q * z))
            gn_scr[here, :] = gt
            di_scr[here, :] = gt.astype(BF16)
            sums_ref[3:4, :] += jnp.sum(gt, axis=0, keepdims=True)
            sums_ref[5:6, :] += jnp.sum(c, axis=0, keepdims=True)
            sums_ref[7:8, :] += jnp.sum(c * z, axis=0, keepdims=True)

    for j in range(chunks):
        cols = slice(j * width, (j + 1) * width)

        @pl.when(step == chunks + 2 * j)
        def _():
            grad_ref[...] = dotf(act_scr[:, cols], di_scr[...], TN).astype(BF16)
            total = None
            for first, rows in tiles:
                here = slice(first, first + rows)
                gi = dotf(di_scr[here, :], down_ref[...], NT) * der_scr[here, cols].astype(F32)
                part = jnp.sum(gi, axis=0, keepdims=True)
                total = part if total is None else total + part
                ih_scr[here, :] = gi.astype(BF16)
            ubg_ref[j : j + 1, :] = total

        @pl.when(step == chunks + 2 * j + 1)
        def _():
            grad_ref[...] = dotf(nh_scr[...], ih_scr[...], TN).astype(BF16)
            for first, rows in tiles:
                here = slice(first, first + rows)
                gn_scr[here, :] += dotf(ih_scr[here, :], up_ref[...], NT)

    @pl.when(step == 3 * chunks)
    def _():
        for first, rows in tiles:
            here = slice(first, first + rows)
            gn = gn_scr[here, :]
            z = z_scr[here, :]
            q = gn * vec(4)
            g1 = r_scr[here, :] * (q - mean_last(q) - z * mean_last(q * z))
            put(g10_ref, g11_ref, first, rows, g1)
            ah = g1.astype(BF16)
            di_scr[here, :] = ah
            put(ga0_ref, ga1_ref, first, rows, dotf(ah, wo_ref[...], NT).astype(BF16))
            sums_ref[2:3, :] += jnp.sum(g1, axis=0, keepdims=True)
            sums_ref[4:5, :] += jnp.sum(gn, axis=0, keepdims=True)
            sums_ref[6:7, :] += jnp.sum(gn * z, axis=0, keepdims=True)
        grad_ref[...] = (
            dotf(a0_ref[...], di_scr[0:own, :], TN) + dotf(a1_ref[...], di_scr[own:, :], TN)
        ).astype(BF16)


def layer_rest(x, att, cot, weights, wo_block, up_block, down_block, vec, up_bias):
    (x0, x1), (a0, a1), (c0, c1) = x, att, cot
    own, width = x0.shape
    extra = x1.shape[0]
    total = own + extra
    chunks = up_bias.shape[0]
    tiles = [(s, r) for s, r in tiles_of(own, 272)] + [(own + s, r) for s, r in tiles_of(extra, 272)]
    fix = lambda s: (0, 0)
    once = pl.Buffered(buffer_count=1)

    def chunk_of(s):
        return jnp.where(s < chunks, s, jnp.clip((s - chunks) // 2, 0, chunks - 1))

    def const(shape):
        return pl.BlockSpec(shape, fix, pipeline_mode=once)

    rows0, rows1 = const((own, width)), const((extra, width))
    square = (width, width)
    return pl.pallas_call(
        functools.partial(layer_kernel, chunks, tiles),
        grid=(3 * chunks + 1,),
        in_specs=[
            rows0, rows1, rows0, rows1, rows0, rows1,
            pl.BlockSpec(square, lambda s: (0, wo_block), pipeline_mode=once),
            pl.BlockSpec(square, lambda s: (0, up_block + chunk_of(s))),
            pl.BlockSpec(square, lambda s: (0, down_block + chunk_of(s))),
            const(vec.shape),
            const(up_bias.shape),
        ],
        out_specs=[
            rows0, rows1, rows0, rows1, rows0, rows1,
            pl.BlockSpec(square, lambda s: (0, jnp.maximum(s - chunks, 0))),
            const((8, width)),
            const(up_bias.shape),
        ],
        out_shape=[
            jax.ShapeDtypeStruct((own, width), BF16),
            jax.ShapeDtypeStruct((extra, width), BF16),
            jax.ShapeDtypeStruct((own, width), BF16),
            jax.ShapeDtypeStruct((extra, width), BF16),
            jax.ShapeDtypeStruct((own, width), F32),
            jax.ShapeDtypeStruct((extra, width), F32),
            jax.ShapeDtypeStruct((width, (2 * chunks + 1) * width), BF16),
            jax.ShapeDtypeStruct((8, width), F32),
            jax.ShapeDtypeStruct(up_bias.shape, F32),
        ],
        scratch_shapes=[
            pltpu.VMEM((total, width), F32),
            pltpu.VMEM((total, 1), F32),
            pltpu.VMEM((total, width), BF16),
            pltpu.VMEM((total, width), F32),
            pltpu.VMEM((total, width), F32),
            pltpu.VMEM((total, width), BF16),
            pltpu.VMEM((total, chunks * width), BF16),
            pltpu.VMEM((total, chunks * width), BF16),
            pltpu.VMEM((total, width), BF16),
        ],
        compiler_params=pltpu.CompilerParams(vmem_limit_bytes=60 * 2**20),
        name="layer_rest",
    )(x0, x1, a0, a1, c0, c1, weights, weights, weights, vec, up_bias)


def shared_input_kernel(dq_ref, dkv_ref, w_ref, part_ref, loc_ref, acc):
    step = pl.program_id(0)

    @pl.when(step == 0)
    def _():
        loc_ref[...] = dotf(dq_ref[...], w_ref[...], NT)

    @pl.when(step == 1)
    def _():
        acc[...] = dotf(dkv_ref[...], w_ref[...], NT)

    @pl.when(step == 2)
    def _():
        part_ref[...] = (acc[...] + dotf(dkv_ref[...], w_ref[...], NT)).astype(BF16)


def shared_input(dq, dkv, weight):
    n_loc, width = dq.shape
    n_all = dkv.shape[1]
    fix = lambda c: (0, 0)
    return pl.pallas_call(
        shared_input_kernel,
        grid=(3,),
        in_specs=[
            pl.BlockSpec((n_loc, width), fix),
            pl.BlockSpec((None, n_all, width), lambda c: (jnp.maximum(c - 1, 0), 0, 0)),
            pl.BlockSpec((width, width), lambda c: (0, c)),
        ],
        out_specs=[pl.BlockSpec((n_all, width), fix), pl.BlockSpec((n_loc, width), fix)],
        out_shape=[
            jax.ShapeDtypeStruct((n_all, width), BF16),
            jax.ShapeDtypeStruct((n_loc, width), F32),
        ],
        scratch_shapes=[pltpu.VMEM((n_all, width), F32)],
        compiler_params=pltpu.CompilerParams(vmem_limit_bytes=48 * 2**20),
        name="shared_input",
    )(dq, dkv, weight)


def tail_kernel(
    x0_ref, x4_ref, loc_ref, dq_ref, dkv_ref, dq4_ref, dkv4_ref, w_ref, base_ref,
    dx_ref, grad_ref, sums_ref, acc,
):
    step = pl.program_id(0)
    w = w_ref[...]

    def column_sums(row, first, second):
        sums_ref[row : row + 1, :] = jnp.sum(first.astype(F32), axis=0, keepdims=True) + jnp.sum(
            second.astype(F32), axis=0, keepdims=True
        )

    @pl.when(step == 0)
    def _():
        sums_ref[...] = jnp.zeros_like(sums_ref)
        dq, dq4 = dq_ref[...], dq4_ref[...]
        grad_ref[...] = (dotf(x0_ref[...], dq, TN) + dotf(loc_ref[...], dq4, TN)).astype(BF16)
        column_sums(0, dq, dq4)
        acc[...] = base_ref[...] + dotf(dq, w, NT)

    for c in (1, 2):
        @pl.when(step == c)
        def _():
            d, d4 = dkv_ref[...], dkv4_ref[...]
            grad_ref[...] = (dotf(x0_ref[...], d, TN) + dotf(x4_ref[...], d4, TN)).astype(BF16)
            total = acc[...] + dotf(d, w, NT)
            if c == 1:
                acc[...] = total
            else:
                column_sums(1, d, d4)
                dx_ref[...] = total.astype(BF16)


def tail(x_own, x_all, x_loc, dq, dkv, dq4, dkv4, weight, base):
    own, width = x_own.shape
    n_all, n_loc = x_all.shape[0], x_loc.shape[0]
    fix = lambda c: (0, 0)
    half = lambda c: (jnp.maximum(c - 1, 0), 0, 0)
    return pl.pallas_call(
        tail_kernel,
        grid=(3,),
        in_specs=[
            pl.BlockSpec((own, width), fix),
            pl.BlockSpec((n_all, width), fix),
            pl.BlockSpec((n_loc, width), fix),
            pl.BlockSpec((own, width), fix),
            pl.BlockSpec((None, own, width), half),
            pl.BlockSpec((n_loc, width), fix),
            pl.BlockSpec((None, n_all, width), half),
            pl.BlockSpec((width, width), lambda c: (0, c)),
            pl.BlockSpec((own, width), fix),
        ],
        out_specs=[
            pl.BlockSpec((own, width), fix),
            pl.BlockSpec((width, width), lambda c: (0, c)),
            pl.BlockSpec((8, width), fix),
        ],
        out_shape=[
            jax.ShapeDtypeStruct((own, width), BF16),
            jax.ShapeDtypeStruct((width, 3 * width), BF16),
            jax.ShapeDtypeStruct((8, width), F32),
        ],
        scratch_shapes=[pltpu.VMEM((own, width), F32)],
        compiler_params=pltpu.CompilerParams(vmem_limit_bytes=60 * 2**20),
        name="projection_backward",
    )(x_own, x_all, x_loc, dq, dkv, dq4, dkv4, weight, base)


def gate_logits(x, dirs):
    return lax.dot_general(dirs, x.astype(F32), (((0,), (1,)), ((), ())), precision=HIGHEST)


def shards(
    hidden_in,
    segment_ids,
    bucket_map,
    qkv_weight,
    out_weight,
    up_weight,
    down_weight,
    bias_cols,
    norm_gains,
    up_bias,
    rel_table,
    gate_weight,
    gate_scale,
    cotangent,
):
    row_count, block_len, width = hidden_in.shape
    heads = gate_scale.shape[0]
    pairs = heads // 2
    head_dim = width // heads
    bucket_count = rel_table.shape[0]
    cycle = lax.axis_size("blk")
    place = lax.axis_index("blk")
    frames = block_len * cycle
    shared = row_count - 1
    inner_width = up_weight.shape[1]
    chunks = inner_width // width
    local_rows = qkv_weight.shape[0]
    every = ("rows", "blk")
    assert row_count == cycle + 1

    def hop(array, s):
        return lax.ppermute(array, "blk", [(i, (i + s) % cycle) for i in range(cycle)])

    def take(array, index):
        return lax.dynamic_index_in_dim(array, index, 0, keepdims=False)

    def spread(blocks):
        out = jnp.zeros((cycle,) + blocks[0].shape, blocks[0].dtype)
        for s, block in enumerate(blocks):
            out = lax.dynamic_update_index_in_dim(out, block, (place - s) % cycle, 0)
        return out.reshape((cycle * blocks[0].shape[0],) + blocks[0].shape[1:])

    seg_rows = jnp.pad(
        segment_ids.astype(BF16), ((0, 0), (0, width - block_len))
    )
    own_blocks, shared_blocks, own_segs, shared_segs = [], [], [], []
    for s in range(cycle):
        target = (place + s) % cycle
        packed = jnp.concatenate(
            [
                take(hidden_in, target),
                hidden_in[shared],
                jnp.pad(
                    jnp.stack([take(seg_rows, target), seg_rows[shared]]), ((0, 14), (0, 0))
                ),
            ],
            axis=0,
        )
        got = packed if s == 0 else hop(packed, s)
        own_blocks.append(got[:block_len])
        shared_blocks.append(got[block_len : 2 * block_len])
        own_segs.append(got[2 * block_len, :block_len])
        shared_segs.append(got[2 * block_len + 1, :block_len])
    x_own, x_all = spread(own_blocks), spread(shared_blocks)
    x_loc = hidden_in[shared]
    seg_own, seg_all = spread(own_segs), spread(shared_segs)

    extras = jnp.concatenate(
        [bias_cols, norm_gains, up_bias.reshape(local_rows, chunks)], axis=1
    )
    qkv_pack = jnp.concatenate(
        [qkv_weight, jnp.pad(extras, ((0, 0), (0, SMALL - extras.shape[1])))], axis=1
    )
    up_turned = up_weight.reshape(local_rows, width, chunks).transpose(0, 2, 1)
    rest_pack = jnp.concatenate(
        [
            up_turned.reshape(local_rows, inner_width),
            down_weight.reshape(local_rows, inner_width),
            out_weight,
        ],
        axis=1,
    )
    qkv_full = lax.all_gather(qkv_pack, every, axis=0, tiled=True)
    rest_full = lax.all_gather(rest_pack, every, axis=0, tiled=True)
    small = qkv_full[:, 3 * width :].astype(F32).T
    biases, gains = small[0:6], small[6:8]
    up_bias_rows = small[8 : 8 + chunks]

    cot_blocks = []
    for s in range(cycle):
        part = take(cotangent, (place + s) % cycle)
        cot_blocks.append(part if s == 0 else hop(part, s))
    c_own, c_loc = spread(cot_blocks), cotangent[shared]

    first_dir = jnp.sum(gate_weight[:, :4], axis=1)
    second_dir = jnp.sum(gate_weight[:, 4:], axis=1)
    picks = jnp.repeat(jnp.eye(heads, dtype=F32), head_dim, axis=0)
    dirs = jnp.concatenate(
        [picks * jnp.tile(first_dir, heads)[:, None], picks * jnp.tile(second_dir, heads)[:, None]],
        axis=1,
    )

    def gates(x):
        logits = jax.nn.sigmoid(gate_logits(x, dirs))
        a, b = logits[:heads], logits[heads:]
        return a, b, a * (b * gate_scale[:, None] - 1.0) + 2.0

    a_own, b_own, g_own = gates(x_own)
    a_loc, b_loc, g_loc = gates(x_loc)

    shift = -(-frames // LANES)
    span = 2 * frames - 1
    lead = shift * LANES - (frames - 1)
    table_width = 2 * shift * LANES
    turned = bucket_map[::-1]
    slots = jnp.pad(turned, (lead, table_width - lead - span), constant_values=-1)
    slots_loc = lax.dynamic_slice_in_dim(
        jnp.pad(slots, (0, frames), constant_values=-1), place * block_len, table_width
    )
    bucket_ids = jnp.arange(bucket_count, dtype=jnp.int32)

    def table_rows(slot):
        hot = (bucket_ids[:, None] == slot[None, :]).astype(F32)
        rows = lax.dot_general(rel_table, hot, (((0,), (0,)), ((), ())), precision=HIGHEST)
        return hot, rows.reshape(pairs, 2, table_width)

    hot_own, u_own = table_rows(slots)
    hot_loc, u_loc = table_rows(slots_loc)

    lane = jnp.arange(LANES) % (LANES // 2)

    def penalty(seg):
        seg = seg.astype(jnp.int32)
        return jnp.where((lane < 4)[None, :] & (lane[None, :] != seg[:, None]), -1e30, 0.0).astype(BF16)

    def member(seg):
        return (lane[None, :] == seg.astype(jnp.int32)[:, None]).astype(BF16)

    qa_own, ka_own = penalty(seg_own), member(seg_own)
    qa_loc, ka_all = penalty(segment_ids[shared]), member(seg_all)

    zeros = jnp.zeros((width,), F32)
    proj_bias = jnp.broadcast_to(
        jnp.concatenate([biases[0], zeros, biases[1]])[None, :], (8, 3 * width)
    )
    qkv_own, q_loc, kv_all = project(x_own, x_all, x_loc, qkv_full, proj_bias)
    pair_rows = lambda v: v.reshape(pairs, 2, -1)
    own_cols = (0, pairs, 2 * pairs)
    loc_cols = (0, 0, pairs)
    att_own, atth_own, lse_own = attend_forward(
        u_own, qkv_own, qkv_own, qkv_own, qa_own, ka_own, pair_rows(g_own), own_cols, frames, True
    )
    att_loc, atth_loc, lse_loc = attend_forward(
        u_loc, q_loc, kv_all, kv_all, qa_loc, ka_all, pair_rows(g_loc), loc_cols, frames, False
    )
    vec = jnp.stack(
        [biases[2], biases[3], biases[4], biases[5], gains[0], gains[1], zeros, zeros]
    )
    h_own, h_loc, ga_own, ga_loc, g1_own, g1_loc, rest_grad, sums, up_bias_grad = layer_rest(
        (x_own, x_loc), (atth_own, atth_loc), (c_own, c_loc), rest_full,
        2 * chunks, 0, chunks, vec, up_bias_rows,
    )

    def send_home(own, mine):
        blocks = own.reshape(cycle, block_len, width)
        out = jnp.zeros((row_count, block_len, width), own.dtype)
        out = lax.dynamic_update_index_in_dim(out, mine, shared, 0)
        for s in range(cycle):
            part = take(blocks, (place + s) % cycle)
            got = part if s == 0 else hop(part, s)
            out = lax.dynamic_update_index_in_dim(out, got, (place - s) % cycle, 0)
        return out

    hidden_out = send_home(h_own, h_loc)
    rest_sum = lax.psum_scatter(rest_grad, every, scatter_dimension=0, tiled=True)

    dq_loc, dkv_all, gate_loc, diag_loc = attend_backward(
        u_loc, q_loc, kv_all, kv_all, ga_loc, att_loc, qa_loc, ka_all, pair_rows(g_loc), lse_loc, loc_cols
    )
    part_all, dx_loc = shared_input(dq_loc, dkv_all, qkv_full)
    part_blocks = part_all.reshape(cycle, block_len, width)
    for s in range(cycle):
        part = take(part_blocks, (place + s) % cycle)
        dx_loc = dx_loc + (part if s == 0 else hop(part, s)).astype(F32)

    dq_own, dkv_own, gate_own, diag_own = attend_backward(
        u_own, qkv_own, qkv_own, qkv_own, ga_own, att_own, qa_own, ka_own, pair_rows(g_own), lse_own, own_cols
    )

    def gate_back(grad, a, b, x):
        grad = grad.reshape(heads, -1)
        c = gate_scale[:, None]
        da = grad * (b * c - 1.0) * a * (1.0 - a)
        db = grad * a * c * b * (1.0 - b)
        d = jnp.concatenate([da, db], axis=0)
        dx = lax.dot_general(d, dirs, (((0,), (1,)), ((), ())), precision=HIGHEST)
        dw = jnp.dot(d, x.astype(F32), precision=HIGHEST)
        return dx, dw, jnp.sum(grad * a * b, axis=1)

    gx_own, gw_own, gs_own = gate_back(gate_own, a_own, b_own, x_own)
    gx_loc, gw_loc, gs_loc = gate_back(gate_loc, a_loc, b_loc, x_loc)
    dx_own, qkv_grad, tail_sums = tail(
        x_own, x_all, x_loc, dq_own, dkv_own, dq_loc, dkv_all, qkv_full, g1_own + gx_own
    )
    grad_input = send_home(dx_own, (dx_loc + g1_loc + gx_loc).astype(BF16))

    dw = (gw_own + gw_loc).reshape(2, heads, heads, head_dim)
    dw = jnp.einsum("sggd->sd", dw)
    gate_weight_grad = jnp.broadcast_to(dw[:, None, :], (2, 4, head_dim)).reshape(8, head_dim).T
    diag = lambda hot, d: jnp.dot(hot, d.reshape(heads, -1).T, precision=HIGHEST)
    table_grad = diag(hot_own, diag_own) + diag(hot_loc, diag_loc)
    table_sum, gate_weight_sum, gate_scale_sum = lax.psum(
        (table_grad, gate_weight_grad, gs_own + gs_loc), every
    )

    small_grad = jnp.concatenate(
        [tail_sums[0:2], sums[2:8], up_bias_grad], axis=0
    ).T
    small_grad = jnp.pad(small_grad, ((0, 0), (0, SMALL - small_grad.shape[1]))).astype(BF16)
    last_sum = lax.psum_scatter(
        jnp.concatenate([qkv_grad, small_grad], axis=1), every, scatter_dimension=0, tiled=True
    ).astype(F32)
    rest_sum = rest_sum.astype(F32)
    up_sum = rest_sum.reshape(local_rows, 2 * chunks + 1, width)
    grad_down = up_sum[:, 0 : 2 * chunks : 2].reshape(local_rows * chunks, width)
    grad_up = up_sum[:, 1 : 2 * chunks : 2].transpose(0, 2, 1).reshape(local_rows, inner_width)
    grad_out = up_sum[:, 2 * chunks]
    extra_sum = last_sum[:, 3 * width :]
    return (
        hidden_out,
        grad_input,
        last_sum[:, : 3 * width],
        grad_out,
        grad_up,
        grad_down,
        extra_sum[:, 0:6],
        extra_sum[:, 6:8],
        extra_sum[:, 8 : 8 + chunks].reshape(-1),
        table_sum,
        gate_weight_sum,
        gate_scale_sum,
    )


def solution(mesh):
    placed = (
        P("rows", "blk", None),
        P("rows", "blk"),
        P(),
        P(("rows", "blk"), None),
        P(("rows", "blk"), None),
        P(("rows", "blk"), None),
        P(("rows", "blk"), None),
        P(("rows", "blk"), None),
        P(("rows", "blk"), None),
        P(("rows", "blk")),
        P(),
        P(),
        P(),
        P("rows", "blk", None),
    )
    return jax.shard_map(
        shards,
        mesh=mesh,
        in_specs=placed,
        out_specs=(
            P("rows", "blk", None),
            P("rows", "blk", None),
            P(("rows", "blk"), None),
            P(("rows", "blk"), None),
            P(("rows", "blk"), None),
            P(("rows", "blk"), None),
            P(("rows", "blk"), None),
            P(("rows", "blk"), None),
            P(("rows", "blk")),
            P(),
            P(),
            P(),
        ),
        check_vma=False,
    )
```

time: 1470 us -> 1030 us (0.70); the launches traced: 1450 us -> 1030 us
  Pallas kernels: 0 us -> 578 us
  local copies, waits for them, and re-layouts: 442 us -> 59.9 us
  matrix products: 281 us -> 10.9 us
  waiting for transfers between devices: 414 us -> 219 us
  blocking collectives: 241 us -> 66.5 us
  starting transfers between devices: 0.48 us -> 59.7 us
  other arithmetic: 55.3 us -> 15.5 us
    pallas_call x0 -> x8, Pallas kernels: none -> 578 us  [the longest x1 468 us: layer_rest(): pl.pallas_call(functools.partial(layer_kernel, chunks, tiles), grid=(3 *...]
    dot_general x24 -> x10, matrix products: 281 us -> 10.9 us  [the longest x2 2.9 us: gate_back(): dx = lax.dot_general(d, dirs, (((0,), (1,)), ((), ())), precision=HIGHEST)]
    unnamed x15 -> x5, waiting for transfers between devices: 201 us -> 0.54 us
    rev x2 -> x0, local copies, waits for them, and re-layouts: 163 us -> none  [the longest x1 81.6 us: toeplitz_rows(): return shaped[:, ::-1, :col_total]]
    all_gather x3 -> x0, blocking collectives: 155 us -> none  [the longest x1 72.5 us: shards(): lax.all_gather(norm_gains, ('rows', 'blk'), axis=0, tiled=True)]
    reshape x12 -> x15, local copies, waits for them, and re-layouts: 104 us -> 8.24 us  [the longest x2 1.41 us: shards(): d.reshape(heads, -1)]
    unnamed x2 -> x0, blocking collectives: 86.5 us -> none
    psum x0 -> x1, blocking collectives: none -> 66.5 us  [shards(): lax.psum((table_grad, gate_weight_grad, gs_own + gs_loc), every)]
  transfers between devices with their start and end apart: 12 -> 19, of which waited for: 5 -> 9; matrix products, arithmetic and copies ran while one was open for 46% -> 5% of each run, Pallas kernels for 0% -> 4%
where the time goes in v1:
time: 1030 us
  Pallas kernels  578 us (56%)
  waiting for transfers between devices  219 us (21%)
  blocking collectives  66.5 us (6%)
  local copies, waits for them, and re-layouts  59.9 us (6%)
  starting transfers between devices  59.7 us (6%)
  other arithmetic  15.5 us (2%)
  between operations  15.2 us (1%)
  matrix products  10.9 us (1%)
    pallas_call x1, Pallas kernels, layer_rest(): pl.pallas_call(functools.partial(layer_kernel, chunks, tiles), grid=(3 *...  468 us
    reduce_scatter x1, waiting for transfers between devices, shards(): lax.psum_scatter(rest_grad, every, scatter_dimension=0, tiled=True)  117 us
    psum x1, blocking collectives, shards(): lax.psum((table_grad, gate_weight_grad, gs_own + gs_loc), every)  66.5 us
    ppermute x15, starting transfers between devices, hop(): lax.ppermute(array, 'blk', [(i, (i + s) % cycle) for i in range(cycle)])  59.5 us
    ppermute x15, waiting for transfers between devices, hop(): lax.ppermute(array, 'blk', [(i, (i + s) % cycle) for i in range(cycle)])  58.1 us
    pallas_call x2, Pallas kernels, attend_backward(): pl.pallas_call(backward_kernel, grid=(pairs,), in_specs=[wide_spec, pl.Bl...  54.3 us
    all_gather x1, waiting for transfers between devices, shards(): rest_full = lax.all_gather(rest_pack, every, axis=0, tiled=True)  39 us
    pallas_call x2, Pallas kernels, attend_forward(): pl.pallas_call(functools.partial(forward_kernel, tile, flip), grid=(pairs...  26.8 us
  transfers between devices with their start and end apart: 19, of which 9 were waited for; matrix products, arithmetic and copies ran while one was open for 5% of the time, Pallas kernels for 4%

profile of v1, /device:TPU:0, one launch (start us, length us, event | category | flops | bytes accessed | tf_op | source)
XLA Modules:
  0.0 1025.0 jit_solution(2427064876052990742)
XLA Ops:
  9.6 1.6 pad_maximum_fusion.4
  12.3 1.3 copy.53
  16.6 4.0 collective-permute-start.4
  20.6 1.6 collective-permute-start.3
  22.2 2.2 collective-permute-start.5
  24.8 1.4 fusion.24
  26.2 1.2 collective-permute-start.1
  28.1 1.4 fusion.21
  34.0 5.6 collective-permute-done.3
  39.6 39.1 %collective-permute-start = (bf16[416,768]{1,0:T(8,128)(2,1)}, bf16[416,768]{1,0:T(8,128)(2,1)S(1)}, u32[]{:S(2)}, u32[]{:S(2)}) collective-permute-start(bf16[416,768]{1,0:T(8,128)(2,1)} %get-tuple-element.152), channel_id=1, source_target_pairs={{0,1},{1,2},{2,3},{3,0},{4,5},{5,6},{6,7},{7,4},{8,9},{9,10},{10,1... | collective-permute-start | bytes 1916936 | tf_op jit(solution)/shard_map/ppermute | solution.py:593
  78.7 1.7 bitcast_dynamic-update-slice_fusion.8
  80.4 1.7 bitcast_dynamic-update-slice_fusion.7
  82.1 1.7 bitcast_dynamic-update-slice_fusion.6
  83.8 13.2 %collective-permute-done = bf16[416,768]{1,0:T(8,128)(2,1)S(1)} collective-permute-done((bf16[416,768]{1,0:T(8,128)(2,1)}, bf16[416,768]{1,0:T(8,128)(2,1)S(1)}, u32[]{:S(2)}, u32[]{:S(2)}) %collective-permute-start) | collective-permute-done | bytes 639008 | tf_op jit(solution)/shard_map/ppermute | solution.py:593
  97.9 12.5 %collective-permute-done.1 = bf16[416,768]{1,0:T(8,128)(2,1)} collective-permute-done((bf16[416,768]{1,0:T(8,128)(2,1)}, bf16[416,768]{1,0:T(8,128)(2,1)}, u32[]{:S(2)}, u32[]{:S(2)}) %collective-permute-start.1) | collective-permute-done | bytes 639008 | tf_op jit(solution)/shard_map/ppermute | solution.py:593
  120.1 4.6 all-gather.3.cloned.1.call-done.w_ref
  127.4 1.8 copy.63
  129.2 1.7 copy.56.ub_ref
  130.9 1.3 stack.21.clone.vec_ref
  132.3 1.5 slice_reduce_fusion.1
  133.9 8.7 projection.1
  142.6 18.9 %attention_forward.2 = (f32[800,768]{1,0:T(8,128)S(1)}, bf16[800,768]{1,0:T(8,128)(2,1)S(1)}, f32[6,2,800]{2,1,0:T(2,128)S(1)}) custom-call(f32[6,2,1792]{2,1,0:T(2,128)S(1)} %reshape.147.u_ref, bf16[800,2304]{1,0:T(8,128)(2,1)} %get-tuple-element.43.q_ref.k_ref.v_ref, bf16[800,2304]{1,0:T(8,128)(2,1)} %get-tuple-element.43.q_ref.k_ref.v_ref, ...), custom_call_target="tpu_custom_call" | custom-call | tf_op jit(solution)/shard_map/attention_forward/pallas_call | solution.py:93
  161.6 1.4 copy-done.8
  164.7 7.9 attention_forward.3
  174.7 39.0 %all-gather.5.cloned.1.call-done.wo_ref.up_ref.down_ref = bf16[768,6912]{1,0:T(8,128)(2,1)} async-done(((bf16[24,6912]{1,0:T(8,128)(2,1)}), bf16[768,6912]{1,0:T(8,128)(2,1)}) %all-gather.5.cloned.1.call-update) | async-done | bytes 10616848 | tf_op jit(solution)/shard_map/all_gather | solution.py:645
  213.7 467.6 %layer_rest.1 = (bf16[800,768]{1,0:T(8,128)(2,1)}, bf16[200,768]{1,0:T(8,128)(2,1)}, bf16[800,768]{1,0:T(8,128)(2,1)}, bf16[200,768]{1,0:T(8,128)(2,1)}, f32[800...) custom-call(bf16[800,768]{1,0:T(8,128)(2,1)} %bitcast.122, ...), custom_call_target="tpu_custom_call" | custom-call | tf_op jit(solution)/shard_map/layer_rest/pallas_call | solution.py:406
  682.8 37.7 %attention_backward.3 = (bf16[800,768]{1,0:T(8,128)(2,1)}, bf16[2,800,768]{2,1,0:T(8,128)(2,1)}, f32[6,2,800]{2,1,0:T(2,128)}, f32[6,2,1792]{2,1,0:T(2,128)}) custom-call(f32[6,2,1792]{2,1,0:T(2,128)} %copy-done.15, bf16[800,2304]{1,0:T(8,128)(2,1)} %get-tuple-element.43.q_ref.k_ref.v_ref, bf16[800,2304]{1,0:T(8,128)(2,1)} %get-tuple-element.43.q_ref.k_ref.v_ref, ...), custom_call_target="tpu_custom_call" | custom-call | tf_op jit(solution)/shard_map/attention_backward/pallas_call | solution.py:183
  721.6 2.2 fusion.38
  723.8 1.8 add.322.base_ref
  725.6 16.6 %attention_backward.2 = (bf16[200,768]{1,0:T(8,128)(2,1)}, bf16[2,800,768]{2,1,0:T(8,128)(2,1)}, f32[6,2,200]{2,1,0:T(2,128)}, f32[6,2,1792]{2,1,0:T(2,128)}) custom-call(f32[6,2,1792]{2,1,0:T(2,128)} %copy-done.16, bf16[200,768]{1,0:T(8,128)(2,1)} %copy-done.13, bf16[800,1536]{1,0:T(8,128)(2,1)} %copy-done.4, bf16[800,1536]{1,0:T(8,128)(2,1)} %copy-done.4, ...), custom_call_target="tpu_custom_call" | custom-call | tf_op jit(solution)/shard_map/attention_backward/pallas_call | solution.py:183
  742.2 16.1 %projection_backward.1 = (bf16[800,768]{1,0:T(8,128)(2,1)}, bf16[768,2304]{1,0:T(8,128)(2,1)}, f32[8,768]{1,0:T(8,128)}) custom-call(bf16[800,768]{1,0:T(8,128)(2,1)} %bitcast.123, bf16[800,768]{1,0:T(8,128)(2,1)} %bitcast.126, bf16[200,768]{1,0:T(8,128)(2,1)} %copy-done.7, bf16[800,768]{1,0:T(8,128)(2,1)} %get-tuple-element.62.dq_ref, ...), custom_call_target="tpu_custom_call" | custom-call | tf_op jit(solution)/shard_map/projection_backward/pallas_call | solution.py:527
  759.3 4.1 fusion.1
  765.9 1.2 fusion.39
  769.4 1.8 collective-permute-start.8
  772.3 4.5 shared_input.1
  778.8 2.8 collective-permute-start.11
  784.0 66.5 %all-reduce.12 = (f32[320,12]{0,1:T(8,128)}, f32[64,8]{0,1:T(8,128)}, f32[12]{0:T(128)}) all-reduce(f32[320,12]{0,1:T(8,128)S(1)} %fusion.18, f32[64,8]{0,1:T(8,128)S(1)} %bitcast.140, f32[12]{0:T(128)S(1)} %add.325), channel_id=1, replica_groups=mesh['rows'=8,'blk'=4] {'rows','blk'}, use_global_device_ids=true, to_apply=%region_4.5 | all-reduce | flops 4364 | bytes 34912 | tf_op jit(solution)/shard_map/psum | solution.py:773
  851.3 1.4 fusion.31
  852.8 1.2 copy-done.31
  854.1 3.9 collective-permute-start.14
  858.0 6.7 collective-permute-done.6
  866.1 1.7 bitcast_dynamic-update-slice_fusion.4
  867.8 1.7 bitcast_dynamic-update-slice_fusion.3
  869.5 13.7 %collective-permute-done.12 = bf16[200,768]{1,0:T(8,128)(2,1)S(1)} collective-permute-done((bf16[200,768]{1,0:T(8,128)(2,1)S(1)}, bf16[200,768]{1,0:T(8,128)(2,1)S(1)}, u32[]{:S(2)}, u32[]{:S(2)}) %collective-permute-start.12) | collective-permute-done | bytes 307232 | tf_op jit(solution)/shard_map/ppermute | solution.py:593
  883.2 6.3 collective-permute-done.13
  893.8 1.6 slice.211
  895.4 117.3 %reduce-scatter.5.cloned.1.call-done = bf16[24,6912]{1,0:T(8,128)(2,1)} async-done(((bf16[768,6912]{1,0:T(8,128)(2,1)}), bf16[24,6912]{1,0:T(8,128)(2,1)}) %reduce-scatter.5.cloned.1.call-update) | async-done | bytes 331792 | tf_op jit(solution)/shard_map/reduce_scatter | solution.py:736
  1017.1 1.2 copy.59
  (257 shorter events, 53.2 us)
Async XLA Ops:
  7.2 23.1 %copy-start = (f32[320,12]{0,1:T(8,128)S(1)}, f32[320,12]{0,1:T(8,128)}, u32[]{:S(2)}) copy-start(f32[320,12]{0,1:T(8,128)} %param.24) | copy-start | bytes 46084
  7.2 6.9 copy-start.48
  7.2 117.4 %all-gather.3.cloned.1.call-start = ((), (), s32[]{:S(2)}) async-start(), calls=%async_computation.2 | async-start | bytes 3852288 | tf_op jit(solution)/shard_map/all_gather | solution.py:644
  11.2 202.5 %all-gather.5.cloned.1.call-start = ((), (), s32[]{:S(2)}) async-start(), calls=%async_computation.3 | async-start | bytes 10948608 | tf_op jit(solution)/shard_map/all_gather | solution.py:645
  14.9 874.7 %reduce-scatter.7.cloned.1.call-start = ((), (), s32[]{:S(2)}) async-start(), calls=%async_computation.5 | async-start | bytes 3852288
  15.6 8.9 copy-start.52
  15.6 9.0 copy-start.27
  16.6 8.1 copy-start.25
  16.6 63.8 %collective-permute-start.4 = (bf16[200,768]{1,0:T(8,128)(2,1)}, bf16[200,768]{1,0:T(8,128)(2,1)}, u32[]{:S(2)}, u32[]{:S(2)}) collective-permute-start(bf16[200,768]{1,0:T(8,128)(2,1)} %get-tuple-element.118), channel_id=1, source_target_pairs={{0,2},{1,3},{2,0},{3,1},{4,6},{5,7},{6,4},{7,5},{8,10},{9,11},{10,... | collective-permute-start | bytes 921608 | tf_op jit(solution)/shard_map/ppermute | solution.py:593
  20.6 18.9 %collective-permute-start.3 = (bf16[200,768]{1,0:T(8,128)(2,1)}, bf16[200,768]{1,0:T(8,128)(2,1)}, u32[]{:S(2)}, u32[]{:S(2)}) collective-permute-start(bf16[200,768]{1,0:T(8,128)(2,1)} %get-tuple-element.119), channel_id=1, source_target_pairs={{0,1},{1,2},{2,3},{3,0},{4,5},{5,6},{6,7},{7,4},{8,9},{9,10},{10,1... | collective-permute-start | bytes 921608 | tf_op jit(solution)/shard_map/ppermute | solution.py:593
  22.2 59.9 %collective-permute-start.5 = (bf16[200,768]{1,0:T(8,128)(2,1)S(1)}, bf16[200,768]{1,0:T(8,128)(2,1)}, u32[]{:S(2)}, u32[]{:S(2)}) collective-permute-start(bf16[200,768]{1,0:T(8,128)(2,1)S(1)} %get-tuple-element.121), channel_id=1, source_target_pairs={{0,3},{1,0},{2,1},{3,2},{4,7},{5,4},{6,5},{7,6},{8,11},{9,8},{10,9... | collective-permute-start | bytes 921608 | tf_op jit(solution)/shard_map/ppermute | solution.py:593
  24.7 109.1 %copy-start.7 = (bf16[200,768]{1,0:T(8,128)(2,1)}, bf16[200,768]{1,0:T(8,128)(2,1)S(1)}, u32[]{:S(2)}) copy-start(bf16[200,768]{1,0:T(8,128)(2,1)S(1)} %get-tuple-element.123.loc_ref.x1_ref) | copy-start | bytes 921604
  26.2 85.0 %collective-permute-start.2 = (bf16[416,768]{1,0:T(8,128)(2,1)}, bf16[416,768]{1,0:T(8,128)(2,1)}, u32[]{:S(2)}, u32[]{:S(2)}) collective-permute-start(bf16[416,768]{1,0:T(8,128)(2,1)} %get-tuple-element.150), channel_id=1, source_target_pairs={{0,3},{1,0},{2,1},{3,2},{4,7},{5,4},{6,5},{7,6},{8,11},{9,8},{10,9... | collective-permute-start | bytes 1916936 | tf_op jit(solution)/shard_map/ppermute | solution.py:593
  26.2 84.2 %collective-permute-start.1 = (bf16[416,768]{1,0:T(8,128)(2,1)}, bf16[416,768]{1,0:T(8,128)(2,1)}, u32[]{:S(2)}, u32[]{:S(2)}) collective-permute-start(bf16[416,768]{1,0:T(8,128)(2,1)} %get-tuple-element.151), channel_id=1, source_target_pairs={{0,2},{1,3},{2,0},{3,1},{4,6},{5,7},{6,4},{7,5},{8,10},{9,11},{10,... | collective-permute-start | bytes 1916936 | tf_op jit(solution)/shard_map/ppermute | solution.py:593
  28.1 88.3 %copy-start.35 = (f32[768,12]{0,1:T(8,128)}, f32[768,12]{0,1:T(8,128)S(1)}, u32[]{:S(2)}) copy-start(f32[768,12]{0,1:T(8,128)S(1)} %get-tuple-element.156) | copy-start | bytes 110596
  28.1 88.3 %copy-start.37 = (f32[768,12]{0,1:T(8,128)}, f32[768,12]{0,1:T(8,128)S(1)}, u32[]{:S(2)}) copy-start(f32[768,12]{0,1:T(8,128)S(1)} %get-tuple-element.157) | copy-start | bytes 110596
  31.2 133.5 %copy-start.16 = (f32[6,2,1792]{2,1,0:T(2,128)}, f32[6,2,1792]{2,1,0:T(2,128)S(1)}, u32[]{:S(2)}) copy-start(f32[6,2,1792]{2,1,0:T(2,128)S(1)} %reshape.152.u_ref) | copy-start | bytes 258052
  32.0 110.6 %copy-start.15 = (f32[6,2,1792]{2,1,0:T(2,128)}, f32[6,2,1792]{2,1,0:T(2,128)S(1)}, u32[]{:S(2)}) copy-start(f32[6,2,1792]{2,1,0:T(2,128)S(1)} %reshape.147.u_ref) | copy-start | bytes 258052
  32.2 86.6 %copy-start.58 = (s32[128]{0:T(128)}, s32[128]{0:T(128)S(1)}, u32[]{:S(2)}) copy-start(s32[128]{0:T(128)S(1)} %and_select_fusion) | copy-start | bytes 1540
  39.6 57.5 %collective-permute-start = (bf16[416,768]{1,0:T(8,128)(2,1)}, bf16[416,768]{1,0:T(8,128)(2,1)S(1)}, u32[]{:S(2)}, u32[]{:S(2)}) collective-permute-start(bf16[416,768]{1,0:T(8,128)(2,1)} %get-tuple-element.152), channel_id=1, source_target_pairs={{0,1},{1,2},{2,3},{3,0},{4,5},{5,6},{6,7},{7,4},{8,9},{9,10},{10,1... | collective-permute-start | bytes 1916936 | tf_op jit(solution)/shard_map/ppermute | solution.py:593
  116.4 17.5 %copy-start.2 = (bf16[4,200,768]{2,1,0:T(8,128)(2,1)}, bf16[4,200,768]{2,1,0:T(8,128)(2,1)S(1)}, u32[]{:S(2)}) copy-start(bf16[4,200,768]{2,1,0:T(8,128)(2,1)S(1)} %get-tuple-element.145) | copy-start | bytes 3686404
  116.4 17.5 %copy-start.5 = (bf16[4,200,768]{2,1,0:T(8,128)(2,1)}, bf16[4,200,768]{2,1,0:T(8,128)(2,1)S(1)}, u32[]{:S(2)}) copy-start(bf16[4,200,768]{2,1,0:T(8,128)(2,1)S(1)} %get-tuple-element.144) | copy-start | bytes 3686404
  119.0 23.6 %copy-start.9 = (bf16[800,128]{1,0:T(8,128)(2,1)}, bf16[800,128]{1,0:T(8,128)(2,1)S(1)}, u32[]{:S(2)}) copy-start(bf16[800,128]{1,0:T(8,128)(2,1)S(1)} %select_convert_fusion.qa_ref) | copy-start | bytes 614404
  120.0 22.5 %copy-start.10 = (bf16[800,128]{1,0:T(8,128)(2,1)}, bf16[800,128]{1,0:T(8,128)(2,1)S(1)}, u32[]{:S(2)}) copy-start(bf16[800,128]{1,0:T(8,128)(2,1)S(1)} %get-tuple-element.171.ka_ref) | copy-start | bytes 614404
  120.1 44.6 %copy-start.11 = (bf16[800,128]{1,0:T(8,128)(2,1)}, bf16[800,128]{1,0:T(8,128)(2,1)S(1)}, u32[]{:S(2)}) copy-start(bf16[800,128]{1,0:T(8,128)(2,1)S(1)} %get-tuple-element.170.ka_ref) | copy-start | bytes 614404
  133.9 8.7 copy-start.19
  142.6 22.1 %copy-start.4 = (bf16[800,1536]{1,0:T(8,128)(2,1)}, bf16[800,1536]{1,0:T(8,128)(2,1)S(1)}, u32[]{:S(2)}) copy-start(bf16[800,1536]{1,0:T(8,128)(2,1)S(1)} %get-tuple-element.46.k_ref.v_ref) | copy-start | bytes 7372804
  142.6 22.1 %copy-start.13 = (bf16[200,768]{1,0:T(8,128)(2,1)}, bf16[200,768]{1,0:T(8,128)(2,1)S(1)}, u32[]{:S(2)}) copy-start(bf16[200,768]{1,0:T(8,128)(2,1)S(1)} %get-tuple-element.45.q_ref) | copy-start | bytes 921604
  142.6 22.0 %copy-start.18 = (bf16[200,128]{1,0:T(8,128)(2,1)S(1)}, bf16[200,128]{1,0:T(8,128)(2,1)}, u32[]{:S(2)}) copy-start(bf16[200,128]{1,0:T(8,128)(2,1)} %select_convert_fusion.1.qa_ref) | copy-start | bytes 153604
  142.6 22.0 %copy-start.21 = (f32[6,2,200]{2,1,0:T(2,128)S(1)}, f32[6,2,200]{2,1,0:T(2,128)}, u32[]{:S(2)}) copy-start(f32[6,2,200]{2,1,0:T(2,128)} %reshape.153.g_ref) | copy-start | bytes 28804
  682.8 38.7 %copy-start.34 = (f32[24,800]{1,0:T(8,128)S(1)}, f32[24,800]{1,0:T(8,128)}, u32[]{:S(2)}) copy-start(f32[24,800]{1,0:T(8,128)} %copy-done.33) | copy-start | bytes 230404
  682.8 38.7 %copy-start.54 = (f32[12]{0:T(128)S(1)}, f32[12]{0:T(128)}, u32[]{:S(2)}) copy-start(f32[12]{0:T(128)} %param.26) | copy-start | bytes 148
  682.8 38.8 %copy-start.36 = (f32[768,12]{0,1:T(8,128)S(1)}, f32[768,12]{0,1:T(8,128)}, u32[]{:S(2)}) copy-start(f32[768,12]{0,1:T(8,128)} %copy-done.35) | copy-start | bytes 110596
  682.8 38.8 %copy-start.38 = (f32[768,12]{0,1:T(8,128)S(1)}, f32[768,12]{0,1:T(8,128)}, u32[]{:S(2)}) copy-start(f32[768,12]{0,1:T(8,128)} %copy-done.37) | copy-start | bytes 110596
  763.4 249.3 %reduce-scatter.5.cloned.1.call-start = ((), (), s32[]{:S(2)}) async-start(), calls=%async_computation.4 | async-start | bytes 10948608 | tf_op jit(solution)/shard_map/reduce_scatter | solution.py:736
  769.4 98.4 %collective-permute-start.8 = (bf16[200,768]{1,0:T(8,128)(2,1)S(1)}, bf16[200,768]{1,0:T(8,128)(2,1)}, u32[]{:S(2)}, u32[]{:S(2)}) collective-permute-start(bf16[200,768]{1,0:T(8,128)(2,1)S(1)} %get-tuple-element.134), channel_id=1, source_target_pairs={{0,3},{1,0},{2,1},{3,2},{4,7},{5,4},{6,5},{7,6},{8,11},{9,8},{10,9... | collective-permute-start | bytes 921608 | tf_op jit(solution)/shard_map/ppermute | solution.py:593
  771.2 94.9 %collective-permute-start.7 = (bf16[200,768]{1,0:T(8,128)(2,1)}, bf16[200,768]{1,0:T(8,128)(2,1)}, u32[]{:S(2)}, u32[]{:S(2)}) collective-permute-start(bf16[200,768]{1,0:T(8,128)(2,1)} %get-tuple-element.135), channel_id=1, source_target_pairs={{0,2},{1,3},{2,0},{3,1},{4,6},{5,7},{6,4},{7,5},{8,10},{9,11},{10,... | collective-permute-start | bytes 921608 | tf_op jit(solution)/shard_map/ppermute | solution.py:593
  776.8 5.9 copy-start.45
  776.9 5.9 copy-start.50
  777.8 73.5 %copy-start.39 = (f32[200,768]{1,0:T(8,128)S(1)}, f32[200,768]{1,0:T(8,128)}, u32[]{:S(2)}) copy-start(f32[200,768]{1,0:T(8,128)} %get-tuple-element.57) | copy-start | bytes 1843204
  777.8 73.4 %collective-permute-start.9 = (bf16[200,768]{1,0:T(8,128)(2,1)}, bf16[200,768]{1,0:T(8,128)(2,1)}, u32[]{:S(2)}, u32[]{:S(2)}) collective-permute-start(bf16[200,768]{1,0:T(8,128)(2,1)} %get-tuple-element.131), channel_id=1, source_target_pairs={{0,1},{1,2},{2,3},{3,0},{4,5},{5,6},{6,7},{7,4},{8,9},{9,10},{10,1... | collective-permute-start | bytes 921608 | tf_op jit(solution)/shard_map/ppermute | solution.py:593
  778.8 72.5 %collective-permute-start.11 = (bf16[200,768]{1,0:T(8,128)(2,1)}, bf16[200,768]{1,0:T(8,128)(2,1)}, u32[]{:S(2)}, u32[]{:S(2)}) collective-permute-start(bf16[200,768]{1,0:T(8,128)(2,1)} %get-tuple-element.132), channel_id=1, source_target_pairs={{0,3},{1,0},{2,1},{3,2},{4,7},{5,4},{6,5},{7,6},{8,11},{9,8},{10,9... | collective-permute-start | bytes 921608 | tf_op jit(solution)/shard_map/ppermute | solution.py:593
  781.6 69.6 %collective-permute-start.10 = (bf16[200,768]{1,0:T(8,128)(2,1)S(1)}, bf16[200,768]{1,0:T(8,128)(2,1)}, u32[]{:S(2)}, u32[]{:S(2)}) collective-permute-start(bf16[200,768]{1,0:T(8,128)(2,1)S(1)} %get-tuple-element.133), channel_id=1, source_target_pairs={{0,2},{1,3},{2,0},{3,1},{4,6},{5,7},{6,4},{7,5},{8,10},{9,11},{10,... | collective-permute-start | bytes 921608 | tf_op jit(solution)/shard_map/ppermute | solution.py:593
  851.2 13.5 %collective-permute-start.6 = (bf16[200,768]{1,0:T(8,128)(2,1)}, bf16[200,768]{1,0:T(8,128)(2,1)S(1)}, u32[]{:S(2)}, u32[]{:S(2)}) collective-permute-start(bf16[200,768]{1,0:T(8,128)(2,1)} %get-tuple-element.136), channel_id=1, source_target_pairs={{0,1},{1,2},{2,3},{3,0},{4,5},{5,6},{6,7},{7,4},{8,9},{9,10},{10,1... | collective-permute-start | bytes 921608 | tf_op jit(solution)/shard_map/ppermute | solution.py:593
  854.1 35.4 %collective-permute-start.14 = (bf16[200,768]{1,0:T(8,128)(2,1)S(1)}, bf16[200,768]{1,0:T(8,128)(2,1)S(1)}, u32[]{:S(2)}, u32[]{:S(2)}) collective-permute-start(bf16[200,768]{1,0:T(8,128)(2,1)S(1)} %get-tuple-element.127), channel_id=1, source_target_pairs={{0,3},{1,0},{2,1},{3,2},{4,7},{5,4},{6,5},{7,6},{8,11},{9,8},{10,9... | collective-permute-start | bytes 921608 | tf_op jit(solution)/shard_map/ppermute | solution.py:593
  858.0 31.5 %collective-permute-start.13 = (bf16[200,768]{1,0:T(8,128)(2,1)S(1)}, bf16[200,768]{1,0:T(8,128)(2,1)S(1)}, u32[]{:S(2)}, u32[]{:S(2)}) collective-permute-start(bf16[200,768]{1,0:T(8,128)(2,1)S(1)} %get-tuple-element.128), channel_id=1, source_target_pairs={{0,2},{1,3},{2,0},{3,1},{4,6},{5,7},{6,4},{7,5},{8,10},{9,11},{10,... | collective-permute-start | bytes 921608 | tf_op jit(solution)/shard_map/ppermute | solution.py:593
  864.7 18.4 %collective-permute-start.12 = (bf16[200,768]{1,0:T(8,128)(2,1)S(1)}, bf16[200,768]{1,0:T(8,128)(2,1)S(1)}, u32[]{:S(2)}, u32[]{:S(2)}) collective-permute-start(bf16[200,768]{1,0:T(8,128)(2,1)S(1)} %get-tuple-element.129), channel_id=1, source_target_pairs={{0,1},{1,2},{2,3},{3,0},{4,5},{5,6},{6,7},{7,4},{8,9},{9,10},{10,1... | collective-permute-start | bytes 921608 | tf_op jit(solution)/shard_map/ppermute | solution.py:593
  889.6 125.4 %copy-start.29 = (bf16[5,200,768]{2,1,0:T(8,128)(2,1)}, bf16[5,200,768]{2,1,0:T(8,128)(2,1)S(1)}, u32[]{:S(2)}) copy-start(bf16[5,200,768]{2,1,0:T(8,128)(2,1)S(1)} %bitcast_dynamic-update-slice_fusion) | copy-start | bytes 4608004
  (31 other events, 71.8 us)
Sparse Core Ops, SparseCore 0:
  11.3 113.2 all-gather.2
  127.4 86.2 all-gather.4
  763.6 101.2 reduce-scatter.6
  870.7 141.9 reduce-scatter.4

commit v2 on v1

v2 whole, which is shorter than its diff:
```python
import functools

import jax
import jax.numpy as jnp
from jax import lax
from jax.experimental import pallas as pl
from jax.experimental.pallas import tpu as pltpu
from jax.sharding import PartitionSpec as P

EPS_NORM = 1e-05
LANES = 128
SMALL = 128
BF16 = jnp.bfloat16
F32 = jnp.float32
NN = (((1,), (0,)), ((), ()))
NT = (((1,), (1,)), ((), ()))
TN = (((0,), (0,)), ((), ()))
HIGHEST = lax.Precision.HIGHEST


def dotf(a, b, dims):
    return lax.dot_general(a, b, dims, preferred_element_type=F32)


def tiles_of(total, tile):
    return [(s, min(tile, total - s)) for s in range(0, total, tile)]


ANY_SPEC = pl.BlockSpec(memory_space=pl.ANY)


def ignoring(kernel, inputs, count):
    return lambda *refs: kernel(*refs[:inputs], *refs[inputs + count :])


def cost(us):
    return pl.CostEstimate(flops=int(us * 1.1e9), bytes_accessed=0, transcendentals=0)


SMEM_SPEC = pl.BlockSpec(memory_space=pltpu.SMEM)


def table_rows_of(u, width):
    return pltpu.roll(jnp.broadcast_to(u, (LANES, width)), 0, 1, stride=1, stride_axis=0)


def forward_kernel(
    tile, flip, u_ref, q_ref, k_ref, v_ref, qa_ref, ka_ref, g_ref, _o, _ob,
    o_ref, ob_ref, lse_ref, t_scr,
):
    nq, nk, width = q_ref.shape[0], k_ref.shape[0], u_ref.shape[-1]
    pair = pl.program_id(0)
    half = LANES // 2
    shift = -(-nk // LANES)
    low = lax.broadcasted_iota(jnp.int32, (1, LANES), 1) < half
    low_rows = lax.broadcasted_iota(jnp.int32, (LANES, 1), 0) < half
    k, v, q = k_ref[...], v_ref[...], q_ref[...]
    zero = jnp.zeros((), BF16)
    khs, qhs, vzs, gs = [], [], [], []
    for hh in range(2):
        head = pl.ds(2 * pair + hh, 1)
        t_scr[hh] = table_rows_of(u_ref[head, :], width)
        gs.append(g_ref[head, :])
        sel = low if hh == 0 else jnp.logical_not(low)
        khs.append(jnp.where(sel, k, ka_ref[...]))
        qhs.append(jnp.where(sel, q, qa_ref[...]))
        vzs.append(jnp.where(sel, v, zero))
    vt = v.T if flip else None
    for first, cols in tiles_of(nq, tile):
        total, scales, parts = None, [], []
        for hh in range(2):
            raw = dotf(khs[hh], qhs[hh][first : first + cols], NT)
            g = gs[hh][:, first : first + cols]
            scores, peak = [], None
            for f2, r2 in tiles_of(nk, LANES):
                col = (shift - f2 // LANES) * LANES + first
                s = raw[f2 : f2 + r2] + g * t_scr[hh, 0:r2, col : col + cols]
                top = jnp.max(s, axis=0, keepdims=True)
                peak = top if peak is None else jnp.maximum(peak, top)
                scores.append(s)
            probs, mass = [], None
            for s in scores:
                p = jnp.exp(s - peak)
                part = jnp.sum(p, axis=0, keepdims=True)
                mass = part if mass is None else mass + part
                probs.append(p.astype(BF16))
            lse_ref[pl.ds(2 * pair + hh, 1), first : first + cols] = peak + jnp.log(mass)
            pb = jnp.concatenate(probs, axis=0)
            if flip:
                parts.append(dotf(vt[hh * half : (hh + 1) * half], pb, NN) / mass)
            else:
                x = dotf(pb, vzs[hh], TN)
                total = x if total is None else total + x
                scales.append(1.0 / mass)
        if flip:
            o = jnp.concatenate(parts, axis=0).T
        else:
            o = total * jnp.where(low_rows, scales[0], scales[1]).T
        o_ref[first : first + cols, :] = o
        ob_ref[first : first + cols, :] = o.astype(BF16)


def attend_forward(
    u, q, k, v, qa, ka, g, cols, tile, flip, into, row_block, us, deps=()
):
    nq, nk = qa.shape[0], ka.shape[0]
    heads, width = u.shape
    pairs = heads // 2
    col = lambda c: (lambda p: (0, c + p))
    fix = lambda p: (0, 0)
    out_spec = pl.BlockSpec((nq, LANES), lambda p: (row_block, p))
    return pl.pallas_call(
        ignoring(functools.partial(forward_kernel, tile, flip), 9, len(deps)),
        grid=(pairs,),
        in_specs=[
            pl.BlockSpec(u.shape, fix),
            pl.BlockSpec((nq, LANES), col(cols[0])),
            pl.BlockSpec((nk, LANES), col(cols[1])),
            pl.BlockSpec((nk, LANES), col(cols[2])),
            pl.BlockSpec((nq, LANES), fix),
            pl.BlockSpec((nk, LANES), fix),
            pl.BlockSpec(g.shape, fix),
            ANY_SPEC,
            ANY_SPEC,
        ]
        + [ANY_SPEC] * len(deps),
        out_specs=[out_spec, out_spec, pl.BlockSpec((heads, nq), fix)],
        out_shape=[
            jax.ShapeDtypeStruct(into[0].shape, F32),
            jax.ShapeDtypeStruct(into[1].shape, BF16),
            jax.ShapeDtypeStruct((heads, nq), F32),
        ],
        input_output_aliases={7: 0, 8: 1},
        scratch_shapes=[pltpu.VMEM((2, LANES, width), F32)],
        compiler_params=pltpu.CompilerParams(vmem_limit_bytes=48 * 2**20),
        cost_estimate=cost(us),
        name="attention_forward",
    )(u, q, k, v, qa, ka, g, *into, *deps)


def backward_kernel(
    start, u_ref, q_ref, k_ref, v_ref, do_ref, att_ref, qa_ref, ka_ref, g_ref, lse_ref,
    gate_in, diag_in, dq_ref, dkv_ref, col_ref, gate_ref, diag_ref, t_scr, c_scr,
):
    nq, nk, width = q_ref.shape[0], k_ref.shape[0], u_ref.shape[-1]
    step = pl.program_id(0)
    shift = -(-nk // LANES)

    @pl.when(step == 0)
    def _():
        gate_ref[...] = gate_in[...]
        diag_ref[...] = diag_in[...]

    low = lax.broadcasted_iota(jnp.int32, (1, LANES), 1) < LANES // 2
    k, v, q, do = k_ref[...], v_ref[...], q_ref[...], do_ref[...]
    prod = do.astype(F32) * att_ref[...]
    zero = jnp.zeros((), BF16)
    dq, dk, dv = None, None, None
    for hh in range(2):
        head = pl.ds(2 * (start + step) + hh, 1)
        t_scr[hh] = table_rows_of(u_ref[head, :], width)
        c_scr[hh] = jnp.zeros_like(c_scr[hh])
        sel = low if hh == 0 else jnp.logical_not(low)
        ones = jnp.broadcast_to(jnp.where(sel, 1.0, 0.0), (8, LANES))
        delta = lax.dot_general(ones, prod, NT, precision=HIGHEST, preferred_element_type=F32)[0:1]
        ka = jnp.where(sel, k, ka_ref[...])
        qa = jnp.where(sel, q, qa_ref[...])
        kz, qz, doz = jnp.where(sel, k, zero), jnp.where(sel, q, zero), jnp.where(sel, do, zero)
        lse = lse_ref[head, :]
        g = g_ref[head, :]
        gate = jnp.zeros((1, nq), F32)
        raw = dotf(ka, qa, NT)
        dp = dotf(v, doz, NT)
        ps, ds = [], []
        for first, rows in tiles_of(nk, LANES):
            col = (shift - first // LANES) * LANES
            t = t_scr[hh, 0:rows, col : col + nq]
            p = jnp.exp(raw[first : first + rows] + (g * t - lse))
            d = p * (dp[first : first + rows] - delta)
            gate += jnp.sum(d * t, axis=0, keepdims=True)
            c_scr[hh, 0:rows, col : col + nq] += d * g
            ps.append(p.astype(BF16))
            ds.append(d.astype(BF16))
        pb, db = jnp.concatenate(ps, axis=0), jnp.concatenate(ds, axis=0)
        dk_add, dv_add, dq_add = dotf(db, qz, NN), dotf(pb, doz, NN), dotf(db, kz, TN)
        dk = dk_add if dk is None else dk + dk_add
        dv = dv_add if dv is None else dv + dv_add
        dq = dq_add if dq is None else dq + dq_add
        gate_ref[head, :] = gate
        half = LANES // 2
        acc = c_scr[hh]
        while half >= 8:
            acc = acc[:half] + pltpu.roll(acc[half:], width - half, 1)
            half //= 2
        row = lax.broadcasted_iota(jnp.int32, (8, 1), 0)
        for bit in (1, 2, 4):
            acc = jnp.where((row & bit) != 0, pltpu.roll(acc, width - bit, 1), acc)
        diag_ref[head, :] += jnp.sum(acc, axis=0, keepdims=True)
    dq_ref[...] = (dq.astype(BF16) * (LANES // 2) ** -0.5).astype(BF16)
    dkv_ref[0] = dk.astype(BF16)
    dkv_ref[1] = dv.astype(BF16)
    col_ref[0:1, :] = jnp.sum(dq, axis=0, keepdims=True) * (LANES // 2) ** -0.5
    col_ref[1:2, :] = jnp.sum(dv, axis=0, keepdims=True)


def attend_backward(
    u, q, k, v, do, att, qa, ka, g, lse, gate, diag, cols, row_block, us,
    start=0, count=None, into=(), deps=(),
):
    nq, nk = qa.shape[0], ka.shape[0]
    heads, width = u.shape
    pairs = heads // 2
    count = count or pairs
    col = lambda c: (lambda p: (0, c + start + p))
    row = lambda p: (row_block, start + p)
    fix = lambda p: (0, 0)
    return pl.pallas_call(
        ignoring(functools.partial(backward_kernel, start), 12, len(into) + len(deps)),
        grid=(count,),
        in_specs=[
            pl.BlockSpec(u.shape, fix),
            pl.BlockSpec((nq, LANES), col(cols[0])),
            pl.BlockSpec((nk, LANES), col(cols[1])),
            pl.BlockSpec((nk, LANES), col(cols[2])),
            pl.BlockSpec((nq, LANES), row),
            pl.BlockSpec((nq, LANES), row),
            pl.BlockSpec((nq, LANES), fix),
            pl.BlockSpec((nk, LANES), fix),
            pl.BlockSpec(g.shape, fix),
            pl.BlockSpec(lse.shape, fix),
            pl.BlockSpec(gate.shape, fix),
            pl.BlockSpec(diag.shape, fix),
        ]
        + [ANY_SPEC] * (len(into) + len(deps)),
        out_specs=[
            pl.BlockSpec((nq, LANES), col(0)),
            pl.BlockSpec((2, nk, LANES), lambda p: (0, 0, start + p)),
            pl.BlockSpec((2, LANES), col(0)),
            pl.BlockSpec(gate.shape, fix),
            pl.BlockSpec(diag.shape, fix),
        ],
        out_shape=[
            jax.ShapeDtypeStruct((nq, pairs * LANES), BF16),
            jax.ShapeDtypeStruct((2, nk, pairs * LANES), BF16),
            jax.ShapeDtypeStruct((2, pairs * LANES), F32),
            jax.ShapeDtypeStruct(gate.shape, F32),
            jax.ShapeDtypeStruct(diag.shape, F32),
        ],
        input_output_aliases={12 + i: i for i in range(len(into))},
        scratch_shapes=[pltpu.VMEM((2, LANES, width), F32), pltpu.VMEM((2, LANES, width), F32)],
        compiler_params=pltpu.CompilerParams(vmem_limit_bytes=56 * 2**20),
        cost_estimate=cost(us),
        name="attention_backward",
    )(u, q, k, v, do, att, qa, ka, g, lse, gate, diag, *into, *deps)


def project_own_kernel(x_ref, mine_ref, other_ref, core_ref, out_ref, w_ref, small_ref):
    step = pl.program_id(0)
    width = x_ref.shape[1]
    cut = 3 * width // 2

    def unpack(first, second):
        w_ref[:, 0:cut] = first[:, 0:cut]
        w_ref[:, cut : 2 * cut] = second[:, 0:cut]
        small_ref[...] = first[:, cut : cut + SMALL].astype(F32).T[0 : small_ref.shape[0]]

    @pl.when((step == 0) & (core_ref[0] == 0))
    def _():
        unpack(mine_ref, other_ref)

    @pl.when((step == 0) & (core_ref[0] != 0))
    def _():
        unpack(other_ref, mine_ref)

    bias = jnp.where(step == 0, small_ref[0:1, :], jnp.where(step == 2, small_ref[1:2, :], 0.0))
    scale = jnp.where(step == 0, (LANES // 2) ** -0.5, 1.0)
    w = w_ref[:, pl.ds(pl.multiple_of(step * width, LANES), width)]
    out_ref[...] = ((dotf(x_ref[...], w, NN) + bias) * scale).astype(BF16)


def project_own(x, rows, mine, other, core):
    width = x.shape[1]
    fix = lambda c: (0, 0)
    return pl.pallas_call(
        project_own_kernel,
        grid=(3,),
        in_specs=[
            pl.BlockSpec((rows, width), fix),
            pl.BlockSpec(mine.shape, fix),
            pl.BlockSpec(other.shape, fix),
            SMEM_SPEC,
        ],
        out_specs=[
            pl.BlockSpec((rows, width), lambda c: (0, c)),
            pl.BlockSpec((width, 3 * width), fix),
            pl.BlockSpec((16, width), fix),
        ],
        out_shape=[
            jax.ShapeDtypeStruct((rows, 3 * width), BF16),
            jax.ShapeDtypeStruct((width, 3 * width), BF16),
            jax.ShapeDtypeStruct((16, width), F32),
        ],
        compiler_params=pltpu.CompilerParams(vmem_limit_bytes=48 * 2**20),
        cost_estimate=cost(8),
        name="projection_own",
    )(x, mine, other, core)


def project_shared_kernel(all_ref, loc_ref, w_ref, b_ref, q_out, kv_out):
    step = pl.program_id(0)

    @pl.when(step == 0)
    def _():
        q = dotf(loc_ref[...], w_ref[...], NN) + b_ref[0:1, :]
        q_out[...] = (q * (LANES // 2) ** -0.5).astype(BF16)

    @pl.when(step > 0)
    def _():
        bias = jnp.where(step == 2, b_ref[1:2, :], 0.0)
        kv_out[...] = (dotf(all_ref[...], w_ref[...], NN) + bias).astype(BF16)


def project_shared(x_all, x_loc, weight, small, deps=()):
    n_all, width = x_all.shape
    n_loc = x_loc.shape[0]
    fix = lambda c: (0, 0)
    return pl.pallas_call(
        ignoring(project_shared_kernel, 4, len(deps)),
        grid=(3,),
        in_specs=[
            pl.BlockSpec((n_all, width), fix),
            pl.BlockSpec((n_loc, width), fix),
            pl.BlockSpec((width, width), lambda c: (0, c)),
            pl.BlockSpec(small.shape, fix),
        ]
        + [ANY_SPEC] * len(deps),
        out_specs=[
            pl.BlockSpec((n_loc, width), fix),
            pl.BlockSpec((n_all, width), lambda c: (0, jnp.maximum(c - 1, 0))),
        ],
        out_shape=[
            jax.ShapeDtypeStruct((n_loc, width), BF16),
            jax.ShapeDtypeStruct((n_all, 2 * width), BF16),
        ],
        compiler_params=pltpu.CompilerParams(vmem_limit_bytes=48 * 2**20),
        cost_estimate=cost(5),
        name="projection_shared",
    )(x_all, x_loc, weight, small, *deps)


def gelu_parts(x):
    size = jnp.abs(x)
    t = 1.0 / (1.0 + (0.3275911 * 0.7071067811865476) * size)
    poly = t * (
        0.254829592
        + t * (-0.284496736 + t * (1.421413741 + t * (-1.453152027 + t * 1.061405429)))
    )
    bell = jnp.exp(-0.5 * x * x)
    tail = 0.5 * poly * bell
    phi = jnp.where(x >= 0, 1.0 - tail, tail)
    return x * phi, phi + x * bell * 0.3989422804014327


def mean_last(v):
    return jnp.sum(v, axis=-1, keepdims=True) * (1.0 / v.shape[-1])


def layer_kernel(
    chunks, tile,
    x_ref, a_ref, c_ref, wom_ref, woo_ref, mine_ref, other_ref, vec_ref, core_ref,
    h_ref, ga_ref, g1_ref, keep_ref, send_ref, sums_ref,
    z_scr, r_scr, nh_scr, acc_scr, di_scr, act_scr, der_scr, ih_scr, wo_ref, up_ref, down_ref,
):
    step = pl.program_id(0)
    total, width = x_ref.shape
    half = width // 2
    low_core = core_ref[0] == 0
    high_core = core_ref[0] != 0

    vec = lambda i: vec_ref[i : i + 1, :]

    def over_tiles(body):
        @pl.loop(0, total // tile)
        def _(i):
            body(pl.ds(pl.multiple_of(i * tile, tile), tile))

    def add_sum(row, value):
        sums_ref[row : row + 1, :] += jnp.sum(value, axis=0, keepdims=True)

    def load(ref, is_mine):
        @pl.when(is_mine)
        def _():
            ref[...] = mine_ref[...]

        @pl.when(jnp.logical_not(is_mine))
        def _():
            ref[...] = other_ref[...]

    def emit(is_mine, value, cols=slice(None)):
        @pl.when(is_mine)
        def _():
            keep_ref[:, cols] = value

        @pl.when(jnp.logical_not(is_mine))
        def _():
            send_ref[:, cols] = value

    back = jnp.maximum(step - chunks, 0)
    j = back // 2
    forth = step < chunks
    even = (step >= chunks) & (step < 3 * chunks) & (back % 2 == 0)
    odd = (step >= chunks) & (step < 3 * chunks) & (back % 2 == 1)

    @pl.when(step == 0)
    def _():
        sums_ref[...] = jnp.zeros_like(sums_ref)

        @pl.when(low_core)
        def _():
            wo_ref[:, 0:half] = wom_ref[...]
            wo_ref[:, half:width] = woo_ref[...]

        @pl.when(high_core)
        def _():
            wo_ref[:, 0:half] = woo_ref[...]
            wo_ref[:, half:width] = wom_ref[...]

        def body(here):
            y = dotf(a_ref[here, :], wo_ref[...], NN) + vec(2) + x_ref[here, :].astype(F32)
            y = y - mean_last(y)
            r = lax.rsqrt(mean_last(y * y) + EPS_NORM)
            z = y * r
            z_scr[here, :] = z
            r_scr[here, :] = r
            nh_scr[here, :] = (z * vec(6) + vec(4)).astype(BF16)
            acc_scr[here, :] = jnp.zeros_like(z)

        over_tiles(body)

    @pl.when(forth | odd)
    def _():
        load(up_ref, low_core)

    @pl.when(forth | even)
    def _():
        load(down_ref, high_core)

    @pl.when(forth)
    def _():
        def body(here):
            inner = dotf(nh_scr[here, :], up_ref[...], NN) + vec_ref[pl.ds(8 + step, 1), :]
            act, der = gelu_parts(inner)
            act = act.astype(BF16)
            act_scr[step, here, :] = act
            der_scr[step, here, :] = der.astype(BF16)
            acc_scr[here, :] += dotf(act, down_ref[...], NN)

        over_tiles(body)

    @pl.when(step == chunks)
    def _():
        def body(here):
            v = z_scr[here, :] * vec(6) + vec(4) + acc_scr[here, :] + vec(3)
            v = v - mean_last(v)
            r = lax.rsqrt(mean_last(v * v) + EPS_NORM)
            z = v * r
            h_ref[here, :] = (z * vec(7) + vec(5)).astype(BF16)
            c = c_ref[here, :].astype(F32)
            q = c * vec(7)
            gt = r * (q - mean_last(q) - z * mean_last(q * z))
            acc_scr[here, :] = gt
            di_scr[here, :] = gt.astype(BF16)
            add_sum(3, gt)
            add_sum(5, c)
            add_sum(7, c * z)

        over_tiles(body)

    @pl.when(even)
    def _():
        emit(high_core, dotf(act_scr[j], di_scr[...], TN).astype(BF16))

        def body(here):
            gi = dotf(di_scr[here, :], down_ref[...], NT) * der_scr[j, here, :].astype(F32)
            sums_ref[pl.ds(8 + j, 1), :] += jnp.sum(gi, axis=0, keepdims=True)
            ih_scr[here, :] = gi.astype(BF16)

        over_tiles(body)

    @pl.when(odd)
    def _():
        emit(low_core, dotf(nh_scr[...], ih_scr[...], TN).astype(BF16))

        def body(here):
            acc_scr[here, :] += dotf(ih_scr[here, :], up_ref[...], NT)

        over_tiles(body)

    @pl.when(step == 3 * chunks)
    def _():
        def body(here):
            gn = acc_scr[here, :]
            z = z_scr[here, :]
            q = gn * vec(6)
            g1 = r_scr[here, :] * (q - mean_last(q) - z * mean_last(q * z))
            g1_ref[here, :] = g1
            ah = g1.astype(BF16)
            di_scr[here, :] = ah
            ga_ref[here, :] = dotf(ah, wo_ref[...], NT).astype(BF16)
            add_sum(2, g1)
            add_sum(4, gn)
            add_sum(6, gn * z)

        over_tiles(body)
        out = dotf(a_ref[...], di_scr[...], TN).astype(BF16)
        emit(low_core, out[:, 0:half], slice(0, half))
        emit(high_core, out[:, half:width], slice(0, half))


def layer_rest(x, att, cot, mine, other, vec, core, chunks):
    total, width = x.shape
    fix = lambda s: (0, 0)
    once = pl.Buffered(buffer_count=1)

    def chunk_of(s):
        return jnp.where(s < chunks, s, jnp.clip((s - chunks) // 2, 0, chunks - 1))

    def const(shape):
        return pl.BlockSpec(shape, fix, pipeline_mode=once)

    rows = const((total, width))
    square = (width, width)
    out_half = pl.BlockSpec((width, width // 2), lambda s: (0, 2 * chunks), pipeline_mode=once)
    weight_spec = pl.BlockSpec(square, lambda s: (0, chunk_of(s)))
    grad_spec = pl.BlockSpec(square, lambda s: (0, jnp.maximum(s - chunks, 0) // 2))
    return pl.pallas_call(
        functools.partial(layer_kernel, chunks, 256),
        grid=(3 * chunks + 1,),
        in_specs=[
            rows, rows, rows, out_half, out_half, weight_spec, weight_spec, const(vec.shape), SMEM_SPEC,
        ],
        out_specs=[rows, rows, rows, grad_spec, grad_spec, const(vec.shape)],
        out_shape=[
            jax.ShapeDtypeStruct((total, width), BF16),
            jax.ShapeDtypeStruct((total, width), BF16),
            jax.ShapeDtypeStruct((total, width), F32),
            jax.ShapeDtypeStruct(mine.shape, BF16),
            jax.ShapeDtypeStruct(mine.shape, BF16),
            jax.ShapeDtypeStruct(vec.shape, F32),
        ],
        scratch_shapes=[
            pltpu.VMEM((total, width), F32),
            pltpu.VMEM((total, 1), F32),
            pltpu.VMEM((total, width), BF16),
            pltpu.VMEM((total, width), F32),
            pltpu.VMEM((total, width), BF16),
            pltpu.VMEM((chunks, total, width), BF16),
            pltpu.VMEM((chunks, total, width), BF16),
            pltpu.VMEM((total, width), BF16),
            pltpu.VMEM(square, BF16),
            pltpu.VMEM(square, BF16),
            pltpu.VMEM(square, BF16),
        ],
        compiler_params=pltpu.CompilerParams(vmem_limit_bytes=60 * 2**20),
        cost_estimate=cost(70),
        name="layer_rest",
    )(x, att, cot, mine, other, mine, other, vec, core)


def shared_input_kernel(dq_ref, dkv_ref, w_ref, part_ref, loc_ref, acc):
    step = pl.program_id(0)

    @pl.when(step == 0)
    def _():
        loc_ref[...] = dotf(dq_ref[...], w_ref[...], NT)

    @pl.when(step == 1)
    def _():
        acc[...] = dotf(dkv_ref[...], w_ref[...], NT)

    @pl.when(step == 2)
    def _():
        part_ref[...] = (acc[...] + dotf(dkv_ref[...], w_ref[...], NT)).astype(BF16)


def shared_input(dq, dkv, weight, deps=()):
    n_loc, width = dq.shape
    n_all = dkv.shape[1]
    fix = lambda c: (0, 0)
    return pl.pallas_call(
        ignoring(shared_input_kernel, 3, len(deps)),
        grid=(3,),
        in_specs=[
            pl.BlockSpec((n_loc, width), fix),
            pl.BlockSpec((None, n_all, width), lambda c: (jnp.maximum(c - 1, 0), 0, 0)),
            pl.BlockSpec((width, width), lambda c: (0, c)),
        ]
        + [ANY_SPEC] * len(deps),
        out_specs=[pl.BlockSpec((n_all, width), fix), pl.BlockSpec((n_loc, width), fix)],
        out_shape=[
            jax.ShapeDtypeStruct((n_all, width), BF16),
            jax.ShapeDtypeStruct((n_loc, width), F32),
        ],
        scratch_shapes=[pltpu.VMEM((n_all, width), F32)],
        compiler_params=pltpu.CompilerParams(vmem_limit_bytes=48 * 2**20),
        cost_estimate=cost(5),
        name="shared_input",
    )(dq, dkv, weight, *deps)


def weight_grad_kernel(
    x0_ref, x4_ref, loc_ref, dq_ref, dkv_ref, dq4_ref, dkv4_ref, core_ref, keep_ref, send_ref
):
    step = pl.program_id(0)
    width = x0_ref.shape[1]
    half = width // 2
    cut = 3 * half
    low_core = core_ref[0] == 0
    high_core = core_ref[0] != 0

    def emit(is_mine, cols, value):
        @pl.when(is_mine)
        def _():
            keep_ref[:, cols] = value

        @pl.when(jnp.logical_not(is_mine))
        def _():
            send_ref[:, cols] = value

    @pl.when(step == 0)
    def _():
        grad = dotf(x0_ref[...], dq_ref[...], TN) + dotf(loc_ref[...], dq4_ref[...], TN)
        emit(low_core, slice(0, width), grad.astype(BF16))

    @pl.when(step > 0)
    def _():
        grad = dotf(x0_ref[...], dkv_ref[...], TN) + dotf(x4_ref[...], dkv4_ref[...], TN)
        grad = grad.astype(BF16)

        @pl.when(step == 1)
        def _():
            emit(low_core, slice(width, cut), grad[:, 0:half])
            emit(high_core, slice(0, half), grad[:, half:width])

        @pl.when(step == 2)
        def _():
            emit(high_core, slice(half, cut), grad)


def weight_grad(x_cat, x_all, x_loc, dq, dkv, dq4, dkv4, core, deps=()):
    own, width = dq.shape
    n_all, n_loc = x_all.shape[0], x_loc.shape[0]
    fix = lambda c: (0, 0)
    half = lambda c: (jnp.maximum(c - 1, 0), 0, 0)
    shape = (width, 3 * width // 2)
    return pl.pallas_call(
        ignoring(weight_grad_kernel, 8, len(deps)),
        grid=(3,),
        in_specs=[
            pl.BlockSpec((own, width), fix),
            pl.BlockSpec((n_all, width), fix),
            pl.BlockSpec((n_loc, width), fix),
            pl.BlockSpec((own, width), fix),
            pl.BlockSpec((None, own, width), half),
            pl.BlockSpec((n_loc, width), fix),
            pl.BlockSpec((None, n_all, width), half),
            SMEM_SPEC,
        ]
        + [ANY_SPEC] * len(deps),
        out_specs=[pl.BlockSpec(shape, fix)] * 2,
        out_shape=[jax.ShapeDtypeStruct(shape, BF16)] * 2,
        compiler_params=pltpu.CompilerParams(vmem_limit_bytes=56 * 2**20),
        cost_estimate=cost(10),
        name="projection_weight_grad",
    )(x_cat, x_all, x_loc, dq, dkv, dq4, dkv4, core, *deps)


def own_input_kernel(dq_ref, dkv_ref, w_ref, base_ref, gate_ref, dirs_ref, dx_ref, acc):
    step = pl.program_id(0)

    @pl.when(step == 0)
    def _():
        gate = dotf(gate_ref[...], dirs_ref[...], TN)[0 : acc.shape[0]]
        acc[...] = base_ref[...] + gate + dotf(dq_ref[...], w_ref[...], NT)

    @pl.when(step == 1)
    def _():
        acc[...] += dotf(dkv_ref[...], w_ref[...], NT)

    @pl.when(step == 2)
    def _():
        dx_ref[...] = (acc[...] + dotf(dkv_ref[...], w_ref[...], NT)).astype(BF16)


def own_input(dq, dkv, weight, base, gate, dirs, deps=()):
    own, width = dq.shape
    fix = lambda c: (0, 0)
    return pl.pallas_call(
        ignoring(own_input_kernel, 6, len(deps)),
        grid=(3,),
        in_specs=[
            pl.BlockSpec((own, width), fix),
            pl.BlockSpec((None, own, width), lambda c: (jnp.maximum(c - 1, 0), 0, 0)),
            pl.BlockSpec((width, width), lambda c: (0, c)),
            pl.BlockSpec((own, width), fix),
            pl.BlockSpec(gate.shape, fix),
            pl.BlockSpec(dirs.shape, fix),
        ]
        + [ANY_SPEC] * len(deps),
        out_specs=pl.BlockSpec((own, width), fix),
        out_shape=jax.ShapeDtypeStruct((own, width), BF16),
        scratch_shapes=[pltpu.VMEM((own, width), F32)],
        compiler_params=pltpu.CompilerParams(vmem_limit_bytes=56 * 2**20),
        cost_estimate=cost(8),
        name="own_input",
    )(dq, dkv, weight, base, gate, dirs, *deps)


hold = lax.optimization_barrier


def after(value, *earlier):
    return lax.optimization_barrier((value,) + earlier)[0]


def thirds(v):
    high = v.astype(BF16)
    rest = v - high.astype(F32)
    middle = rest.astype(BF16)
    return high, middle, (rest - middle.astype(F32)).astype(BF16)


def swap(array, axis, bit):
    size = lax.axis_size(axis)
    return lax.ppermute(array, axis, [(i, i ^ (1 << bit)) for i in range(size)])


def swap_places(array, mask):
    return lax.ppermute(array, "blk", [(i, i ^ mask) for i in range(lax.axis_size("blk"))])


def by_place(arrays):
    place = lax.axis_index("blk")
    odd, upper = (place & 1) == 1, (place >> 1) == 1
    near = [jnp.where(odd, arrays[1 - i], arrays[i]) for i in range(2)]
    far = [jnp.where(odd, arrays[3 - i], arrays[2 + i]) for i in range(2)]
    return [jnp.where(upper, f, n) for f, n in zip(far, near)] + [
        jnp.where(upper, n, f) for f, n in zip(far, near)
    ]


def bit_of(axis, bit):
    return (lax.axis_index(axis) >> bit) & 1


def bit_count(axis):
    count = lax.axis_size(axis).bit_length() - 1
    assert 1 << count == lax.axis_size(axis)
    return count


def join(array, axis, bit, position):
    def finish(flight):
        mine, other = flight
        upper = bit_of(axis, bit) == 1
        return jnp.stack(
            [jnp.where(upper, other, mine), jnp.where(upper, mine, other)], axis=position
        )

    return (array, swap(array, axis, bit)), finish


def at_once(step):
    flight, finish = step
    return finish(flight)


def together(steps):
    flights, finishes = zip(*steps)
    return flights, lambda done: [finish(flight) for finish, flight in zip(finishes, done)]


def gather_begin(first, second):
    low = bit_of("rows", 0) == 0
    keep, send = jnp.where(low, first, second), jnp.where(low, second, first)

    def finish(flight):
        mine, got = flight
        return jnp.stack([jnp.where(low, mine, got), jnp.where(low, got, mine)], axis=0)

    return (keep, swap(send, "rows", 0)), finish


def blk_bits():
    return list(reversed(range(bit_count("blk"))))


def gather_blk(part, number):
    return join(part, "blk", blk_bits()[number], 1 + number)


def halves_of(array):
    array = array.reshape(-1, array.shape[-1])
    cut = array.shape[-1] // 2 // LANES * LANES
    return [array[:, :cut], array[:, cut:]]


def orders():
    high = list(range(1, bit_count("rows")))
    return high, high[::-1]


def gather_high(halves, step):
    steps = []
    for half, order in zip(halves, orders()):
        position = sum(1 for other in order[:step] if other > order[step])
        steps.append(join(half, "rows", order[step], position))
    return together(steps)


def whole(halves):
    return jnp.concatenate([h.reshape(-1, h.shape[-1]) for h in halves], axis=-1)


def halve(array, axis, bit, position):
    mine = bit_of(axis, bit)
    keep = lax.dynamic_index_in_dim(array, mine, position, keepdims=False)
    send = lax.dynamic_index_in_dim(array, 1 - mine, position, keepdims=False)

    def finish(flight):
        return (flight[0].astype(F32) + flight[1].astype(F32)).astype(BF16)

    return (keep, swap(send, axis, bit)), finish


def scatter_begin(keep, send):
    def finish(flight):
        return (flight[0].astype(F32) + flight[1].astype(F32)).astype(BF16)

    return (keep, swap(send, "rows", 0)), finish


def scatter_high(halves, step):
    steps = []
    for half, order in zip(halves, orders()):
        left = sorted(order[step:], reverse=True)
        view = half.reshape((2,) * len(left) + (-1, half.shape[-1]))
        steps.append(halve(view, "rows", order[step], left.index(order[step])))
    return together(steps)


def scatter_blk(part, bit):
    count = bit_count("blk")
    part = part.reshape((2,) * (1 + count - bit) + (-1, part.shape[-1]))
    return halve(part, "blk", bit, count - bit)


def scatter_end(part):
    core = bit_of("rows", 0)
    part = part.reshape((2, -1, part.shape[-1]))
    keep = lax.dynamic_index_in_dim(part, core, 0, keepdims=False)
    send = lax.dynamic_index_in_dim(part, 1 - core, 0, keepdims=False)

    def finish(flight):
        keep, got = flight
        low = core == 0
        first, second = jnp.where(low, keep, got), jnp.where(low, got, keep)
        return first.astype(F32), second.astype(F32)

    return (keep, swap(send, "rows", 0)), finish


def exchange_first(blocks):
    upper = bit_of("blk", 1)
    pairs = blocks.reshape((2, 2) + blocks.shape[1:])
    keep = lax.dynamic_index_in_dim(pairs, upper, 0, keepdims=False)
    send = lax.dynamic_index_in_dim(pairs, 1 - upper, 0, keepdims=False)
    return (keep, swap_places(send, 2))


def exchange_second(flight):
    odd = bit_of("blk", 0)
    keep, got = flight
    pick = lambda array, index: lax.dynamic_index_in_dim(array, index, 0, keepdims=False)
    send = jnp.stack([pick(keep, 1 - odd), pick(got, 1 - odd)])
    return (pick(keep, odd), pick(got, odd), swap_places(send, 1))


def exchange_end(flight):
    mine, far, other = flight
    return by_place([mine, other[0], far, other[1]])


def shards(
    hidden_in,
    segment_ids,
    bucket_map,
    qkv_weight,
    out_weight,
    up_weight,
    down_weight,
    bias_cols,
    norm_gains,
    up_bias,
    rel_table,
    gate_weight,
    gate_scale,
    cotangent,
):
    row_count, block_len, width = hidden_in.shape
    heads = gate_scale.shape[0]
    pairs = heads // 2
    head_dim = width // heads
    bucket_count = rel_table.shape[0]
    cycle = lax.axis_size("blk")
    place = lax.axis_index("blk")
    core = bit_of("rows", 0).reshape(1)
    frames = block_len * cycle
    shared = row_count - 1
    used = frames + block_len
    total = -(-used // 256) * 256
    inner_width = up_weight.shape[1]
    chunks = inner_width // width
    local_rows = qkv_weight.shape[0]
    half = width // 2
    cut = 3 * half
    high_steps = len(orders()[0])
    assert row_count == cycle + 1 and cycle == 4

    def take(array, index):
        return lax.dynamic_index_in_dim(array, index, 0, keepdims=False)

    def with_rest(blocks, last):
        return jnp.concatenate(blocks + [last, jnp.zeros((total - used, width), BF16)], axis=0)

    extras = jnp.concatenate(
        [bias_cols, norm_gains, up_bias.reshape(local_rows, chunks)], axis=1
    )
    extras = jnp.pad(extras, ((0, 0), (0, SMALL - extras.shape[1])))
    qkv_part = at_once(
        gather_begin(
            jnp.concatenate([qkv_weight[:, :cut], extras], axis=1),
            jnp.concatenate([qkv_weight[:, cut:], jnp.zeros_like(extras)], axis=1),
        )
    )
    up_turned = up_weight.reshape(local_rows, width, chunks).transpose(0, 2, 1)
    rest_flight, rest_finish = gather_begin(
        jnp.concatenate([up_turned.reshape(local_rows, inner_width), out_weight[:, :half]], axis=1),
        jnp.concatenate([down_weight.reshape(local_rows, inner_width), out_weight[:, half:]], axis=1),
    )
    hidden_in, segment_ids, rest_flight, qkv_part = hold(
        (hidden_in, segment_ids, rest_flight, qkv_part)
    )
    seg_rows = jnp.pad(segment_ids.astype(BF16), ((0, 0), (0, width - block_len)))

    def with_segment(index):
        tail_rows = jnp.pad(take(seg_rows, index)[None, :], ((0, 15), (0, 0)))
        return jnp.concatenate([take(hidden_in, index), tail_rows], axis=0)

    packs = [with_segment(place ^ s) for s in range(cycle)]
    qkv_flight, qkv_finish = gather_blk(qkv_part, 0)
    packs[1] = swap_places(packs[1], 1)
    qkv_flight, rest_flight = hold((qkv_flight, rest_flight))
    qkv_flight, qkv_finish = gather_blk(qkv_finish(qkv_flight), 1)
    rest_flight, rest_finish = gather_blk(rest_finish(rest_flight), 0)
    qkv_part = qkv_finish(qkv_flight)
    qkv_halves = halves_of(qkv_part)
    for step in range(high_steps - 2):
        qkv_halves = at_once(gather_high(qkv_halves, step))
    qkv_flight, qkv_finish = gather_high(qkv_halves, high_steps - 2)
    qkv_flight, rest_flight, packs = hold((qkv_flight, rest_flight, packs))
    packs[2], packs[3] = swap_places(packs[2], 2), swap_places(packs[3], 3)
    qkv_flight, qkv_finish = gather_high(qkv_finish(qkv_flight), high_steps - 1)
    rest_flight, rest_finish = gather_blk(rest_finish(rest_flight), 1)
    qkv_flight, rest_flight = hold((qkv_flight, rest_flight))
    qkv_mine = whole(qkv_finish(qkv_flight))
    qkv_other = swap(qkv_mine, "rows", 0)
    rest_halves = halves_of(rest_finish(rest_flight))
    for step in range(high_steps - 2):
        rest_halves = at_once(gather_high(rest_halves, step))
    rest_flight, rest_finish = gather_high(rest_halves, high_steps - 2)
    shared_pack = with_segment(shared)
    packs, qkv_mine, shared_pack = hold((packs, qkv_mine, shared_pack))
    shared_flight, shared_finish = join(shared_pack, "blk", 1, 0)
    x_loc = hidden_in[shared]
    x_cat = with_rest(by_place([p[:block_len] for p in packs]), x_loc)
    seg_own = jnp.concatenate(by_place([p[block_len, :block_len] for p in packs]))

    gate_weight, bucket_map, _ = hold((gate_weight, bucket_map, qkv_part))
    first_dir = jnp.sum(gate_weight[:, :4], axis=1)
    second_dir = jnp.sum(gate_weight[:, 4:], axis=1)
    picks = jnp.repeat(jnp.eye(heads, dtype=F32), head_dim, axis=0)
    dirs = jnp.concatenate(
        [picks * jnp.tile(first_dir, heads)[:, None], picks * jnp.tile(second_dir, heads)[:, None]],
        axis=1,
    ).T
    gate_count = 2 * heads
    dirs_high, dirs_middle, dirs_low = thirds(dirs)
    logits = dotf(jnp.concatenate([dirs_high, dirs_middle, dirs_low], axis=0), x_cat, NT)
    logits = logits[:gate_count] + (
        logits[gate_count : 2 * gate_count] + logits[2 * gate_count :]
    )
    sig = jax.nn.sigmoid(logits)
    gate_a, gate_b = sig[:heads], sig[heads:]
    gating = gate_a * (gate_b * gate_scale[:, None] - 1.0) + 2.0
    g_own, g_loc = gating[:, :frames], gating[:, frames:used]

    shift = -(-frames // LANES)
    span = 2 * frames - 1
    lead = shift * LANES - (frames - 1)
    table_width = 2 * shift * LANES
    slots = jnp.pad(bucket_map[::-1], (lead, table_width - lead - span), constant_values=-1)
    bucket_ids = jnp.arange(bucket_count, dtype=jnp.int32)
    hot = (bucket_ids[:, None] == slots[None, :]).astype(F32)
    u_own = lax.dot_general(rel_table, hot, (((0,), (0,)), ((), ())), precision=HIGHEST)
    narrow = -(-(shift * LANES + block_len) // LANES) * LANES
    u_loc = lax.dynamic_slice_in_dim(
        jnp.pad(u_own, ((0, 0), (0, frames))), place * block_len, narrow, 1
    )

    lane = jnp.arange(LANES) % (LANES // 2)

    def penalty(seg):
        seg = seg.astype(jnp.int32)
        return jnp.where((lane < 4)[None, :] & (lane[None, :] != seg[:, None]), -1e30, 0.0).astype(BF16)

    def member(seg):
        return (lane[None, :] == seg.astype(jnp.int32)[:, None]).astype(BF16)

    qa_own, ka_own = penalty(seg_own), member(seg_own)

    own_cols = (0, pairs, 2 * pairs)
    loc_cols = (0, 0, pairs)
    qkv_own, qkv_full, small = project_own(x_cat, frames, qkv_mine, qkv_other, core)
    rest_flight, shared_flight, qkv_own, small, cotangent = hold(
        (rest_flight, shared_flight, qkv_own, small, cotangent)
    )
    rest_flight, rest_finish = gather_high(rest_finish(rest_flight), high_steps - 1)
    shared_flight, shared_finish = join(shared_finish(shared_flight), "blk", 0, 1)
    cot_flight = exchange_first(cotangent[:cycle])
    into = (jnp.zeros((total, width), F32), jnp.zeros((total, width), BF16))
    att, att_half, lse_own = attend_forward(
        u_own, qkv_own, qkv_own, qkv_own, qa_own, ka_own, g_own, own_cols, frames, True, into, 0, 18,
    )
    shared_flight, cot_flight, rest_flight, att, att_half, lse_own = hold(
        (shared_flight, cot_flight, rest_flight, att, att_half, lse_own)
    )
    rest_mine = whole(rest_finish(rest_flight))
    rest_other = swap(rest_mine, "rows", 0)
    cot_flight = exchange_second(cot_flight)
    shared_pack = shared_finish(shared_flight).reshape((cycle, -1, width))
    x_all = shared_pack[:, :block_len].reshape(frames, width)
    seg_all = shared_pack[:, block_len, :block_len].reshape(frames)
    qa_loc, ka_all = penalty(segment_ids[shared]), member(seg_all)
    q_loc, kv_all = project_shared(x_all, x_loc, qkv_full, small, (rest_mine,))
    att, att_half, lse_loc = attend_forward(
        u_loc, q_loc, kv_all, kv_all, qa_loc, ka_all, g_loc, loc_cols, frames, False,
        (att, att_half), cycle, 8,
    )
    cot_flight, rest_other, att, att_half, lse_loc = hold(
        (cot_flight, rest_other, att, att_half, lse_loc)
    )
    c_cat = with_rest(exchange_end(cot_flight), cotangent[shared])
    h_cat, ga_cat, g1_cat, rest_keep, rest_send, sums = layer_rest(
        x_cat, att_half, c_cat, rest_mine, rest_other, small, core, chunks
    )

    def blocks_of(own):
        return own[:frames].reshape(cycle, block_len, width)

    rest_flight, rest_finish = scatter_begin(rest_keep, rest_send)
    hidden_flight = exchange_first(blocks_of(h_cat))
    dq_loc, dkv_all, col_loc, gate_loc, diag_loc = attend_backward(
        u_loc, q_loc, kv_all, kv_all, ga_cat, att, qa_loc, ka_all, g_loc, lse_loc,
        jnp.zeros((heads, block_len), F32), jnp.zeros((heads, narrow), F32), loc_cols, cycle, 16,
    )
    part_all, dx_loc = shared_input(dq_loc, dkv_all, qkv_full)
    rest_flight, part_all, dx_loc, diag_loc = hold((rest_flight, part_all, dx_loc, diag_loc))
    rest_halves = halves_of(rest_finish(rest_flight))
    rest_flight, rest_finish = scatter_high(rest_halves, 0)
    part_flight, part_finish = halve(part_all.reshape(2, 2, block_len, width), "blk", 0, 1)
    diag = lax.dynamic_slice_in_dim(
        jnp.pad(diag_loc, ((0, 0), (frames, table_width))), frames - place * block_len, table_width, 1
    )
    split = pairs - pairs // 3
    into = attend_backward(
        u_own, qkv_own, qkv_own, qkv_own, ga_cat, att, qa_own, ka_own, g_own, lse_own,
        jnp.zeros((heads, frames), F32), diag, own_cols, 0, 26, 0, split, (), (part_all,),
    )
    rest_flight, hidden_flight, part_flight, into = hold(
        (rest_flight, hidden_flight, part_flight, into)
    )
    rest_halves = rest_finish(rest_flight)
    for step in range(1, high_steps):
        rest_flight, rest_finish = scatter_high(rest_halves, step)
        rest_halves = rest_finish(rest_flight) if step < high_steps - 1 else rest_halves
    hidden_flight = exchange_second(hidden_flight)
    part_flight, part_finish = halve(part_finish(part_flight), "blk", 1, 0)
    dq_own, dkv_own, col_own, gate_own, diag = into
    into = attend_backward(
        u_own, qkv_own, qkv_own, qkv_own, ga_cat, att, qa_own, ka_own, g_own, lse_own,
        gate_own, diag, own_cols, 0, 13, split, pairs - split, (dq_own, dkv_own, col_own),
        tuple(rest_halves),
    )
    rest_flight, hidden_flight, part_flight, into = hold(
        (rest_flight, hidden_flight, part_flight, into)
    )
    dq_own, dkv_own, col_own, gate_own, diag = into
    rest_flight, rest_finish = scatter_blk(whole(rest_finish(rest_flight)), 0)

    gate_grad = jnp.concatenate(
        [gate_own, gate_loc, jnp.zeros((heads, total - used), F32)], axis=1
    )
    a, b, c = gate_a, gate_b, gate_scale[:, None]
    da = gate_grad * (b * c - 1.0) * a * (1.0 - a)
    db = gate_grad * a * c * b * (1.0 - b)
    d = jnp.concatenate([da, db], axis=0)
    d_high, d_middle, d_low = thirds(d)
    d_mix = jnp.concatenate([d_high, d_middle, d_high], axis=0)
    dirs_mix = jnp.concatenate([dirs_high, dirs_high, dirs_middle], axis=0)
    dx_own = own_input(dq_own, dkv_own, qkv_full, g1_cat, d_mix, dirs_mix)
    rest_flight, dx_own, hidden_flight, part_flight, sums = hold(
        (rest_flight, dx_own, hidden_flight, part_flight, sums)
    )
    input_flight = exchange_first(blocks_of(dx_own))
    rest_flight, rest_finish = scatter_blk(rest_finish(rest_flight), 1)
    qkv_keep, qkv_send = weight_grad(
        x_cat, x_all, x_loc, dq_own, dkv_own, dq_loc, dkv_all, core, (dx_own,)
    )
    back_flight, back_finish = scatter_begin(qkv_keep, qkv_send)
    diag, d_high, sums, back_flight = hold((diag, d_high, sums, back_flight))

    dw = dotf(jnp.concatenate([d_high, d_middle, d_low], axis=0), x_cat, NN)
    dw = dw[:gate_count] + (dw[gate_count : 2 * gate_count] + dw[2 * gate_count :])
    dw = jnp.einsum("sggd->sd", dw.reshape(2, heads, heads, head_dim))
    scale_grad = jnp.sum(gate_grad * a * b, axis=1)
    table_grad = lax.dot_general(diag, hot, NT, precision=HIGHEST)
    wide = lambda v: jnp.pad(v, ((0, 0), (0, width - v.shape[1])))
    flat = jnp.concatenate(
        [col_own + col_loc, sums[2 : 8 + chunks], wide(table_grad), wide(dw), wide(scale_grad[None])],
        axis=0,
    )
    flat_steps = [("rows", bit) for bit in range(bit_count("rows"))] + [("blk", 0), ("blk", 1)]
    back_halves = halves_of(back_finish(back_flight))
    for step in range(high_steps):
        back_flight, back_finish = scatter_high(back_halves, step)
        flat_other = swap(flat, *flat_steps[step])
        back_flight, flat, flat_other = hold((back_flight, flat, flat_other))
        back_halves, flat = back_finish(back_flight), flat + flat_other
    back_flight, back_finish = scatter_blk(whole(back_halves), 0)
    input_flight, rest_flight, flat = hold((input_flight, rest_flight, flat))
    input_flight = exchange_second(input_flight)
    rest_flight, rest_finish = scatter_end(rest_finish(rest_flight))
    flat_other = swap(flat, *flat_steps[high_steps])
    back_flight, flat, flat_other, rest_flight = hold((back_flight, flat, flat_other, rest_flight))
    flat = flat + flat_other
    back_flight, back_finish = scatter_blk(back_finish(back_flight), 1)
    flat_other = swap(flat, *flat_steps[high_steps + 1])
    back_flight, flat, flat_other = hold((back_flight, flat, flat_other))
    flat = flat + flat_other
    back_flight, back_finish = scatter_end(back_finish(back_flight))
    for step in flat_steps[high_steps + 2 :]:
        flat = flat + swap(flat, *step)
    gate_x = dotf(d_mix[:, frames:used], dirs_mix, TN)
    mine = dx_loc + part_finish(part_flight).astype(F32) + g1_cat[frames:used] + gate_x
    in_rows = lambda flight, last: jnp.stack(exchange_end(flight) + [last])
    hidden_out = in_rows(hidden_flight, h_cat[frames:used])
    grad_input = in_rows(input_flight, mine.astype(BF16))
    rest_first, rest_second = rest_finish(rest_flight)
    last_first, last_second = back_finish(back_flight)
    cols = 8 + chunks
    first_row = (lax.axis_index("rows") * cycle + place) * local_rows
    local_sums = lax.dynamic_slice(flat, (0, first_row), (cols, local_rows)).T
    table_sum = flat[cols : cols + heads, :bucket_count].T
    dw = flat[cols + heads : cols + heads + 2, :head_dim]
    gate_weight_sum = jnp.broadcast_to(dw[:, None, :], (2, 4, head_dim)).reshape(8, head_dim).T
    gate_scale_sum = flat[cols + heads + 2, :heads]

    grad_up = rest_first[:, :inner_width].reshape(local_rows, chunks, width).transpose(0, 2, 1)
    grad_down = rest_second[:, :inner_width].reshape(local_rows * chunks, width)
    return (
        hidden_out,
        grad_input,
        jnp.concatenate([last_first, last_second], axis=1),
        jnp.concatenate([rest_first[:, inner_width:], rest_second[:, inner_width:]], axis=1),
        grad_up.reshape(local_rows, inner_width),
        grad_down,
        local_sums[:, 0:6],
        local_sums[:, 6:8],
        local_sums[:, 8:cols].reshape(-1),
        table_sum,
        gate_weight_sum,
        gate_scale_sum,
    )


def solution(mesh):
    placed = (
        P("rows", "blk", None),
        P("rows", "blk"),
        P(),
        P(("rows", "blk"), None),
        P(("rows", "blk"), None),
        P(("rows", "blk"), None),
        P(("rows", "blk"), None),
        P(("rows", "blk"), None),
        P(("rows", "blk"), None),
        P(("rows", "blk")),
        P(),
        P(),
        P(),
        P("rows", "blk", None),
    )
    return jax.shard_map(
        shards,
        mesh=mesh,
        in_specs=placed,
        out_specs=(
            P("rows", "blk", None),
            P("rows", "blk", None),
            P(("rows", "blk"), None),
            P(("rows", "blk"), None),
            P(("rows", "blk"), None),
            P(("rows", "blk"), None),
            P(("rows", "blk"), None),
            P(("rows", "blk"), None),
            P(("rows", "blk")),
            P(),
            P(),
            P(),
        ),
        check_vma=False,
    )
```

time: 1030 us -> 467 us (0.45)
  Pallas kernels: 578 us -> 189 us
  waiting for transfers between devices: 219 us -> 103 us
  blocking collectives: 66.5 us -> 0 us
  other arithmetic: 15.5 us -> 47.3 us
  between operations: 15.2 us -> 2.97 us
    pallas_call x8 -> x11, Pallas kernels: 578 us -> 189 us  [the longest x1 72.4 us: layer_rest(): pl.pallas_call(functools.partial(layer_kernel, chunks, 256), grid=(3 * ch...]
    reduce_scatter x1 -> x0, waiting for transfers between devices: 117 us -> none  [shards(): lax.psum_scatter(rest_grad, every, scatter_dimension=0, tiled=True)]
    psum x1 -> x0, blocking collectives: 66.5 us -> none  [shards(): lax.psum((table_grad, gate_weight_grad, gs_own + gs_loc), every)]
    ppermute x15 -> x50, waiting for transfers between devices: 58.1 us -> 103 us  [the longest x41 80.1 us: swap(): return lax.ppermute(array, axis, [(i, i ^ 1 << bit) for i in range(size)])]
    all_gather x2 -> x0, waiting for transfers between devices: 43.5 us -> none  [the longest x1 39 us: shards(): rest_full = lax.all_gather(rest_pack, every, axis=0, tiled=True)]
    dynamic_update_slice x24 -> x0, local copies, waits for them, and re-layouts: 14.4 us -> none  [the longest x16 10 us: spread(): out = lax.dynamic_update_index_in_dim(out, block, (place - s) % cycle, 0)]
    convert_element_type x0 -> x20, other arithmetic: none -> 13.1 us  [the longest x15 12.4 us: finish(): return (flight[0].astype(F32) + flight[1].astype(F32)).astype(BF16)]
    another operation x2 -> x36, other arithmetic: 0.73 us -> 12.6 us  [the longest x28 9.35 us: finish(): jnp.stack([jnp.where(upper, other, mine), jnp.where(upper, mine, other)],...]
  transfers between devices with their start and end apart: 19 -> 50, of which waited for: 9 -> 25; matrix products, arithmetic and copies ran while one was open for 5% -> 15% of each run, Pallas kernels for 4% -> 23%
where the time goes in v2:
time: 467 us; the launch traced here: 458 us
  Pallas kernels  189 us (40%)
  waiting for transfers between devices  103 us (22%)
  starting transfers between devices  58.2 us (12%)
  local copies, waits for them, and re-layouts  53.9 us (12%)
  other arithmetic  47.3 us (10%)
    ppermute x41, waiting for transfers between devices, swap(): return lax.ppermute(array, axis, [(i, i ^ 1 << bit) for i in range(size)])  80.1 us
    pallas_call x1, Pallas kernels, layer_rest(): pl.pallas_call(functools.partial(layer_kernel, chunks, 256), grid=(3 * ch...  72.4 us
    pallas_call x3, Pallas kernels, attend_backward(): pl.pallas_call(ignoring(functools.partial(backward_kernel, start), 12, le...  55.3 us
    ppermute x41, starting transfers between devices, swap(): return lax.ppermute(array, axis, [(i, i ^ 1 << bit) for i in range(size)])  47.9 us
    pallas_call x2, Pallas kernels, attend_forward(): pl.pallas_call(ignoring(functools.partial(forward_kernel, tile, flip), 9,...  27 us
    ppermute x9, waiting for transfers between devices, swap_places(): lax.ppermute(array, 'blk', [(i, i ^ mask) for i in range(lax.axis_size('b...  22.6 us
    unnamed x183, local copies, waits for them, and re-layouts  19.8 us
    pallas_call x1, Pallas kernels, weight_grad(): pl.pallas_call(ignoring(weight_grad_kernel, 8, len(deps)), grid=(3,), in_...  12.5 us
  transfers between devices with their start and end apart: 50, of which 25 were waited for; matrix products, arithmetic and copies ran while one was open for 15% of the time, Pallas kernels for 23%

profile of v2, /device:TPU:0, one launch (start us, length us, event | category | flops | bytes accessed | tf_op | source)
XLA Modules:
  0.0 458.4 jit_solution(2790142846717864997)
XLA Ops:
  9.6 4.1 collective-permute-start.2
  14.4 1.6 collective-permute-start.7
  16.8 3.2 collective-permute-done.2
  20.9 3.5 collective-permute-start.6
  24.4 12.4 %collective-permute-done.3 = bf16[2,2,24,1280]{3,2,1,0:T(8,128)(2,1)S(1)} collective-permute-done((bf16[2,2,24,1280]{3,2,1,0:T(8,128)(2,1)S(1)}, bf16[2,2,24,1280]{3,2,1,0:T(8,128)(2,1)S(1)}, u32[]{:S(2)}, u32[]{:S(2)}) %collective-permute-start.3) | collective-permute-done | bytes 245792 | tf_op jit(solution)/shard_map/ppermute | solution.py:735
  41.8 2.4 collective-permute-done.4
  51.7 3.0 collective-permute-start.8
  56.1 2.9 collective-permute-done.11
  59.0 1.7 collective-permute-done.10
  60.6 10.3 %collective-permute-done.12 = bf16[2,2,24,3456]{3,2,0,1:T(8,128)(2,1)} collective-permute-done((bf16[2,2,24,3456]{3,2,0,1:T(8,128)(2,1)S(1)}, bf16[2,2,24,3456]{3,2,0,1:T(8,128)(2,1)}, u32[]{:S(2)}, u32[]{:S(2)}) %collective-permute-start.12) | collective-permute-done | bytes 663584 | tf_op jit(solution)/shard_map/ppermute | solution.py:735
  75.5 2.3 collective-permute-done.8
  82.6 5.0 %collective-permute-start.15 = (bf16[216,768]{1,0:T(8,128)(2,1)S(1)}, bf16[216,768]{1,0:T(8,128)(2,1)S(1)}, u32[]{:S(2)}, u32[]{:S(2)}) collective-permute-start(bf16[216,768]{1,0:T(8,128)(2,1)S(1)} %copy-done.41), channel_id=1, source_target_pairs={{0,2},{1,3},{2,0},{3,1},{4,6},{5,7},{6,4},{7,5},{8,10},{9,11},{10,... | collective-permute-start | bytes 995336 | tf_op jit(solution)/shard_map/ppermute | solution.py:735
  88.1 5.2 %projection_own.1 = (bf16[800,2304]{1,0:T(8,128)(2,1)}, bf16[768,2304]{1,0:T(8,128)(2,1)}, f32[16,768]{1,0:T(8,128)S(1)}) custom-call(bf16[1024,768]{1,0:T(8,128)(2,1)S(1)} %constant_dynamic-update-slice_fusion.x_ref.refs_0_, bf16[768,1280]{1,0:T(8,128)(2,1)S(1)} %pad_maximum_fusion.3.mine_ref, bf16[768,1280]{1,0:T(8,128)(2,1)S(1)} %collective-permute-done.16.other_ref, ...), custom_call_target="tpu_custom_call" | custom-call | flops 8800000000 | tf_op jit(solution)/shard_map/projection_own/pallas_call | solution.py:284
  93.3 5.1 %collective-permute-done.15 = bf16[216,768]{1,0:T(8,128)(2,1)S(1)} collective-permute-done((bf16[216,768]{1,0:T(8,128)(2,1)S(1)}, bf16[216,768]{1,0:T(8,128)(2,1)S(1)}, u32[]{:S(2)}, u32[]{:S(2)}) %collective-permute-start.15) | collective-permute-done | bytes 331808 | tf_op jit(solution)/shard_map/ppermute | solution.py:735
  98.7 1.8 collective-permute-start.20
  103.6 2.5 collective-permute-start.17
  106.4 18.8 %attention_forward.2 = (f32[1024,768]{1,0:T(8,128)S(1)}, bf16[1024,768]{1,0:T(8,128)(2,1)S(1)}, f32[12,800]{1,0:T(8,128)S(1)}) custom-call(f32[12,1792]{1,0:T(8,128)S(1)} %fusion.2.refs_0_, bf16[800,2304]{1,0:T(8,128)(2,1)} %get-tuple-element.222.refs_1_.refs_2_.refs_3_, ...), custom_call_target="tpu_custom_call", output_to_operand_aliasing={{0}: (7, {}), {1}: (8, {})} | custom-call | flops 19800000512 | tf_op jit(solution)/shard_map/attention_forward/pallas_call | solution.py:112
  125.2 6.2 %collective-permute-done.18 = bf16[2,200,768]{2,1,0:T(8,128)(2,1)S(1)} collective-permute-done((bf16[2,200,768]{2,1,0:T(8,128)(2,1)S(1)}, bf16[2,200,768]{2,1,0:T(8,128)(2,1)S(1)}, u32[]{:S(2)}, u32[]{:S(2)}) %collective-permute-start.18) | collective-permute-done | bytes 614432 | tf_op jit(solution)/shard_map/ppermute | solution.py:739
  135.1 2.7 pad_maximum_fusion.refs_4_.wom_ref.mine_ref
  142.8 4.3 projection_shared.1
  147.2 8.2 %attention_forward.3 = (f32[1024,768]{1,0:T(8,128)}, bf16[1024,768]{1,0:T(8,128)(2,1)S(1)}, f32[12,200]{1,0:T(8,128)S(1)}) custom-call(f32[12,1152]{1,0:T(8,128)S(1)} %pad_dynamic-slice_fusion.1.refs_0_, bf16[200,768]{1,0:T(8,128)(2,1)S(1)} %get-tuple-element.237.refs_1_, ...), custom_call_target="tpu_custom_call", output_to_operand_aliasing={{0}: (7, {}), {1}: (8, {})} | custom-call | flops 8800000000 | tf_op jit(solution)/shard_map/attention_forward/pallas_call | solution.py:112
  155.5 3.0 collective-permute-done.21
  163.4 72.4 %layer_rest.1 = (bf16[1024,768]{1,0:T(8,128)(2,1)}, bf16[1024,768]{1,0:T(8,128)(2,1)}, f32[1024,768]{1,0:T(8,128)}, bf16[768,3456]{1,0:T(8,128)(2,1)}, bf16[768,3456]{1,0:T(8,128)(2,1)}, /*index=5*/f32[16,768]{1,0:T(8,128)}) custom-call(bf16[1024,768]{1,0:T(8,128)(2,1)} %copy-done.2, bf16[1024,768]{1,0:T(8,128)(2,1)} %copy-done.7, ...), custom_call_target="tpu_custom_call" | custom-call | flops 76999999488 | tf_op jit(solution)/shard_map/layer_rest/pallas_call | solution.py:536
  240.6 15.5 %attention_backward.3 = (bf16[200,768]{1,0:T(8,128)(2,1)}, bf16[2,800,768]{2,1,0:T(8,128)(2,1)}, f32[2,768]{1,0:T(2,128)}, f32[12,200]{1,0:T(8,128)}, f32[12,1152]{1,0:T(8,128)}) custom-call(f32[12,1152]{1,0:T(8,128)} %copy-done.16, bf16[200,768]{1,0:T(8,128)(2,1)} %copy-done.22, bf16[800,1536]{1,0:T(8,128)(2,1)} %copy-done.20, ...), custom_call_target="tpu_custom_call" | custom-call | flops 17600000000 | tf_op jit(solution)/shard_map/attention_backward/pallas_call | solution.py:217
  256.1 1.7 copy-done.21
  258.8 4.4 shared_input.1
  263.2 5.8 %add_convert_fusion = bf16[768,3456]{1,0:T(8,128)(2,1)S(1)} fusion(bf16[768,3456]{1,0:T(8,128)(2,1)} %collective-permute-done.23, bf16[768,3456]{1,0:T(8,128)(2,1)} %get-tuple-element.259), kind=kLoop, calls=%fused_computation | loop fusion | flops 10616832 | bytes 15925248 | tf_op jit(solution)/shard_map/convert_element_type | solution.py:838
  269.2 2.1 copy-done.28
  273.5 1.7 dynamic-slice_bitcast_fusion.2
  275.6 1.8 collective-permute-start.27
  278.8 25.5 %attention_backward.4 = (bf16[800,768]{1,0:T(8,128)(2,1)}, bf16[2,800,768]{2,1,0:T(8,128)(2,1)}, f32[2,768]{1,0:T(2,128)}, f32[12,800]{1,0:T(8,128)}, f32[12,1792]{1,0:T(8,128)}) custom-call(f32[12,1792]{1,0:T(8,128)} %copy-done.14, bf16[800,2304]{1,0:T(8,128)(2,1)} %get-tuple-element.222.refs_1_.refs_2_.refs_3_, ...), custom_call_target="tpu_custom_call" | custom-call | flops 28600000512 | tf_op jit(solution)/shard_map/attention_backward/pallas_call | solution.py:217
  306.6 2.6 collective-permute-start.31
  310.6 1.7 add_convert_fusion.2.refs_16_
  315.8 14.2 %attention_backward.5 = (bf16[800,768]{1,0:T(8,128)(2,1)}, bf16[2,800,768]{2,1,0:T(8,128)(2,1)}, f32[2,768]{1,0:T(2,128)}, f32[12,800]{1,0:T(8,128)}, f32[12,1792]{1,0:T(8,128)}) custom-call(f32[12,1792]{1,0:T(8,128)} %copy-done.14, ...), custom_call_target="tpu_custom_call", output_to_operand_aliasing={{0}: (12, {}), {1}: (13, {}), {2}: (14, {})} | custom-call | flops 14300000256 | tf_op jit(solution)/shard_map/attention_backward/pallas_call | solution.py:217
  335.4 8.2 %own_input.1.refs_8_ = bf16[800,768]{1,0:T(8,128)(2,1)} custom-call(bf16[800,768]{1,0:T(8,128)(2,1)} %get-tuple-element.292.refs_0_.refs_3_, bf16[2,800,768]{2,1,0:T(8,128)(2,1)} %get-tuple-element.293.refs_1_.refs_4_, bf16[768,2304]{1,0:T(8,128)(2,1)} %get-tuple-element.235.refs_2_, f32[1024,768]{1,0:T(8,128)} %get-tuple-element.294.refs_3_, ...), custom_call_target="tpu_custom_call" | custom-call | flops 8800000000 | tf_op jit(solution)/shard_map/own_input/pallas_call | solution.py:698
  343.6 4.5 collective-permute-done.32
  348.2 12.5 %projection_weight_grad.1 = (bf16[768,1152]{1,0:T(8,128)(2,1)}, bf16[768,1152]{1,0:T(8,128)(2,1)}) custom-call(bf16[1024,768]{1,0:T(8,128)(2,1)} %copy-done.2, bf16[800,768]{1,0:T(8,128)(2,1)} %bitcast.287, bf16[200,768]{1,0:T(8,128)(2,1)} %copy-done.10, bf16[800,768]{1,0:T(8,128)(2,1)} %get-tuple-element.292.refs_0_.refs_3_, ...), custom_call_target="tpu_custom_call" | custom-call | flops 11000000512 | tf_op jit(solution)/shard_map/projection_weight_grad/pallas_call | solution.py:656
  361.8 1.7 collective-permute-start.34
  380.1 5.4 %collective-permute-done.36 = bf16[2,192,512]{2,1,0:T(8,128)(2,1)} collective-permute-done((bf16[2,192,512]{2,1,0:T(8,128)(2,1)}, bf16[2,192,512]{2,1,0:T(8,128)(2,1)}, u32[]{:S(2)}, u32[]{:S(2)}) %collective-permute-start.36) | collective-permute-done | bytes 393248 | tf_op jit(solution)/shard_map/ppermute | solution.py:735
  391.4 1.7 bitcast_dynamic-update-slice_fusion
  393.1 3.1 collective-permute-done.39
  396.2 10.4 %collective-permute-done.33 = bf16[2,200,768]{2,1,0:T(8,128)(2,1)} collective-permute-done((bf16[2,200,768]{2,1,0:T(8,128)(2,1)}, bf16[2,200,768]{2,1,0:T(8,128)(2,1)}, u32[]{:S(2)}, u32[]{:S(2)}) %collective-permute-start.33) | collective-permute-done | bytes 614432 | tf_op jit(solution)/shard_map/ppermute | solution.py:739
  411.0 1.9 collective-permute-start.42
  413.4 2.9 collective-permute-done.43
  416.6 2.5 collective-permute-start.46
  419.2 14.5 %collective-permute-done.47 = f32[27,768]{1,0:T(8,128)S(1)} collective-permute-done((f32[27,768]{1,0:T(8,128)S(1)}, f32[27,768]{1,0:T(8,128)S(1)}, u32[]{:S(2)}, u32[]{:S(2)}) %collective-permute-start.47) | collective-permute-done | bytes 82976 | tf_op jit(solution)/shard_map/ppermute | solution.py:735
  436.1 2.6 copy.71
  441.4 6.3 %collective-permute-done.49 = f32[27,768]{1,0:T(8,128)S(1)} collective-permute-done((f32[27,768]{1,0:T(8,128)S(1)}, f32[27,768]{1,0:T(8,128)S(1)}, u32[]{:S(2)}, u32[]{:S(2)}) %collective-permute-start.49) | collective-permute-done | bytes 82976 | tf_op jit(solution)/shard_map/ppermute | solution.py:735
  (460 shorter events, 117.6 us)
Async XLA Ops:
  4.0 4.7 %collective-permute-start.1 = (bf16[24,1280]{1,0:T(8,128)(2,1)S(1)}, bf16[24,1280]{1,0:T(8,128)(2,1)S(1)}, u32[]{:S(2)}, u32[]{:S(2)}) collective-permute-start(bf16[24,1280]{1,0:T(8,128)(2,1)S(1)} %broadcast_select_fusion.10), channel_id=1, source_target_pairs={{0,4},{4,0},{8,12},{12,8},{16,20},{20,16},{24,28},{28,24},{1,5},{5... | collective-permute-start | bytes 184328 | tf_op jit(solution)/shard_map/ppermute | solution.py:735
  9.6 10.4 %collective-permute-start.2 = (bf16[2,24,1280]{2,1,0:T(8,128)(2,1)S(1)}, bf16[2,24,1280]{2,1,0:T(8,128)(2,1)S(1)}, u32[]{:S(2)}, u32[]{:S(2)}) collective-permute-start(bf16[2,24,1280]{2,1,0:T(8,128)(2,1)S(1)} %pad_maximum_fusion.28), channel_id=1, source_target_pairs={{0,2},{1,3},{2,0},{3,1},{4,6},{5,7},{6,4},{7,5},{8,10},{9,11},{10,... | collective-permute-start | bytes 368648 | tf_op jit(solution)/shard_map/ppermute | solution.py:735
  14.4 27.4 %collective-permute-start.7 = (bf16[216,768]{1,0:T(8,128)(2,1)}, bf16[216,768]{1,0:T(8,128)(2,1)S(1)}, u32[]{:S(2)}, u32[]{:S(2)}) collective-permute-start(bf16[216,768]{1,0:T(8,128)(2,1)} %fusion.11), channel_id=1, source_target_pairs={{0,1},{1,0},{2,3},{3,2},{4,5},{5,4},{6,7},{7,6},{8,9},{9,8},{10,11... | collective-permute-start | bytes 995336 | tf_op jit(solution)/shard_map/ppermute | solution.py:739
  20.0 16.7 %collective-permute-start.3 = (bf16[2,2,24,1280]{3,2,1,0:T(8,128)(2,1)S(1)}, bf16[2,2,24,1280]{3,2,1,0:T(8,128)(2,1)S(1)}, u32[]{:S(2)}, u32[]{:S(2)}) collective-permute-start(bf16[2,2,24,1280]{3,2,1,0:T(8,128)(2,1)S(1)} %pad_maximum_fusion.21), channel_id=1, source_target_pairs={{0,1},{1,0},{2,3},{3,2},{4,5},{5,4},{6,7},{7,6},{8,9},{9,8},{10,11... | collective-permute-start | bytes 737288 | tf_op jit(solution)/shard_map/ppermute | solution.py:735
  20.9 20.9 %collective-permute-start.6 = (bf16[2,24,3456]{2,1,0:T(8,128)(2,1)S(1)}, bf16[2,24,3456]{2,1,0:T(8,128)(2,1)}, u32[]{:S(2)}, u32[]{:S(2)}) collective-permute-start(bf16[2,24,3456]{2,1,0:T(8,128)(2,1)S(1)} %pad_maximum_fusion.20), channel_id=1, source_target_pairs={{0,2},{1,3},{2,0},{3,1},{4,6},{5,7},{6,4},{7,5},{8,10},{9,11},{10,... | collective-permute-start | bytes 995336 | tf_op jit(solution)/shard_map/ppermute | solution.py:735
  36.9 7.2 %collective-permute-start.4 = (bf16[192,640]{1,0:T(8,128)(2,1)S(1)}, bf16[192,640]{1,0:T(8,128)(2,1)S(1)}, u32[]{:S(2)}, u32[]{:S(2)}) collective-permute-start(bf16[192,640]{1,0:T(8,128)(2,1)S(1)} %get-tuple-element.195), channel_id=1, source_target_pairs={{0,8},{4,12},{8,0},{12,4},{16,24},{20,28},{24,16},{28,20},{1,9},{5... | collective-permute-start | bytes 737288 | tf_op jit(solution)/shard_map/ppermute | solution.py:735
  38.5 6.9 %collective-permute-start.5 = (bf16[192,640]{1,0:T(8,128)(2,1)S(1)}, bf16[192,640]{1,0:T(8,128)(2,1)S(1)}, u32[]{:S(2)}, u32[]{:S(2)}) collective-permute-start(bf16[192,640]{1,0:T(8,128)(2,1)S(1)} %get-tuple-element.197), channel_id=1, source_target_pairs={{0,16},{4,20},{8,24},{12,28},{16,0},{20,4},{24,8},{28,12},{1,17},{... | collective-permute-start | bytes 737288 | tf_op jit(solution)/shard_map/ppermute | solution.py:735
  47.3 23.7 %collective-permute-start.12 = (bf16[2,2,24,3456]{3,2,0,1:T(8,128)(2,1)S(1)}, bf16[2,2,24,3456]{3,2,0,1:T(8,128)(2,1)}, u32[]{:S(2)}, u32[]{:S(2)}) collective-permute-start(bf16[2,2,24,3456]{3,2,0,1:T(8,128)(2,1)S(1)} %pad_maximum_fusion.11), channel_id=1, source_target_pairs={{0,1},{1,0},{2,3},{3,2},{4,5},{5,4},{6,7},{7,6},{8,9},{9,8},{10,11... | collective-permute-start | bytes 1990664 | tf_op jit(solution)/shard_map/ppermute | solution.py:735
  47.6 11.4 %collective-permute-start.11 = (bf16[2,192,640]{2,1,0:T(8,128)(2,1)S(1)}, bf16[2,192,640]{2,1,0:T(8,128)(2,1)}, u32[]{:S(2)}, u32[]{:S(2)}) collective-permute-start(bf16[2,192,640]{2,1,0:T(8,128)(2,1)S(1)} %pad_maximum_fusion.18), channel_id=1, source_target_pairs={{0,8},{4,12},{8,0},{12,4},{16,24},{20,28},{24,16},{28,20},{1,9},{5... | collective-permute-start | bytes 1474568 | tf_op jit(solution)/shard_map/ppermute | solution.py:735
  49.1 11.6 %collective-permute-start.10 = (bf16[2,192,640]{2,1,0:T(8,128)(2,1)}, bf16[2,192,640]{2,1,0:T(8,128)(2,1)}, u32[]{:S(2)}, u32[]{:S(2)}) collective-permute-start(bf16[2,192,640]{2,1,0:T(8,128)(2,1)} %pad_maximum_fusion.17), channel_id=1, source_target_pairs={{0,16},{4,20},{8,24},{12,28},{16,0},{20,4},{24,8},{28,12},{1,17},{... | collective-permute-start | bytes 1474568 | tf_op jit(solution)/shard_map/ppermute | solution.py:735
  51.7 26.2 %collective-permute-start.8 = (bf16[216,768]{1,0:T(8,128)(2,1)}, bf16[216,768]{1,0:T(8,128)(2,1)S(1)}, u32[]{:S(2)}, u32[]{:S(2)}) collective-permute-start(bf16[216,768]{1,0:T(8,128)(2,1)} %get-tuple-element.192), channel_id=1, source_target_pairs={{0,2},{1,3},{2,0},{3,1},{4,6},{5,7},{6,4},{7,5},{8,10},{9,11},{10,... | collective-permute-start | bytes 995336 | tf_op jit(solution)/shard_map/ppermute | solution.py:739
  54.7 23.2 %collective-permute-start.9 = (bf16[216,768]{1,0:T(8,128)(2,1)}, bf16[216,768]{1,0:T(8,128)(2,1)S(1)}, u32[]{:S(2)}, u32[]{:S(2)}) collective-permute-start(bf16[216,768]{1,0:T(8,128)(2,1)} %fusion.13), channel_id=1, source_target_pairs={{0,3},{1,2},{2,1},{3,0},{4,7},{5,6},{6,5},{7,4},{8,11},{9,10},{10,... | collective-permute-start | bytes 995336 | tf_op jit(solution)/shard_map/ppermute | solution.py:739
  75.5 12.6 %collective-permute-start.16 = (bf16[768,1280]{1,0:T(8,128)(2,1)S(1)}, bf16[768,1280]{1,0:T(8,128)(2,1)S(1)}, u32[]{:S(2)}, u32[]{:S(2)}) collective-permute-start(bf16[768,1280]{1,0:T(8,128)(2,1)S(1)} %pad_maximum_fusion.3.mine_ref), channel_id=1, source_target_pairs={{0,4},{4,0},{8,12},{12,8},{16,20},{20,16},{24,28},{28,24},{1,5},{5... | collective-permute-start | bytes 5898248 | tf_op jit(solution)/shard_map/ppermute | solution.py:735
  80.5 17.9 %collective-permute-start.14 = (bf16[192,1792]{1,0:T(8,128)(2,1)S(1)}, bf16[192,1792]{1,0:T(8,128)(2,1)S(1)}, u32[]{:S(2)}, u32[]{:S(2)}) collective-permute-start(bf16[192,1792]{1,0:T(8,128)(2,1)S(1)} %slice.238), channel_id=1, source_target_pairs={{0,16},{4,20},{8,24},{12,28},{16,0},{20,4},{24,8},{28,12},{1,17},{... | collective-permute-start | bytes 2064392 | tf_op jit(solution)/shard_map/ppermute | solution.py:735
  81.4 17.0 %collective-permute-start.13 = (bf16[192,1664]{1,0:T(8,128)(2,1)S(1)}, bf16[192,1664]{1,0:T(8,128)(2,1)S(1)}, u32[]{:S(2)}, u32[]{:S(2)}) collective-permute-start(bf16[192,1664]{1,0:T(8,128)(2,1)S(1)} %slice.237), channel_id=1, source_target_pairs={{0,8},{4,12},{8,0},{12,4},{16,24},{20,28},{24,16},{28,20},{1,9},{5... | collective-permute-start | bytes 1916936 | tf_op jit(solution)/shard_map/ppermute | solution.py:735
  82.6 15.8 %collective-permute-start.15 = (bf16[216,768]{1,0:T(8,128)(2,1)S(1)}, bf16[216,768]{1,0:T(8,128)(2,1)S(1)}, u32[]{:S(2)}, u32[]{:S(2)}) collective-permute-start(bf16[216,768]{1,0:T(8,128)(2,1)S(1)} %copy-done.41), channel_id=1, source_target_pairs={{0,2},{1,3},{2,0},{3,1},{4,6},{5,7},{6,4},{7,5},{8,10},{9,11},{10,... | collective-permute-start | bytes 995336 | tf_op jit(solution)/shard_map/ppermute | solution.py:735
  98.7 34.2 %collective-permute-start.20 = (bf16[2,192,1792]{2,1,0:T(8,128)(2,1)S(1)}, bf16[2,192,1792]{2,1,0:T(8,128)(2,1)S(1)}, u32[]{:S(2)}, u32[]{:S(2)}) collective-permute-start(bf16[2,192,1792]{2,1,0:T(8,128)(2,1)S(1)} %pad_maximum_fusion.4), channel_id=1, source_target_pairs={{0,8},{4,12},{8,0},{12,4},{16,24},{20,28},{24,16},{28,20},{1,9},{5... | collective-permute-start | bytes 4128776 | tf_op jit(solution)/shard_map/ppermute | solution.py:735
  100.7 32.1 %collective-permute-start.19 = (bf16[2,192,1664]{2,1,0:T(8,128)(2,1)S(1)}, bf16[2,192,1664]{2,1,0:T(8,128)(2,1)S(1)}, u32[]{:S(2)}, u32[]{:S(2)}) collective-permute-start(bf16[2,192,1664]{2,1,0:T(8,128)(2,1)S(1)} %pad_maximum_fusion.8), channel_id=1, source_target_pairs={{0,16},{4,20},{8,24},{12,28},{16,0},{20,4},{24,8},{28,12},{1,17},{... | collective-permute-start | bytes 3833864 | tf_op jit(solution)/shard_map/ppermute | solution.py:735
  102.9 28.5 %collective-permute-start.18 = (bf16[2,200,768]{2,1,0:T(8,128)(2,1)S(1)}, bf16[2,200,768]{2,1,0:T(8,128)(2,1)S(1)}, u32[]{:S(2)}, u32[]{:S(2)}) collective-permute-start(bf16[2,200,768]{2,1,0:T(8,128)(2,1)S(1)} %get-tuple-element.413), channel_id=1, source_target_pairs={{0,2},{1,3},{2,0},{3,1},{4,6},{5,7},{6,4},{7,5},{8,10},{9,11},{10,... | collective-permute-start | bytes 1843208 | tf_op jit(solution)/shard_map/ppermute | solution.py:739
  103.6 29.3 %collective-permute-start.17 = (bf16[2,216,768]{2,1,0:T(8,128)(2,1)S(1)}, bf16[2,216,768]{2,1,0:T(8,128)(2,1)S(1)}, u32[]{:S(2)}, u32[]{:S(2)}) collective-permute-start(bf16[2,216,768]{2,1,0:T(8,128)(2,1)S(1)} %pad_maximum_fusion.12), channel_id=1, source_target_pairs={{0,1},{1,0},{2,3},{3,2},{4,5},{5,4},{6,7},{7,6},{8,9},{9,8},{10,11... | collective-permute-start | bytes 1990664 | tf_op jit(solution)/shard_map/ppermute | solution.py:735
  137.8 20.7 %collective-permute-start.22 = (bf16[768,3456]{1,0:T(8,128)(2,1)}, bf16[768,3456]{1,0:T(8,128)(2,1)}, u32[]{:S(2)}, u32[]{:S(2)}) collective-permute-start(bf16[768,3456]{1,0:T(8,128)(2,1)} %pad_maximum_fusion.refs_4_.wom_ref.mine_ref), channel_id=1, source_target_pairs={{0,4},{4,0},{8,12},{12,8},{16,20},{20,16},{24,28},{28,24},{1,5},{5... | collective-permute-start | bytes 15925256 | tf_op jit(solution)/shard_map/ppermute | solution.py:735
  142.1 16.3 %collective-permute-start.21 = (bf16[2,200,768]{2,1,0:T(8,128)(2,1)S(1)}, bf16[2,200,768]{2,1,0:T(8,128)(2,1)S(1)}, u32[]{:S(2)}, u32[]{:S(2)}) collective-permute-start(bf16[2,200,768]{2,1,0:T(8,128)(2,1)S(1)} %pad_maximum_fusion.13), channel_id=1, source_target_pairs={{0,1},{1,0},{2,3},{3,2},{4,5},{5,4},{6,7},{7,6},{8,9},{9,8},{10,11... | collective-permute-start | bytes 1843208 | tf_op jit(solution)/shard_map/ppermute | solution.py:739
  235.8 27.4 %collective-permute-start.23 = (bf16[768,3456]{1,0:T(8,128)(2,1)}, bf16[768,3456]{1,0:T(8,128)(2,1)}, u32[]{:S(2)}, u32[]{:S(2)}) collective-permute-start(bf16[768,3456]{1,0:T(8,128)(2,1)} %get-tuple-element.250), channel_id=1, source_target_pairs={{0,4},{4,0},{8,12},{12,8},{16,20},{20,16},{24,28},{28,24},{1,5},{5... | collective-permute-start | bytes 15925256 | tf_op jit(solution)/shard_map/ppermute | solution.py:735
  239.0 65.4 %collective-permute-start.26 = (bf16[2,200,768]{2,1,0:T(8,128)(2,1)}, bf16[2,200,768]{2,1,0:T(8,128)(2,1)S(1)}, u32[]{:S(2)}, u32[]{:S(2)}) collective-permute-start(bf16[2,200,768]{2,1,0:T(8,128)(2,1)} %get-tuple-element.411), channel_id=1, source_target_pairs={{0,2},{1,3},{2,0},{3,1},{4,6},{5,7},{6,4},{7,5},{8,10},{9,11},{10,... | collective-permute-start | bytes 1843208 | tf_op jit(solution)/shard_map/ppermute | solution.py:739
  272.6 33.0 %collective-permute-start.25 = (bf16[2,192,1792]{2,1,0:T(8,128)(2,1)}, bf16[2,192,1792]{2,1,0:T(8,128)(2,1)}, u32[]{:S(2)}, u32[]{:S(2)}) collective-permute-start(bf16[2,192,1792]{2,1,0:T(8,128)(2,1)} %get-tuple-element.380), channel_id=1, source_target_pairs={{0,16},{4,20},{8,24},{12,28},{16,0},{20,4},{24,8},{28,12},{1,17},{... | collective-permute-start | bytes 4128776 | tf_op jit(solution)/shard_map/ppermute | solution.py:735
  275.2 30.4 %collective-permute-start.24 = (bf16[2,192,1664]{2,1,0:T(8,128)(2,1)}, bf16[2,192,1664]{2,1,0:T(8,128)(2,1)S(1)}, u32[]{:S(2)}, u32[]{:S(2)}) collective-permute-start(bf16[2,192,1664]{2,1,0:T(8,128)(2,1)} %get-tuple-element.384), channel_id=1, source_target_pairs={{0,8},{4,12},{8,0},{12,4},{16,24},{20,28},{24,16},{28,20},{1,9},{5... | collective-permute-start | bytes 3833864 | tf_op jit(solution)/shard_map/ppermute | solution.py:735
  275.6 28.7 %collective-permute-start.27 = (bf16[2,200,768]{2,1,0:T(8,128)(2,1)S(1)}, bf16[2,200,768]{2,1,0:T(8,128)(2,1)S(1)}, u32[]{:S(2)}, u32[]{:S(2)}) collective-permute-start(bf16[2,200,768]{2,1,0:T(8,128)(2,1)S(1)} %get-tuple-element.409), channel_id=1, source_target_pairs={{0,1},{1,0},{2,3},{3,2},{4,5},{5,4},{6,7},{7,6},{8,9},{9,8},{10,11... | collective-permute-start | bytes 1843208 | tf_op jit(solution)/shard_map/ppermute | solution.py:735
  306.6 23.4 %collective-permute-start.31 = (bf16[200,768]{1,0:T(8,128)(2,1)}, bf16[200,768]{1,0:T(8,128)(2,1)}, u32[]{:S(2)}, u32[]{:S(2)}) collective-permute-start(bf16[200,768]{1,0:T(8,128)(2,1)} %get-tuple-element.429), channel_id=1, source_target_pairs={{0,2},{1,3},{2,0},{3,1},{4,6},{5,7},{6,4},{7,5},{8,10},{9,11},{10,... | collective-permute-start | bytes 921608 | tf_op jit(solution)/shard_map/ppermute | solution.py:735
  310.3 20.5 %collective-permute-start.30 = (bf16[2,200,768]{2,1,0:T(8,128)(2,1)}, bf16[2,200,768]{2,1,0:T(8,128)(2,1)S(1)}, u32[]{:S(2)}, u32[]{:S(2)}) collective-permute-start(bf16[2,200,768]{2,1,0:T(8,128)(2,1)} %pad_maximum_fusion.14), channel_id=1, source_target_pairs={{0,1},{1,0},{2,3},{3,2},{4,5},{5,4},{6,7},{7,6},{8,9},{9,8},{10,11... | collective-permute-start | bytes 1843208 | tf_op jit(solution)/shard_map/ppermute | solution.py:739
  312.4 18.3 %collective-permute-start.29 = (bf16[192,1792]{1,0:T(8,128)(2,1)S(1)}, bf16[192,1792]{1,0:T(8,128)(2,1)S(1)}, u32[]{:S(2)}, u32[]{:S(2)}) collective-permute-start(bf16[192,1792]{1,0:T(8,128)(2,1)S(1)} %get-tuple-element.393), channel_id=1, source_target_pairs={{0,8},{4,12},{8,0},{12,4},{16,24},{20,28},{24,16},{28,20},{1,9},{5... | collective-permute-start | bytes 2064392 | tf_op jit(solution)/shard_map/ppermute | solution.py:735
  314.9 15.8 %collective-permute-start.28 = (bf16[192,1664]{1,0:T(8,128)(2,1)S(1)}, bf16[192,1664]{1,0:T(8,128)(2,1)S(1)}, u32[]{:S(2)}, u32[]{:S(2)}) collective-permute-start(bf16[192,1664]{1,0:T(8,128)(2,1)S(1)} %get-tuple-element.403), channel_id=1, source_target_pairs={{0,16},{4,20},{8,24},{12,28},{16,0},{20,4},{24,8},{28,12},{1,17},{... | collective-permute-start | bytes 1916936 | tf_op jit(solution)/shard_map/ppermute | solution.py:735
  333.0 15.1 %collective-permute-start.32 = (bf16[2,2,24,3456]{3,2,1,0:T(8,128)(2,1)S(1)}, bf16[2,2,24,3456]{3,2,1,0:T(8,128)(2,1)S(1)}, u32[]{:S(2)}, u32[]{:S(2)}) collective-permute-start(bf16[2,2,24,3456]{3,2,1,0:T(8,128)(2,1)S(1)} %get-tuple-element.397), channel_id=1, source_target_pairs={{0,1},{1,0},{2,3},{3,2},{4,5},{5,4},{6,7},{7,6},{8,9},{9,8},{10,11... | collective-permute-start | bytes 1990664 | tf_op jit(solution)/shard_map/ppermute | solution.py:735
  360.7 5.5 %collective-permute-start.35 = (bf16[768,1152]{1,0:T(8,128)(2,1)}, bf16[768,1152]{1,0:T(8,128)(2,1)S(1)}, u32[]{:S(2)}, u32[]{:S(2)}) collective-permute-start(bf16[768,1152]{1,0:T(8,128)(2,1)} %get-tuple-element.312), channel_id=1, source_target_pairs={{0,4},{4,0},{8,12},{12,8},{16,20},{20,16},{24,28},{28,24},{1,5},{5... | collective-permute-start | bytes 5308424 | tf_op jit(solution)/shard_map/ppermute | solution.py:735
  361.8 34.4 %collective-permute-start.34 = (bf16[2,24,3456]{2,1,0:T(8,128)(2,1)}, bf16[2,24,3456]{2,1,0:T(8,128)(2,1)}, u32[]{:S(2)}, u32[]{:S(2)}) collective-permute-start(bf16[2,24,3456]{2,1,0:T(8,128)(2,1)} %get-tuple-element.423), channel_id=1, source_target_pairs={{0,2},{1,3},{2,0},{3,1},{4,6},{5,7},{6,4},{7,5},{8,10},{9,11},{10,... | collective-permute-start | bytes 995336 | tf_op jit(solution)/shard_map/ppermute | solution.py:735
  364.4 42.2 %collective-permute-start.33 = (bf16[2,200,768]{2,1,0:T(8,128)(2,1)}, bf16[2,200,768]{2,1,0:T(8,128)(2,1)}, u32[]{:S(2)}, u32[]{:S(2)}) collective-permute-start(bf16[2,200,768]{2,1,0:T(8,128)(2,1)} %get-tuple-element.407), channel_id=1, source_target_pairs={{0,2},{1,3},{2,0},{3,1},{4,6},{5,7},{6,4},{7,5},{8,10},{9,11},{10,... | collective-permute-start | bytes 1843208 | tf_op jit(solution)/shard_map/ppermute | solution.py:739
  372.5 13.4 %collective-permute-start.37 = (bf16[2,192,640]{2,1,0:T(8,128)(2,1)}, bf16[2,192,640]{2,1,0:T(8,128)(2,1)}, u32[]{:S(2)}, u32[]{:S(2)}) collective-permute-start(bf16[2,192,640]{2,1,0:T(8,128)(2,1)} %get-tuple-element.415), channel_id=1, source_target_pairs={{0,16},{4,20},{8,24},{12,28},{16,0},{20,4},{24,8},{28,12},{1,17},{... | collective-permute-start | bytes 1474568 | tf_op jit(solution)/shard_map/ppermute | solution.py:735
  374.4 11.1 %collective-permute-start.36 = (bf16[2,192,512]{2,1,0:T(8,128)(2,1)}, bf16[2,192,512]{2,1,0:T(8,128)(2,1)}, u32[]{:S(2)}, u32[]{:S(2)}) collective-permute-start(bf16[2,192,512]{2,1,0:T(8,128)(2,1)} %get-tuple-element.421), channel_id=1, source_target_pairs={{0,8},{4,12},{8,0},{12,4},{16,24},{20,28},{24,16},{28,20},{1,9},{5... | collective-permute-start | bytes 1179656 | tf_op jit(solution)/shard_map/ppermute | solution.py:735
  385.9 7.2 %collective-permute-start.41 = (f32[27,768]{1,0:T(8,128)S(1)}, f32[27,768]{1,0:T(8,128)S(1)}, u32[]{:S(2)}, u32[]{:S(2)}) collective-permute-start(f32[27,768]{1,0:T(8,128)S(1)} %add.308), channel_id=1, source_target_pairs={{0,8},{4,12},{8,0},{12,4},{16,24},{20,28},{24,16},{28,20},{1,9},{5... | collective-permute-start | bytes 248840 | tf_op jit(solution)/shard_map/ppermute | solution.py:735
  388.7 7.5 %collective-permute-start.40 = (bf16[192,640]{1,0:T(8,128)(2,1)S(1)}, bf16[192,640]{1,0:T(8,128)(2,1)S(1)}, u32[]{:S(2)}, u32[]{:S(2)}) collective-permute-start(bf16[192,640]{1,0:T(8,128)(2,1)S(1)} %get-tuple-element.439), channel_id=1, source_target_pairs={{0,8},{4,12},{8,0},{12,4},{16,24},{20,28},{24,16},{28,20},{1,9},{5... | collective-permute-start | bytes 737288 | tf_op jit(solution)/shard_map/ppermute | solution.py:735
  390.5 5.7 %collective-permute-start.39 = (bf16[192,512]{1,0:T(8,128)(2,1)S(1)}, bf16[192,512]{1,0:T(8,128)(2,1)S(1)}, u32[]{:S(2)}, u32[]{:S(2)}) collective-permute-start(bf16[192,512]{1,0:T(8,128)(2,1)S(1)} %get-tuple-element.451), channel_id=1, source_target_pairs={{0,16},{4,20},{8,24},{12,28},{16,0},{20,4},{24,8},{28,12},{1,17},{... | collective-permute-start | bytes 589832 | tf_op jit(solution)/shard_map/ppermute | solution.py:735
  407.8 5.7 %collective-permute-start.45 = (bf16[24,3456]{1,0:T(8,128)(2,1)S(1)}, bf16[24,3456]{1,0:T(8,128)(2,1)S(1)}, u32[]{:S(2)}, u32[]{:S(2)}) collective-permute-start(bf16[24,3456]{1,0:T(8,128)(2,1)S(1)} %get-tuple-element.455), channel_id=1, source_target_pairs={{0,4},{4,0},{8,12},{12,8},{16,20},{20,16},{24,28},{28,24},{1,5},{5... | collective-permute-start | bytes 497672 | tf_op jit(solution)/shard_map/ppermute | solution.py:735
  408.1 8.3 %collective-permute-start.43 = (bf16[2,2,24,1152]{3,2,1,0:T(8,128)(2,1)S(1)}, bf16[2,2,24,1152]{3,2,1,0:T(8,128)(2,1)S(1)}, u32[]{:S(2)}, u32[]{:S(2)}) collective-permute-start(bf16[2,2,24,1152]{3,2,1,0:T(8,128)(2,1)S(1)} %get-tuple-element.449), channel_id=1, source_target_pairs={{0,1},{1,0},{2,3},{3,2},{4,5},{5,4},{6,7},{7,6},{8,9},{9,8},{10,11... | collective-permute-start | bytes 663560 | tf_op jit(solution)/shard_map/ppermute | solution.py:735
  408.2 5.3 %collective-permute-start.44 = (f32[27,768]{1,0:T(8,128)S(1)}, f32[27,768]{1,0:T(8,128)S(1)}, u32[]{:S(2)}, u32[]{:S(2)}) collective-permute-start(f32[27,768]{1,0:T(8,128)S(1)} %add.309), channel_id=1, source_target_pairs={{0,16},{4,20},{8,24},{12,28},{16,0},{20,4},{24,8},{28,12},{1,17},{... | collective-permute-start | bytes 248840 | tf_op jit(solution)/shard_map/ppermute | solution.py:735
  411.0 39.8 %collective-permute-start.42 = (bf16[2,200,768]{2,1,0:T(8,128)(2,1)}, bf16[2,200,768]{2,1,0:T(8,128)(2,1)S(1)}, u32[]{:S(2)}, u32[]{:S(2)}) collective-permute-start(bf16[2,200,768]{2,1,0:T(8,128)(2,1)} %pad_maximum_fusion.15), channel_id=1, source_target_pairs={{0,1},{1,0},{2,3},{3,2},{4,5},{5,4},{6,7},{7,6},{8,9},{9,8},{10,11... | collective-permute-start | bytes 1843208 | tf_op jit(solution)/shard_map/ppermute | solution.py:739
  416.4 17.2 %collective-permute-start.47 = (f32[27,768]{1,0:T(8,128)S(1)}, f32[27,768]{1,0:T(8,128)S(1)}, u32[]{:S(2)}, u32[]{:S(2)}) collective-permute-start(f32[27,768]{1,0:T(8,128)S(1)} %add.320), channel_id=1, source_target_pairs={{0,1},{1,0},{2,3},{3,2},{4,5},{5,4},{6,7},{7,6},{8,9},{9,8},{10,11... | collective-permute-start | bytes 248840 | tf_op jit(solution)/shard_map/ppermute | solution.py:735
  416.6 17.0 %collective-permute-start.46 = (bf16[2,24,1152]{2,1,0:T(8,128)(2,1)S(1)}, bf16[2,24,1152]{2,1,0:T(8,128)(2,1)S(1)}, u32[]{:S(2)}, u32[]{:S(2)}) collective-permute-start(bf16[2,24,1152]{2,1,0:T(8,128)(2,1)S(1)} %get-tuple-element.463), channel_id=1, source_target_pairs={{0,2},{1,3},{2,0},{3,1},{4,6},{5,7},{6,4},{7,5},{8,10},{9,11},{10,... | collective-permute-start | bytes 331784 | tf_op jit(solution)/shard_map/ppermute | solution.py:735
  433.7 7.0 %collective-permute-start.48 = (bf16[24,1152]{1,0:T(8,128)(2,1)S(1)}, bf16[24,1152]{1,0:T(8,128)(2,1)S(1)}, u32[]{:S(2)}, u32[]{:S(2)}) collective-permute-start(bf16[24,1152]{1,0:T(8,128)(2,1)S(1)} %dynamic-slice_bitcast_fusion.44), channel_id=1, source_target_pairs={{0,4},{4,0},{8,12},{12,8},{16,20},{20,16},{24,28},{28,24},{1,5},{5... | collective-permute-start | bytes 165896 | tf_op jit(solution)/shard_map/ppermute | solution.py:735
  439.5 8.3 %collective-permute-start.49 = (f32[27,768]{1,0:T(8,128)S(1)}, f32[27,768]{1,0:T(8,128)S(1)}, u32[]{:S(2)}, u32[]{:S(2)}) collective-permute-start(f32[27,768]{1,0:T(8,128)S(1)} %add.322), channel_id=1, source_target_pairs={{0,2},{1,3},{2,0},{3,1},{4,6},{5,7},{6,4},{7,5},{8,10},{9,11},{10,... | collective-permute-start | bytes 248840 | tf_op jit(solution)/shard_map/ppermute | solution.py:735
  (93 other events, 816.1 us)
